TPU v7x, 32 devices: a whole 2x2x4 slice. The times are simulated.
32 devices in a mesh: clip: 2 (over y), tile: 4 (over z), frame: 2 (over x), chan: 2 (over core).
Axes of the slice: x: 2, y: 2, z: 4, core: 2. Of those that a mesh axis runs over, the one named last changes fastest.
Arguments:
- features: bfloat16 [4, 8, 256, 256], P(('clip', 'frame'), 'tile', None, 'chan'), parts along dimension 0, may hold values from -6 to 6
- neighbours: int32 [16, 9], P(('clip', 'tile')), parts along dimension 0, may hold values from 0 to 7, as said below
- pairing: int32 [4, 2], P(('clip', 'frame')), parts along dimension 0, may hold values 0 or 1
- valid_tiles: int32 [16, 256], P(('clip', 'tile')), parts along dimension 0, may hold values 0 or 1
- cotangent: bfloat16 [4, 8, 256, 3060], P(('clip', 'frame'), 'tile', 'chan'), parts along dimension 0, may hold values from -6 to 6
Outputs:
- volume: bfloat16 [4, 8, 256, 3060], P(('clip', 'frame'), 'tile', 'chan'), parts along dimension 0
- feature_grad: float32 [4, 8, 256, 256], P(('clip', 'frame'), 'tile', None, 'chan'), parts along dimension 0
There are 2 independent parts, one for each index of `clip`. A program takes and returns all parts, laid end to end along the dimension named above; each array names one. Nothing has to cross between parts.
Inputs may be any that keep to these rules, and one draw needn't show every extreme that they name: `neighbours`: every entry of row a lies within 2 tiles of a, and in every row one entry lies exactly 2 tiles from a.
All inputs are finite; a program needn't handle non-finite values. No bound on the sum of `pairing` or of `valid_tiles` on one device may be relied on, other than what follows from the above.
Results may differ from a plain program's by a relative error of at most 0.008.
Values may be sent and summed in bfloat16 or wider, within the bound.
No kernel may reach another device: no remote copies, remote signals or barrier semaphores. Data moves between devices by JAX's collectives and lax.ppermute only.
A program may use at most 64 MiB of HBM per device.

v0:
```python
import math

import jax
import jax.numpy as jnp
from jax import lax
from jax.sharding import PartitionSpec as P

CHANNELS = 256
SIDE = 16
PIXELS = 256
LEVELS = 340
NEIGHBOURS = 9


def with_halo(cells, sides, width):
    for axis, dim in sides:
        count = lax.axis_size(axis)
        ends = count - 1
        head = lax.slice_in_dim(cells, 0, width, axis=dim)
        tail = lax.slice_in_dim(cells, cells.shape[dim] - width, cells.shape[dim], axis=dim)
        cells = jnp.concatenate(
            [
                lax.ppermute(tail, axis, [(i, (i + 1) % count) for i in range(ends)]),
                cells,
                lax.ppermute(head, axis, [((i + 1) % count, i) for i in range(ends)]),
            ],
            axis=dim,
        )
    return cells


def pool_weights_table():
    pixel_ids = jnp.arange(PIXELS, dtype=jnp.int32)
    row_of = pixel_ids // SIDE
    column = pixel_ids % SIDE
    pieces = []
    for extent in (1, 2, 4, 8):
        across = SIDE // extent
        target = row_of // extent * across + column // extent
        member = jnp.arange(across * across, dtype=jnp.int32)[:, None] == target[None, :]
        pieces.append(member.astype(jnp.float32) / (extent * extent))
    return jnp.concatenate(pieces, 0)


def local(features, neighbours, pairing, valid_tiles, cotangent):
    tile_count = features.shape[1]
    half_rows = cotangent.shape[2]
    pool_weights = pool_weights_table()
    present = lax.all_gather(features, "chan", axis=3, tiled=True)
    framed = with_halo(present, (("frame", 0),), 1)
    partners = jnp.stack([framed[0], framed[2]], 0)
    window = with_halo(partners, (("tile", 1),), tile_count)
    pyramid = jnp.einsum(
        "mp,jwpc->jwmc",
        pool_weights.astype(jnp.bfloat16),
        window,
        preferred_element_type=jnp.float32,
    ).astype(jnp.bfloat16)
    core_index = lax.axis_index("chan")
    queries = lax.dynamic_slice_in_dim(present[0], core_index * half_rows, half_rows, 1)
    valid_local = lax.dynamic_slice_in_dim(valid_tiles, core_index * half_rows, half_rows, 1)
    slot_ids = neighbours - (lax.axis_index("tile") * tile_count - tile_count)
    chosen = pyramid[:, slot_ids]
    gates = pairing[0].astype(jnp.float32) / math.sqrt(CHANNELS)
    scores = jnp.einsum("apc,jakmc->japkm", queries, chosen, preferred_element_type=jnp.float32)
    summed = (
        jnp.sum(gates[:, None, None, None, None] * scores, axis=0)
        * valid_local.astype(jnp.float32)[:, :, None, None]
    )
    volume = summed.reshape(tile_count, half_rows, NEIGHBOURS * LEVELS).astype(jnp.bfloat16)[None]
    upstream = cotangent[0].reshape(tile_count, half_rows, NEIGHBOURS, LEVELS)
    upstream = upstream * valid_local.astype(jnp.bfloat16)[:, :, None, None]
    partial_query = jnp.einsum(
        "apkm,jakmc->japc", upstream, chosen, preferred_element_type=jnp.float32
    )
    query_grad = jnp.sum(gates[:, None, None, None] * partial_query, axis=0)
    base_grad = jnp.einsum("apkm,apc->akmc", upstream, queries, preferred_element_type=jnp.float32)
    member = (
        slot_ids[:, :, None] == jnp.arange(3 * tile_count, dtype=jnp.int32)[None, None, :]
    ).astype(jnp.float32)
    weighted_member = gates[:, None, None, None] * member[None]
    window_grad = jnp.einsum(
        "akmc,jakw->jwmc", base_grad, weighted_member, precision=lax.Precision.HIGHEST
    )
    window_grad = jnp.einsum(
        "mp,jwmc->jwpc", pool_weights, window_grad, precision=lax.Precision.HIGHEST
    )
    spread = with_halo(window_grad.astype(jnp.bfloat16), (("tile", 1),), tile_count).astype(
        window_grad.dtype
    )
    returned = (
        spread[:, :tile_count]
        + spread[:, 2 * tile_count : 3 * tile_count]
        + spread[:, 4 * tile_count :]
    )
    framed_back = with_halo(returned.astype(jnp.bfloat16), (("frame", 0),), 1).astype(
        returned.dtype
    )
    key_grad = framed_back[0] + framed_back[3]
    placed = lax.dynamic_update_slice_in_dim(
        jnp.zeros(key_grad.shape, jnp.float32), query_grad, core_index * half_rows, 1
    )
    feature_grad = lax.psum_scatter(key_grad + placed, "chan", scatter_dimension=2, tiled=True)
    return (volume, feature_grad[None])


def solution(mesh):
    return jax.shard_map(
        local,
        mesh=mesh,
        in_specs=(
            P(("clip", "frame"), "tile", None, "chan"),
            P(("clip", "tile"), None),
            P(("clip", "frame"), None),
            P(("clip", "tile"), None),
            P(("clip", "frame"), "tile", "chan", None),
        ),
        out_specs=(
            P(("clip", "frame"), "tile", "chan", None),
            P(("clip", "frame"), "tile", None, "chan"),
        ),
        check_vma=False,
    )
```

profile of v0, /device:TPU:0, one launch (start us, length us, event | category | flops | bytes accessed | tf_op | source)
XLA Modules:
  0.0 115.7 jit_solution(81603316902151556)
XLA Ops:
  7.2 0.0 reduce-scatter.2.cloned.1.call-start
  7.2 2.3 %all_gather.3 = bf16[1,2,256,256]{3,2,1,0:T(8,128)(2,1)S(1)} all-gather(bf16[1,2,256,128]{3,2,1,0:T(8,128)(2,1)} %param.5), channel_id=1, replica_groups=mesh['clip'=2,'tile'=4,'frame'=2,'chan'=2] {'chan'}, dimensions={3}, use_global_device_ids=true | all-gather | bytes 393216 | tf_op jit(solution)/shard_map/all_gather | solution.py:49
  9.5 0.0 copy-start.1
  9.5 0.7 compare_select_fusion
  10.2 0.7 multiply_bitcast_fusion
  11.0 0.7 fusion.73
  11.7 2.4 %fusion.38 = f32[2,9,340,256]{3,2,1,0:T(8,128)S(1)} fusion(bf16[2,128,9,340]{1,0,3,2:T(2,128)(2,1)} %bitcast.89, bf16[2,128]{1,0:T(2,128)(2,1)S(1)} %get-tuple-element.14, bf16[1,2,256,256]{3,2,1,0:T(8,128)(2,1)S(1)} %all_gather.3, s32[]{:T(128)S(6)} %select_n.113), kind=kOutput, calls=%fused_computation.27 | convolution fusion | flops 401863680 | bytes 7965188 | tf_op jit(solution)/shard_map/apkm,apc->akmc/dot_general | solution.py:77
  14.0 11.3 %fusion.11 = f32[2,6,340,256]{3,1,2,0:T(8,128)S(1)} fusion(f32[2,9,340,256]{3,2,1,0:T(8,128)S(1)} %fusion.38, f32[2,9,6]{1,2,0:T(8,128)S(1)} %fusion.64, f32[2]{0:T(128)S(1)} %multiply_bitcast_fusion), kind=kOutput, calls=%fused_computation.14 | convolution fusion | flops 225607904 | bytes 10445240 | tf_op jit(solution)/shard_map/akmc,jakw->jwmc/dot_general | solution.py:82
  25.4 8.4 %fusion.25 = bf16[2,6,256,256]{2,3,1,0:T(8,128)(2,1)S(1)} fusion(f32[2,6,340,256]{3,1,2,0:T(8,128)S(1)} %fusion.11, f32[4,256]{1,0:T(4,128)S(1)} %fusion.65, f32[16,256]{1,0:T(8,128)S(1)} %fusion.61, f32[64,256]{1,0:T(8,128)S(1)} %fusion.58, f32[256,256]{1,0:T(8,128)S(1)} %fusion.50), kind=kOutput, calls=%fused_computation.24 | convolution fusion | flops 3209690112 | bytes 6098944 | tf_op jit(solution)/shard_map/mp,jwmc->jwpc/dot_general | solution.py:85
  33.8 0.1 fusion.78
  33.8 4.9 %collective-permute-start.4 = (bf16[2,2,256,256]{2,3,1,0:T(8,128)(2,1)S(1)}, bf16[2,2,256,256]{2,3,1,0:T(8,128)(2,1)S(1)}, u32[]{:S(2)}, u32[]{:S(2)}) collective-permute-start(bf16[2,2,256,256]{2,3,1,0:T(8,128)(2,1)S(1)} %get-tuple-element.10), channel_id=1, source_target_pairs={{0,4},{4,8},{8,12},{1,5},{5,9},{9,13},{2,6},{6,10},{10,14},{3,7},{... | collective-permute-start | bytes 1572872 | tf_op jit(solution)/shard_map/ppermute | solution.py:23
  38.7 1.3 %collective-permute-start.5 = (bf16[2,2,256,256]{2,3,1,0:T(8,128)(2,1)S(1)}, bf16[2,2,256,256]{2,3,1,0:T(8,128)(2,1)S(1)}, u32[]{:S(2)}, u32[]{:S(2)}) collective-permute-start(bf16[2,2,256,256]{2,3,1,0:T(8,128)(2,1)S(1)} %get-tuple-element.11), channel_id=1, source_target_pairs={{4,0},{8,4},{12,8},{5,1},{9,5},{13,9},{6,2},{10,6},{14,10},{7,3},{... | collective-permute-start | bytes 1572872 | tf_op jit(solution)/shard_map/ppermute | solution.py:25
  40.0 3.4 %collective-permute-start = (bf16[1,2,256,256]{3,2,1,0:T(8,128)(2,1)S(1)}, bf16[1,2,256,256]{3,2,1,0:T(8,128)(2,1)S(1)}, u32[]{:S(2)}, u32[]{:S(2)}) collective-permute-start(bf16[1,2,256,256]{3,2,1,0:T(8,128)(2,1)S(1)} %all_gather.3), channel_id=1, source_target_pairs={{0,2},{1,3},{4,6},{5,7},{8,10},{9,11},{12,14},{13,15},{16,18},{17,... | collective-permute-start | bytes 786440 | tf_op jit(solution)/shard_map/ppermute | solution.py:23
  43.4 0.0 copy-done.1
  43.4 1.3 %collective-permute-start.1 = (bf16[1,2,256,256]{3,2,1,0:T(8,128)(2,1)S(1)}, bf16[1,2,256,256]{3,2,1,0:T(8,128)(2,1)S(1)}, u32[]{:S(2)}, u32[]{:S(2)}) collective-permute-start(bf16[1,2,256,256]{3,2,1,0:T(8,128)(2,1)S(1)} %all_gather.3), channel_id=1, source_target_pairs={{2,0},{3,1},{6,4},{7,5},{10,8},{11,9},{14,12},{15,13},{18,16},{19,... | collective-permute-start | bytes 786440 | tf_op jit(solution)/shard_map/ppermute | solution.py:25
  44.7 4.2 %collective-permute-done = bf16[1,2,256,256]{3,2,1,0:T(8,128)(2,1)S(1)} collective-permute-done((bf16[1,2,256,256]{3,2,1,0:T(8,128)(2,1)S(1)}, bf16[1,2,256,256]{3,2,1,0:T(8,128)(2,1)S(1)}, u32[]{:S(2)}, u32[]{:S(2)}) %collective-permute-start) | collective-permute-done | bytes 262176 | tf_op jit(solution)/shard_map/ppermute | solution.py:23
  49.0 0.7 constant_dynamic-update-slice_fusion.1
  49.7 3.4 %collective-permute-done.1 = bf16[1,2,256,256]{3,2,1,0:T(8,128)(2,1)S(1)} collective-permute-done((bf16[1,2,256,256]{3,2,1,0:T(8,128)(2,1)S(1)}, bf16[1,2,256,256]{3,2,1,0:T(8,128)(2,1)S(1)}, u32[]{:S(2)}, u32[]{:S(2)}) %collective-permute-start.1) | collective-permute-done | bytes 262176 | tf_op jit(solution)/shard_map/ppermute | solution.py:25
  53.1 0.7 constant_dynamic-update-slice_fusion
  53.9 4.3 %collective-permute-start.2 = (bf16[2,2,256,256]{3,2,1,0:T(8,128)(2,1)}, bf16[2,2,256,256]{3,2,1,0:T(8,128)(2,1)S(1)}, u32[]{:S(2)}, u32[]{:S(2)}) collective-permute-start(bf16[2,2,256,256]{3,2,1,0:T(8,128)(2,1)} %constant_dynamic-update-slice_fusion), channel_id=1, source_target_pairs={{0,4},{4,8},{8,12},{1,5},{5,9},{9,13},{2,6},{6,10},{10,14},{3,7},{... | collective-permute-start | bytes 1572872 | tf_op jit(solution)/shard_map/ppermute | solution.py:23
  58.1 1.3 %collective-permute-start.3 = (bf16[2,2,256,256]{3,2,1,0:T(8,128)(2,1)}, bf16[2,2,256,256]{3,2,1,0:T(8,128)(2,1)}, u32[]{:S(2)}, u32[]{:S(2)}) collective-permute-start(bf16[2,2,256,256]{3,2,1,0:T(8,128)(2,1)} %constant_dynamic-update-slice_fusion), channel_id=1, source_target_pairs={{4,0},{8,4},{12,8},{5,1},{9,5},{13,9},{6,2},{10,6},{14,10},{7,3},{... | collective-permute-start | bytes 1572872 | tf_op jit(solution)/shard_map/ppermute | solution.py:25
  59.4 0.0 collective-permute-done.4
  59.5 0.0 collective-permute-done.5
  59.5 0.3 fusion.45
  59.8 1.5 %collective-permute-start.6 = (bf16[1,2,256,256]{2,3,1,0:T(8,128)(2,1)S(1)}, bf16[1,2,256,256]{2,3,1,0:T(8,128)(2,1)S(1)}, u32[]{:S(2)}, u32[]{:S(2)}) collective-permute-start(bf16[1,2,256,256]{2,3,1,0:T(8,128)(2,1)S(1)} %get-tuple-element.12), channel_id=1, source_target_pairs={{0,2},{1,3},{4,6},{5,7},{8,10},{9,11},{12,14},{13,15},{16,18},{17,... | collective-permute-start | bytes 786440 | tf_op jit(solution)/shard_map/ppermute | solution.py:23
  61.3 1.5 %collective-permute-start.7 = (bf16[1,2,256,256]{2,3,1,0:T(8,128)(2,1)S(1)}, bf16[1,2,256,256]{2,3,1,0:T(8,128)(2,1)S(1)}, u32[]{:S(2)}, u32[]{:S(2)}) collective-permute-start(bf16[1,2,256,256]{2,3,1,0:T(8,128)(2,1)S(1)} %get-tuple-element.13), channel_id=1, source_target_pairs={{2,0},{3,1},{6,4},{7,5},{10,8},{11,9},{14,12},{15,13},{18,16},{19,... | collective-permute-start | bytes 786440 | tf_op jit(solution)/shard_map/ppermute | solution.py:25
  62.8 0.1 reshape.150
  62.9 2.3 %collective-permute-done.6 = bf16[1,2,256,256]{2,3,1,0:T(8,128)(2,1)S(1)} collective-permute-done((bf16[1,2,256,256]{2,3,1,0:T(8,128)(2,1)S(1)}, bf16[1,2,256,256]{2,3,1,0:T(8,128)(2,1)S(1)}, u32[]{:S(2)}, u32[]{:S(2)}) %collective-permute-start.6) | collective-permute-done | bytes 262176 | tf_op jit(solution)/shard_map/ppermute | solution.py:23
  65.2 4.3 %collective-permute-done.7 = bf16[1,2,256,256]{2,3,1,0:T(8,128)(2,1)S(1)} collective-permute-done((bf16[1,2,256,256]{2,3,1,0:T(8,128)(2,1)S(1)}, bf16[1,2,256,256]{2,3,1,0:T(8,128)(2,1)S(1)}, u32[]{:S(2)}, u32[]{:S(2)}) %collective-permute-start.7) | collective-permute-done | bytes 262176 | tf_op jit(solution)/shard_map/ppermute | solution.py:25
  69.5 0.1 convert_add_fusion.1
  69.7 0.0 collective-permute-done.2
  69.7 0.0 copy-start.3
  69.7 0.8 copy-done.3
  70.5 1.8 %collective-permute-done.3 = bf16[2,2,256,256]{3,2,1,0:T(8,128)(2,1)} collective-permute-done((bf16[2,2,256,256]{3,2,1,0:T(8,128)(2,1)}, bf16[2,2,256,256]{3,2,1,0:T(8,128)(2,1)}, u32[]{:S(2)}, u32[]{:S(2)}) %collective-permute-start.3) | collective-permute-done | bytes 524320 | tf_op jit(solution)/shard_map/ppermute | solution.py:25
  72.3 2.1 %convert_bitcast_fusion = bf16[2,6,340,256]{3,2,1,0:T(8,128)(2,1)S(1)} fusion(bf16[2,2,256,256]{3,2,1,0:T(8,128)(2,1)} %collective-permute-done.3, bf16[2,2,256,256]{3,2,1,0:T(8,128)(2,1)} %constant_dynamic-update-slice_fusion, bf16[2,2,256,256]{3,2,1,0:T(8,128)(2,1)} %copy-done.3, f32[4,256]{1,0:T(4,128)S(1)} %fusion.65, f32[16,256]{1,0:T(8,128)S(1)} %fusion.61, ...), kind=kOutput, calls=%fused_computation.15 | convolution fusion | flops 538087424 | bytes 4009984 | tf_op jit(solution)/shard_map/mp,jwpc->jwmc/dot_general | solution.py:53
  74.4 4.7 %gather_fusion = bf16[18,2,340,256]{3,2,1,0:T(8,128)(2,1)} fusion(bf16[2,6,340,256]{3,2,1,0:T(8,128)(2,1)S(1)} %convert_bitcast_fusion, s32[1024]{0:T(1024)S(1)} %pad_clamp_fusion), kind=kCustom, calls=%fused_computation | custom fusion | bytes 12533832 | tf_op jit(solution)/shard_map/gather | solution.py:63
  79.1 0.0 copy-start.2
  79.1 6.0 %fusion.39 = f32[2,256,128]{2,1,0:T(8,128)S(1)} fusion(bf16[2,128,9,340]{1,0,3,2:T(2,128)(2,1)} %bitcast.90, bf16[2,9,2,340,256]{4,3,2,1,0:T(8,128)(2,1)} %bitcast.85, bf16[2,128]{1,0:T(2,128)(2,1)S(1)} %get-tuple-element.14, f32[2]{0:T(128)S(1)} %multiply_bitcast_fusion), kind=kOutput, calls=%fused_computation.28 | convolution fusion | flops 803140608 | bytes 8096264 | tf_op jit(solution)/shard_map/apkm,jakmc->japc/dot_general | solution.py:73
  85.2 0.0 copy-start
  85.2 0.8 copy-done
  86.0 0.0 reduce-scatter.2.cloned.1.call-update
  86.0 0.0 copy-done.2
  86.0 6.6 %multiply_reduce_fusion = f32[2,9,340,128]{3,2,1,0:T(8,128)} fusion(f32[2]{0:T(128)S(1)} %multiply_bitcast_fusion, bf16[2,9,2,340,256]{4,3,2,1,0:T(8,128)(2,1)} %bitcast.86, bf16[1,2,256,256]{3,2,1,0:T(8,128)(2,1)S(1)} %copy-done.2, s32[]{:T(128)S(6)} %select_n.113), kind=kOutput, calls=%fused_computation.8 | convolution fusion | flops 804510720 | bytes 9531908 | tf_op jit(solution)/shard_map/apc,jakmc->japkm/dot_general | solution.py:65
  92.6 2.1 %reduce_sum.26 = f32[1,2,128,3060]{2,3,1,0:T(8,128)S(1)} reshape(f32[2,128,9,340]{1,3,2,0:T(8,128)} %bitcast.88) | data formatting | bytes 6266880 | tf_op jit(solution)/shard_map/reduce_sum | solution.py:67
  94.7 0.2 multiply_convert_fusion
  94.9 12.1 %copy.18 = bf16[1,2,128,3060]{2,1,3,0:T(2,128)(2,1)} copy(bf16[1,2,128,3060]{2,3,1,0:T(8,128)(2,1)S(1)} %multiply_convert_fusion) | data formatting | bytes 3133440
  107.0 0.0 reduce-scatter.2.cloned.1.call-done
  107.0 1.8 %copy.19 = f32[1,2,256,128]{3,2,1,0:T(8,128)} copy(f32[1,2,256,128]{2,3,1,0:T(8,128)} %bitcast.91) | data formatting | bytes 524288
  (11 shorter events, 0.2 us)
Async XLA Ops:
  7.2 99.9 %reduce-scatter.2.cloned.1.call-start = ((), (), s32[]{:S(2)}) async-start(), calls=%async_computation.1 | async-start | bytes 786432 | tf_op jit(solution)/shard_map/reduce_scatter | solution.py:103
  9.5 33.9 %copy-start.1 = (bf16[1,2,256,256]{3,2,1,0:T(8,128)(2,1)}, bf16[1,2,256,256]{3,2,1,0:T(8,128)(2,1)S(1)}, u32[]{:S(2)}) copy-start(bf16[1,2,256,256]{3,2,1,0:T(8,128)(2,1)S(1)} %all_gather.3) | copy-start | bytes 786436
  33.8 25.6 %collective-permute-start.4 = (bf16[2,2,256,256]{2,3,1,0:T(8,128)(2,1)S(1)}, bf16[2,2,256,256]{2,3,1,0:T(8,128)(2,1)S(1)}, u32[]{:S(2)}, u32[]{:S(2)}) collective-permute-start(bf16[2,2,256,256]{2,3,1,0:T(8,128)(2,1)S(1)} %get-tuple-element.10), channel_id=1, source_target_pairs={{0,4},{4,8},{8,12},{1,5},{5,9},{9,13},{2,6},{6,10},{10,14},{3,7},{... | collective-permute-start | bytes 1572872 | tf_op jit(solution)/shard_map/ppermute | solution.py:23
  38.7 20.7 %collective-permute-start.5 = (bf16[2,2,256,256]{2,3,1,0:T(8,128)(2,1)S(1)}, bf16[2,2,256,256]{2,3,1,0:T(8,128)(2,1)S(1)}, u32[]{:S(2)}, u32[]{:S(2)}) collective-permute-start(bf16[2,2,256,256]{2,3,1,0:T(8,128)(2,1)S(1)} %get-tuple-element.11), channel_id=1, source_target_pairs={{4,0},{8,4},{12,8},{5,1},{9,5},{13,9},{6,2},{10,6},{14,10},{7,3},{... | collective-permute-start | bytes 1572872 | tf_op jit(solution)/shard_map/ppermute | solution.py:25
  40.0 9.0 %collective-permute-start = (bf16[1,2,256,256]{3,2,1,0:T(8,128)(2,1)S(1)}, bf16[1,2,256,256]{3,2,1,0:T(8,128)(2,1)S(1)}, u32[]{:S(2)}, u32[]{:S(2)}) collective-permute-start(bf16[1,2,256,256]{3,2,1,0:T(8,128)(2,1)S(1)} %all_gather.3), channel_id=1, source_target_pairs={{0,2},{1,3},{4,6},{5,7},{8,10},{9,11},{12,14},{13,15},{16,18},{17,... | collective-permute-start | bytes 786440 | tf_op jit(solution)/shard_map/ppermute | solution.py:23
  43.4 9.7 %collective-permute-start.1 = (bf16[1,2,256,256]{3,2,1,0:T(8,128)(2,1)S(1)}, bf16[1,2,256,256]{3,2,1,0:T(8,128)(2,1)S(1)}, u32[]{:S(2)}, u32[]{:S(2)}) collective-permute-start(bf16[1,2,256,256]{3,2,1,0:T(8,128)(2,1)S(1)} %all_gather.3), channel_id=1, source_target_pairs={{2,0},{3,1},{6,4},{7,5},{10,8},{11,9},{14,12},{15,13},{18,16},{19,... | collective-permute-start | bytes 786440 | tf_op jit(solution)/shard_map/ppermute | solution.py:25
  53.9 15.8 %collective-permute-start.2 = (bf16[2,2,256,256]{3,2,1,0:T(8,128)(2,1)}, bf16[2,2,256,256]{3,2,1,0:T(8,128)(2,1)S(1)}, u32[]{:S(2)}, u32[]{:S(2)}) collective-permute-start(bf16[2,2,256,256]{3,2,1,0:T(8,128)(2,1)} %constant_dynamic-update-slice_fusion), channel_id=1, source_target_pairs={{0,4},{4,8},{8,12},{1,5},{5,9},{9,13},{2,6},{6,10},{10,14},{3,7},{... | collective-permute-start | bytes 1572872 | tf_op jit(solution)/shard_map/ppermute | solution.py:23
  58.1 14.1 %collective-permute-start.3 = (bf16[2,2,256,256]{3,2,1,0:T(8,128)(2,1)}, bf16[2,2,256,256]{3,2,1,0:T(8,128)(2,1)}, u32[]{:S(2)}, u32[]{:S(2)}) collective-permute-start(bf16[2,2,256,256]{3,2,1,0:T(8,128)(2,1)} %constant_dynamic-update-slice_fusion), channel_id=1, source_target_pairs={{4,0},{8,4},{12,8},{5,1},{9,5},{13,9},{6,2},{10,6},{14,10},{7,3},{... | collective-permute-start | bytes 1572872 | tf_op jit(solution)/shard_map/ppermute | solution.py:25
  59.8 5.4 %collective-permute-start.6 = (bf16[1,2,256,256]{2,3,1,0:T(8,128)(2,1)S(1)}, bf16[1,2,256,256]{2,3,1,0:T(8,128)(2,1)S(1)}, u32[]{:S(2)}, u32[]{:S(2)}) collective-permute-start(bf16[1,2,256,256]{2,3,1,0:T(8,128)(2,1)S(1)} %get-tuple-element.12), channel_id=1, source_target_pairs={{0,2},{1,3},{4,6},{5,7},{8,10},{9,11},{12,14},{13,15},{16,18},{17,... | collective-permute-start | bytes 786440 | tf_op jit(solution)/shard_map/ppermute | solution.py:23
  61.3 8.3 %collective-permute-start.7 = (bf16[1,2,256,256]{2,3,1,0:T(8,128)(2,1)S(1)}, bf16[1,2,256,256]{2,3,1,0:T(8,128)(2,1)S(1)}, u32[]{:S(2)}, u32[]{:S(2)}) collective-permute-start(bf16[1,2,256,256]{2,3,1,0:T(8,128)(2,1)S(1)} %get-tuple-element.13), channel_id=1, source_target_pairs={{2,0},{3,1},{6,4},{7,5},{10,8},{11,9},{14,12},{15,13},{18,16},{19,... | collective-permute-start | bytes 786440 | tf_op jit(solution)/shard_map/ppermute | solution.py:25
  69.7 0.8 copy-start.3
  79.1 6.9 %copy-start.2 = (bf16[1,2,256,256]{3,2,1,0:T(8,128)(2,1)S(1)}, bf16[1,2,256,256]{3,2,1,0:T(8,128)(2,1)}, u32[]{:S(2)}) copy-start(bf16[1,2,256,256]{3,2,1,0:T(8,128)(2,1)} %copy-done.1) | copy-start | bytes 786436
  85.2 0.8 copy-start
Sparse Core Ops, SparseCore 0:
  86.1 8.3 reduce-scatter.1
where the time goes:
time: 116 us
  matrix products  36.8 us (32%)
  local copies, waits for them, and re-layouts  23.9 us (21%)
  starting transfers between devices  19.5 us (17%)
  waiting for transfers between devices  16.2 us (14%)
  between operations  14.3 us (12%)
  other arithmetic  2.76 us (2%)
  blocking collectives  2.3 us (2%)
    unnamed x12, local copies, waits for them, and re-layouts  16.3 us
    ppermute x4, starting transfers between devices, with_halo(): lax.ppermute(tail, axis, [(i, (i + 1) % count) for i in range(ends)])  14 us
    dot_general x1, matrix products, local(): jnp.einsum('akmc,jakw->jwmc', base_grad, weighted_member, precision=lax.P...  11.3 us
    ppermute x4, waiting for transfers between devices, with_halo(): lax.ppermute(head, axis, [((i + 1) % count, i) for i in range(ends)])  9.58 us
    dot_general x1, matrix products, local(): jnp.einsum('mp,jwmc->jwpc', pool_weights, window_grad, precision=lax.Prec...  8.35 us
    dot_general x1, matrix products, local(): jnp.einsum('apc,jakmc->japkm', queries, chosen, preferred_element_type=jn...  6.57 us
    ppermute x4, waiting for transfers between devices, with_halo(): lax.ppermute(tail, axis, [(i, (i + 1) % count) for i in range(ends)])  6.56 us
    dot_general x1, matrix products, local(): jnp.einsum('apkm,jakmc->japc', upstream, chosen, preferred_element_type=j...  5.99 us
  transfers between devices with their start and end apart: 9, of which 5 were waited for; matrix products, arithmetic and copies ran while one was open for 20% of the time, Pallas kernels for 0%

commit v1 on v0

v1 whole, which is shorter than its diff:
```python
import functools

import jax
import jax.numpy as jnp
import numpy as np
from jax import lax
from jax.experimental import pallas as pl
from jax.experimental.pallas import tpu as pltpu
from jax.sharding import PartitionSpec as P

CHANNELS = 256
SIDE = 16
PIXELS = 256
LEVELS = 340
NEIGHBOURS = 9
REACH = 2
SPAN = 2 * REACH + 1
COARSE = LEVELS - PIXELS
PAD = 128
WIDE = PIXELS + PAD

VMEM = pl.BlockSpec(memory_space=pltpu.VMEM)
SMEM = pl.BlockSpec(memory_space=pltpu.SMEM)


def coarse_weights():
    pixel = np.arange(PIXELS)
    rows, columns = pixel // SIDE, pixel % SIDE
    table = np.zeros((PAD, PIXELS), np.float32)
    base = 0
    for extent in (2, 4, 8):
        across = SIDE // extent
        cell = rows // extent * across + columns // extent
        table[base + cell, pixel] = 1.0 / (extent * extent)
        base += across * across
    return table


def even_pairs(count):
    pairs = []
    for i in range(0, count - 1, 2):
        pairs += [(i, i + 1), (i + 1, i)]
    if count % 2:
        pairs.append((count - 1, count - 1))
    return pairs


def odd_pairs(count, cores):
    pairs, paired = [], set()
    for i in range(1, count - 1, 2):
        paired |= {i, i + 1}
        for c in range(cores):
            pairs += [(i * cores + c, (i + 1) * cores + c), ((i + 1) * cores + c, i * cores + c)]
    for i in range(count):
        if i not in paired:
            pairs += [(i * cores + c, i * cores + (c + 1) % cores) for c in range(cores)]
    return pairs


def frame_links(count):
    if count == 2:
        swap = [(0, 1), (1, 0)]
        return [(swap, swap)]
    onward = [(i, i + 1) for i in range(count - 1)]
    back = [(i + 1, i) for i in range(count - 1)]
    return [(onward, back), (back, onward)]


def column_of(row):
    n = row.shape[1]
    diagonal = lax.broadcasted_iota(jnp.int32, (n, n), 0) == lax.broadcasted_iota(jnp.int32, (n, n), 1)
    return jnp.sum(jnp.where(diagonal, row, 0.0), axis=1, keepdims=True)


def valid_column(valid_ref, a, core, half):
    row = valid_ref[a : a + 1, :].astype(jnp.float32)
    return column_of(jnp.where(core == 0, row[:, :half], row[:, half:]))


def relative(neighbours_ref, a, k, first):
    return neighbours_ref[a, k] - (first + a) + REACH


def fold_kernel(tiles, half, neighbours_ref, valid_ref, pool_ref, cot_ref, up_ref, down_ref, acc):
    core = lax.axis_index("chan")
    first = lax.axis_index("tile") * tiles
    pool = pool_ref[...]
    for a in range(tiles):
        acc[...] = jnp.zeros_like(acc)
        for k in range(NEIGHBOURS):
            w = relative(neighbours_ref, a, k, first)
            piece = cot_ref[0, a, :, k * LEVELS : (k + 1) * LEVELS].astype(jnp.float32)
            acc[w, :, :LEVELS] += piece
        keep = valid_column(valid_ref, a, core, half)
        for w in range(SPAN):
            total = acc[w] * keep
            rounded = total.astype(jnp.bfloat16)
            up_ref[a, w] = rounded
            spread = jnp.dot(rounded[:, PIXELS:], pool, preferred_element_type=jnp.float32)
            down_ref[a, w] = (total[:, :PIXELS] + spread).astype(jnp.bfloat16)


def fold(neighbours, valid, pool, cotangent):
    tiles, half = cotangent.shape[1], cotangent.shape[2]
    return pl.pallas_call(
        functools.partial(fold_kernel, tiles, half),
        out_shape=(
            jax.ShapeDtypeStruct((tiles, SPAN, half, WIDE), jnp.bfloat16),
            jax.ShapeDtypeStruct((tiles, SPAN, half, PIXELS), jnp.bfloat16),
        ),
        in_specs=[SMEM, VMEM, VMEM, VMEM],
        out_specs=(VMEM, VMEM),
        scratch_shapes=[pltpu.VMEM((SPAN, half, WIDE), jnp.float32)],
        compiler_params=pltpu.CompilerParams(vmem_limit_bytes=24 * 2**20),
        cost_estimate=pl.CostEstimate(flops=2 * 10**8, bytes_accessed=4 * 10**6, transcendentals=0),
        name="fold",
    )(neighbours, valid, pool, cotangent)


def keys_kernel(tiles, half, x_ref, mine_ref, other_ref, own_ref, even_ref, odd_ref, window):
    core = lax.axis_index("chan")
    tile = lax.axis_index("tile")
    for a in range(tiles):
        here = x_ref[a, pl.ds(pl.multiple_of(core * half, half), half), :]
        there = x_ref[a, pl.ds(pl.multiple_of((1 - core) * half, half), half), :]
        turned = jnp.concatenate([here, there], axis=0).astype(jnp.float32).T.astype(jnp.bfloat16)
        for w in range(SPAN):
            grads = jnp.concatenate([mine_ref[a, w], other_ref[a, w]], axis=0)
            term = jnp.dot(turned, grads, preferred_element_type=jnp.float32)
            slot = a + w
            if a == 0 or w == SPAN - 1:
                window[slot] = term
            else:
                window[slot] += term
    own_ref[...] = window[tiles : 2 * tiles]
    parity = lax.rem(tile, 2)
    even = (1 - parity) * 2 * tiles
    odd = parity * 2 * tiles
    for a in range(tiles):
        even_ref[a] = window[even + a].astype(jnp.bfloat16)
        odd_ref[a] = window[odd + a].astype(jnp.bfloat16)


def keys(x, mine, other):
    tiles, pixels, channels = x.shape
    half = mine.shape[2]
    shape = (tiles, channels, pixels)
    return pl.pallas_call(
        functools.partial(keys_kernel, tiles, half),
        out_shape=(
            jax.ShapeDtypeStruct(shape, jnp.float32),
            jax.ShapeDtypeStruct(shape, jnp.bfloat16),
            jax.ShapeDtypeStruct(shape, jnp.bfloat16),
        ),
        in_specs=[VMEM] * 3,
        out_specs=(VMEM,) * 3,
        scratch_shapes=[pltpu.VMEM((3 * tiles, channels, pixels), jnp.float32)],
        compiler_params=pltpu.CompilerParams(vmem_limit_bytes=24 * 2**20),
        cost_estimate=pl.CostEstimate(flops=4 * 10**8, bytes_accessed=2 * 10**6, transcendentals=0),
        name="keys",
    )(x, mine, other)


def gate(pairing_ref, j, partners):
    if partners == 1:
        column = 1 - lax.axis_index("frame")
    else:
        column = j
    return pairing_ref[0, column].astype(jnp.float32) / 16.0


def returns_kernel(partners, pairing_ref, own_ref, even_ref, odd_ref, *out_refs):
    tile, count = lax.axis_index("tile"), lax.axis_size("tile")
    parity = lax.rem(tile, 2)
    has_even = jnp.logical_or(parity == 1, tile + 1 < count)
    has_odd = jnp.logical_or(jnp.logical_and(parity == 0, tile > 0), jnp.logical_and(parity == 1, tile + 1 < count))
    total = own_ref[...]
    total = total + jnp.where(has_even, even_ref[...].astype(jnp.float32), 0.0)
    total = total + jnp.where(has_odd, odd_ref[...].astype(jnp.float32), 0.0)
    for j in range(partners):
        out_refs[j][...] = (total * gate(pairing_ref, j, partners)).astype(jnp.bfloat16)


def returns(partners, pairing, own, even, odd):
    return pl.pallas_call(
        functools.partial(returns_kernel, partners),
        out_shape=(jax.ShapeDtypeStruct(own.shape, jnp.bfloat16),) * partners,
        in_specs=[SMEM] + [VMEM] * 3,
        out_specs=(VMEM,) * partners,
        cost_estimate=pl.CostEstimate(flops=10**5, bytes_accessed=5 * 10**5, transcendentals=0),
        name="returns",
    )(pairing, own, even, odd)


def scores_kernel(
    tiles, half, partners, neighbours_ref, pairing_ref, valid_ref, pool_ref, x_ref, xo_ref, up_ref, *refs
):
    inputs, (volume_ref, mine_ref, other_ref, pyramid, queries, table) = refs[: 6 * partners], refs[6 * partners :]
    core, tile = lax.axis_index("chan"), lax.axis_index("tile")
    first = tile * tiles
    parity = lax.rem(tile, 2)
    even = (1 - parity) * 2 * tiles
    odd = parity * 2 * tiles
    pool = pool_ref[...]
    rows = pl.ds(pl.multiple_of(core * half, half), half)
    channels = x_ref.shape[2]

    def both(mine, other):
        return jnp.concatenate([jnp.where(core == 0, mine, other), jnp.where(core == 0, other, mine)], axis=-1)

    for j in range(partners):
        group = inputs[6 * j : 6 * j + 6]
        for part, base in enumerate((tiles, even, odd)):
            for a in range(tiles):
                level = both(group[part][a], group[part + 3][a])
                coarse = jnp.dot(pool, level, preferred_element_type=jnp.float32)
                pyramid[j, base + a, :PIXELS] = level
                pyramid[j, base + a, PIXELS:] = coarse.astype(jnp.bfloat16)
    for a in range(tiles):
        keep = valid_column(valid_ref, a, core, half)
        row = both(x_ref[a, rows, :], xo_ref[a, rows, :]).astype(jnp.float32) * keep
        for j in range(partners):
            queries[j, a * half : (a + 1) * half] = (row * gate(pairing_ref, j, partners)).astype(jnp.bfloat16)
    for a in range(tiles):
        grad = jnp.zeros((half, 2 * channels), jnp.float32)
        for j in range(partners):
            term = jnp.zeros((half, 2 * channels), jnp.float32)
            for w in range(SPAN):
                term += jnp.dot(up_ref[a, w], pyramid[j, a + w], preferred_element_type=jnp.float32)
            grad += term * gate(pairing_ref, j, partners)
        low, high = grad[:, :channels], grad[:, channels:]
        mine_ref[a] = jnp.where(core == 0, low, high)
        other_ref[a] = jnp.where(core == 0, high, low).astype(jnp.bfloat16)
    for s in range(3 * tiles):
        total = jnp.zeros((tiles * half, WIDE), jnp.float32)
        for j in range(partners):
            total += lax.dot_general(
                queries[j], pyramid[j, s], (((1,), (1,)), ((), ())), preferred_element_type=jnp.float32
            )
        table[s] = total.astype(jnp.bfloat16)
    for a in range(tiles):
        for k in range(NEIGHBOURS):
            slot = relative(neighbours_ref, a, k, first) + a
            piece = table[slot, a * half : (a + 1) * half, :]
            volume_ref[0, a, :, k * LEVELS : (k + 1) * LEVELS] = piece[:, :LEVELS]


def scores(partners, neighbours, pairing, valid, pool, x, xo, up, windows):
    tiles, half = up.shape[0], up.shape[2]
    channels = x.shape[2]
    return pl.pallas_call(
        functools.partial(scores_kernel, tiles, half, partners),
        out_shape=(
            jax.ShapeDtypeStruct((1, tiles, half, NEIGHBOURS * LEVELS), jnp.bfloat16),
            jax.ShapeDtypeStruct((tiles, half, channels), jnp.float32),
            jax.ShapeDtypeStruct((tiles, half, channels), jnp.bfloat16),
        ),
        in_specs=[SMEM, SMEM] + [VMEM] * (5 + len(windows)),
        out_specs=(VMEM,) * 3,
        scratch_shapes=[
            pltpu.VMEM((partners, 3 * tiles, WIDE, 2 * channels), jnp.bfloat16),
            pltpu.VMEM((partners, tiles * half, 2 * channels), jnp.bfloat16),
            pltpu.VMEM((3 * tiles, tiles * half, WIDE), jnp.bfloat16),
        ],
        compiler_params=pltpu.CompilerParams(vmem_limit_bytes=32 * 2**20),
        cost_estimate=pl.CostEstimate(flops=10**9, bytes_accessed=4 * 10**6, transcendentals=0),
        name="scores",
    )(neighbours, pairing, valid, pool, x, xo, up, *windows)


def merge_kernel(tiles, half, partners, mine_ref, other_ref, *refs):
    keys_refs, out_ref = refs[:partners], refs[partners]
    core = lax.axis_index("chan")
    here = pl.ds(pl.multiple_of(core * half, half), half)
    there = pl.ds(pl.multiple_of((1 - core) * half, half), half)
    for a in range(tiles):
        total = keys_refs[0][a].astype(jnp.float32)
        for j in range(1, partners):
            total += keys_refs[j][a].astype(jnp.float32)
        out_ref[0, a] = total.T
        out_ref[0, a, here, :] += mine_ref[a]
        out_ref[0, a, there, :] += other_ref[a].astype(jnp.float32)


def merge(mine, other, returned):
    tiles, half, channels = mine.shape
    return pl.pallas_call(
        functools.partial(merge_kernel, tiles, half, len(returned)),
        out_shape=jax.ShapeDtypeStruct((1, tiles, 2 * half, channels), jnp.float32),
        in_specs=[VMEM] * (2 + len(returned)),
        out_specs=VMEM,
        cost_estimate=pl.CostEstimate(flops=10**5, bytes_accessed=7 * 10**5, transcendentals=0),
        name="merge",
    )(mine, other, *returned)


def local(features, neighbours, pairing, valid_tiles, cotangent):
    count = lax.axis_size("tile")
    cores = lax.axis_size("chan")
    links = frame_links(lax.axis_size("frame"))
    partners = len(links)
    pool = jnp.asarray(coarse_weights(), jnp.bfloat16)
    swap = [(c, (c + 1) % cores) for c in range(cores)]
    evens, odds = even_pairs(count), odd_pairs(count, cores)

    def over_even(z):
        return lax.ppermute(z, "tile", evens)

    def over_odd(z):
        return lax.ppermute(z, ("tile", "chan"), odds)

    def over_cores(z):
        return lax.ppermute(z, "chan", swap)

    x = features[0]
    arrived = [lax.ppermute(x, "frame", ahead) for ahead, _ in links]
    xo = over_cores(x)
    up, down = fold(neighbours, valid_tiles, pool, cotangent)
    down_other = over_cores(down)
    own, to_even, to_odd = keys(x, down, down_other)
    windows = []
    for y in arrived:
        parts = [y, over_even(y), over_odd(y)]
        windows += parts + [over_cores(z) for z in parts]
    sent = returns(partners, pairing, own, over_even(to_even), over_odd(to_odd))
    returned = [lax.ppermute(z, "frame", back) for z, (_, back) in zip(sent, links, strict=True)]
    volume, mine, other = scores(partners, neighbours, pairing, valid_tiles, pool, x, xo, up, windows)
    feature_grad = merge(mine, over_cores(other), returned)
    return volume, feature_grad


def solution(mesh):
    return jax.shard_map(
        local,
        mesh=mesh,
        in_specs=(
            P(("clip", "frame"), "tile", None, "chan"),
            P(("clip", "tile"), None),
            P(("clip", "frame"), None),
            P(("clip", "tile"), None),
            P(("clip", "frame"), "tile", "chan", None),
        ),
        out_specs=(
            P(("clip", "frame"), "tile", "chan", None),
            P(("clip", "frame"), "tile", None, "chan"),
        ),
        check_vma=False,
    )
```

time: 116 us -> 37.8 us (0.33)
  matrix products: 36.8 us -> 0 us
  between operations: 14.3 us -> 0.77 us
  local copies, waits for them, and re-layouts: 23.9 us -> 10.7 us
  starting transfers between devices: 19.5 us -> 8.73 us
  Pallas kernels: 0 us -> 8.79 us
  waiting for transfers between devices: 16.2 us -> 8.55 us
  other arithmetic: 2.76 us -> 0 us
  blocking collectives: 2.3 us -> 0 us
    dot_general x6 -> x0, matrix products: 36.8 us -> none  [the longest x1 11.3 us: local(): jnp.einsum('akmc,jakw->jwmc', base_grad, weighted_member, precision=lax.P...]
    ppermute x8 -> x12, starting transfers between devices: 19.4 us -> 8.73 us  [the longest x2 3.42 us: over_even(): return lax.ppermute(z, 'tile', evens)]
    pallas_call x0 -> x5, Pallas kernels: none -> 8.79 us  [the longest x1 2.95 us: scores(): pl.pallas_call(functools.partial(scores_kernel, tiles, half, partners), o...]
    ppermute x8 -> x12, waiting for transfers between devices: 16.1 us -> 8.55 us  [the longest x2 4.44 us: over_even(): return lax.ppermute(z, 'tile', evens)]
    unnamed x12 -> x26, local copies, waits for them, and re-layouts: 16.3 us -> 10.7 us
    gather x1 -> x0, local copies, waits for them, and re-layouts: 4.7 us -> none  [local(): chosen = pyramid[:, slot_ids]]
    all_gather x1 -> x0, blocking collectives: 2.3 us -> none  [local(): present = lax.all_gather(features, 'chan', axis=3, tiled=True)]
    reduce_sum x1 -> x0, local copies, waits for them, and re-layouts: 2.05 us -> none  [local(): jnp.sum(gates[:, None, None, None, None] * scores, axis=0)]
  transfers between devices with their start and end apart: 9 -> 12, of which waited for: 5 -> 3; matrix products, arithmetic and copies ran while one was open for 20% -> 8% of each run, Pallas kernels for 0% -> 14%
where the time goes in v1:
time: 37.8 us; the launch traced here: 37.6 us
  local copies, waits for them, and re-layouts  10.7 us (28%)
  Pallas kernels  8.79 us (23%)
  starting transfers between devices  8.73 us (23%)
  waiting for transfers between devices  8.55 us (23%)
  between operations  0.77 us (2%)
    unnamed x26, local copies, waits for them, and re-layouts  10.7 us
    ppermute x2, waiting for transfers between devices, over_even(): return lax.ppermute(z, 'tile', evens)  4.44 us
    ppermute x1, waiting for transfers between devices, local(): arrived = [lax.ppermute(x, 'frame', ahead) for ahead, _ in links]  4.08 us
    ppermute x2, starting transfers between devices, over_even(): return lax.ppermute(z, 'tile', evens)  3.42 us
    pallas_call x1, Pallas kernels, scores(): pl.pallas_call(functools.partial(scores_kernel, tiles, half, partners), o...  2.95 us
    ppermute x1, starting transfers between devices, local(): arrived = [lax.ppermute(x, 'frame', ahead) for ahead, _ in links]  2.57 us
    pallas_call x1, Pallas kernels, merge(): pl.pallas_call(functools.partial(merge_kernel, tiles, half, len(returned)...  1.88 us
    pallas_call x1, Pallas kernels, returns(): pl.pallas_call(functools.partial(returns_kernel, partners), out_shape=(ja...  1.79 us
  transfers between devices with their start and end apart: 12, of which 3 were waited for; matrix products, arithmetic and copies ran while one was open for 8% of the time, Pallas kernels for 14%

profile of v1, /device:TPU:0, one launch (start us, length us, event | category | flops | bytes accessed | tf_op | source)
XLA Modules:
  0.0 37.6 jit_solution(10243419108774284957)
XLA Ops:
  0.6 0.0 copy-start.2
  0.6 0.0 copy-start.3
  0.7 0.0 copy-start.4
  0.7 3.6 %copy.8.cot_ref = bf16[1,2,128,3060]{3,2,1,0:T(8,128)(2,1)S(1)} copy(bf16[1,2,128,3060]{2,1,3,0:T(2,128)(2,1)} %param.10) | data formatting | bytes 3133440 | tf_op args[4]
  4.3 0.0 copy-done.2
  4.3 0.0 copy-done.3
  4.3 0.0 copy-done.4
  4.3 0.0 copy-start.6
  4.3 0.0 copy-start.5
  4.3 1.7 %fold.1 = (bf16[2,5,128,384]{3,2,1,0:T(8,128)(2,1)S(1)}, bf16[2,5,128,256]{3,2,1,0:T(8,128)(2,1)S(1)}) custom-call(s32[2,9]{1,0:T(2,128)S(1)} %copy-done.4, s32[2,256]{1,0:T(2,128)S(1)} %copy-done.3, bf16[128,256]{1,0:T(8,128)(2,1)S(1)} %copy-done.2, bf16[1,2,128,3060]{3,2,1,0:T(8,128)(2,1)S(1)} %copy.8.cot_ref), custom_call_target="tpu_custom_call" | custom-call | flops 200000000 | bytes 4000000 | tf_op jit(solution)/shard_map/fold/pallas_call | solution.py:105
  6.1 0.5 %collective-permute-start.8 = (bf16[2,5,128,256]{3,2,1,0:T(8,128)(2,1)S(1)}, bf16[2,5,128,256]{3,2,1,0:T(8,128)(2,1)S(1)}, u32[]{:S(2)}, u32[]{:S(2)}) collective-permute-start(bf16[2,5,128,256]{3,2,1,0:T(8,128)(2,1)S(1)} %get-tuple-element.14.mine_ref), channel_id=1, source_target_pairs={{0,1},{1,0},{2,3},{3,2},{4,5},{5,4},{6,7},{7,6},{8,9},{9,8},{10,11... | collective-permute-start | bytes 1966088 | tf_op jit(solution)/shard_map/ppermute | solution.py:313
  6.6 0.0 copy-done.6
  6.6 2.6 %collective-permute-start.1 = (bf16[2,256,128]{2,1,0:T(8,128)(2,1)S(1)}, bf16[2,256,128]{2,1,0:T(8,128)(2,1)S(1)}, u32[]{:S(2)}, u32[]{:S(2)}) collective-permute-start(bf16[2,256,128]{2,1,0:T(8,128)(2,1)S(1)} %bitcast.1), channel_id=1, source_target_pairs={{0,2},{2,0},{1,3},{3,1},{4,6},{6,4},{5,7},{7,5},{8,10},{10,8},{9,1... | collective-permute-start | bytes 393224 | tf_op jit(solution)/shard_map/ppermute | solution.py:316
  9.2 4.1 %collective-permute-done.1.refs_0_ = bf16[2,256,128]{2,1,0:T(8,128)(2,1)S(1)} collective-permute-done((bf16[2,256,128]{2,1,0:T(8,128)(2,1)S(1)}, bf16[2,256,128]{2,1,0:T(8,128)(2,1)S(1)}, u32[]{:S(2)}, u32[]{:S(2)}) %collective-permute-start.1) | collective-permute-done | bytes 131104 | tf_op jit(solution)/shard_map/ppermute | solution.py:316
  13.3 0.0 collective-permute-start.3
  13.3 3.4 %collective-permute-start.2 = (bf16[2,256,128]{2,1,0:T(8,128)(2,1)S(1)}, bf16[2,256,128]{2,1,0:T(8,128)(2,1)S(1)}, u32[]{:S(2)}, u32[]{:S(2)}) collective-permute-start(bf16[2,256,128]{2,1,0:T(8,128)(2,1)S(1)} %collective-permute-done.1.refs_0_), channel_id=1, source_target_pairs={{0,4},{4,0},{8,12},{12,8},{1,5},{5,1},{9,13},{13,9},{2,6},{6,2},{1... | collective-permute-start | bytes 393224 | tf_op jit(solution)/shard_map/ppermute | solution.py:307
  16.7 0.0 collective-permute-done.8.other_ref
  16.7 0.5 %keys.1 = (f32[2,128,256]{2,1,0:T(8,128)S(1)}, bf16[2,128,256]{2,1,0:T(8,128)(2,1)S(1)}, bf16[2,128,256]{2,1,0:T(8,128)(2,1)S(1)}) custom-call(bf16[2,256,128]{2,1,0:T(8,128)(2,1)S(1)} %bitcast.2, bf16[2,5,128,256]{3,2,1,0:T(8,128)(2,1)S(1)} %get-tuple-element.14.mine_ref, bf16[2,5,128,256]{3,2,1,0:T(8,128)(2,1)S(1)} %collective-permute-done.8.other_ref), custom_call_target="tpu_custom_call" | custom-call | flops 400000000 | bytes 2000000 | tf_op jit(solution)/shard_map/keys/pallas_call | solution.py:148
  17.1 0.0 copy-start
  17.1 0.7 %copy-done = f32[2,128,256]{2,1,0:T(8,128)} copy-done((f32[2,128,256]{2,1,0:T(8,128)}, f32[2,128,256]{2,1,0:T(8,128)S(1)}, u32[]{:S(2)}) %copy-start) | copy-done | bytes 262168
  17.8 0.0 collective-permute-start.9
  17.8 0.0 collective-permute-start.10
  17.8 0.5 %collective-permute-start = (bf16[2,256,128]{2,1,0:T(8,128)(2,1)S(1)}, bf16[2,256,128]{2,1,0:T(8,128)(2,1)S(1)}, u32[]{:S(2)}, u32[]{:S(2)}) collective-permute-start(bf16[2,256,128]{2,1,0:T(8,128)(2,1)S(1)} %bitcast.3), channel_id=1, source_target_pairs={{0,1},{1,0},{2,3},{3,2},{4,5},{5,4},{6,7},{7,6},{8,9},{9,8},{10,11... | collective-permute-start | bytes 393224 | tf_op jit(solution)/shard_map/ppermute | solution.py:313
  18.4 0.0 collective-permute-done.3.refs_2_
  18.4 0.0 collective-permute-start.4
  18.4 2.0 %collective-permute-done.2.refs_1_ = bf16[2,256,128]{2,1,0:T(8,128)(2,1)S(1)} collective-permute-done((bf16[2,256,128]{2,1,0:T(8,128)(2,1)S(1)}, bf16[2,256,128]{2,1,0:T(8,128)(2,1)S(1)}, u32[]{:S(2)}, u32[]{:S(2)}) %collective-permute-start.2) | collective-permute-done | bytes 131104 | tf_op jit(solution)/shard_map/ppermute | solution.py:307
  20.4 0.0 collective-permute-start.6
  20.4 2.4 %collective-permute-done.9.even_ref = bf16[2,128,256]{2,1,0:T(8,128)(2,1)S(1)} collective-permute-done((bf16[2,128,256]{2,1,0:T(8,128)(2,1)S(1)}, bf16[2,128,256]{2,1,0:T(8,128)(2,1)S(1)}, u32[]{:S(2)}, u32[]{:S(2)}) %collective-permute-start.9) | collective-permute-done | bytes 131104 | tf_op jit(solution)/shard_map/ppermute | solution.py:307
  22.8 0.0 copy-start.9
  22.8 0.0 collective-permute-start.5
  22.8 0.0 collective-permute-done.10.odd_ref
  22.8 0.0 copy-start.10
  22.8 0.6 %copy-done.9 = bf16[2,128,256]{2,1,0:T(8,128)(2,1)} copy-done((bf16[2,128,256]{2,1,0:T(8,128)(2,1)}, bf16[2,128,256]{2,1,0:T(8,128)(2,1)S(1)}, u32[]{:S(2)}) %copy-start.9) | copy-done | bytes 131096
  23.5 0.0 copy-done.10
  23.5 1.8 %returns.1 = bf16[2,128,256]{2,1,0:T(8,128)(2,1)} custom-call(s32[1,2]{1,0:T(1,128)} %pairing_ref.3, f32[2,128,256]{2,1,0:T(8,128)} %copy-done, bf16[2,128,256]{2,1,0:T(8,128)(2,1)} %copy-done.9, bf16[2,128,256]{2,1,0:T(8,128)(2,1)} %copy-done.10), custom_call_target="tpu_custom_call" | custom-call | flops 100000 | bytes 500000 | tf_op jit(solution)/shard_map/returns/pallas_call | solution.py:185
  25.3 1.5 %collective-permute-start.11 = (bf16[2,128,256]{2,1,0:T(8,128)(2,1)}, bf16[2,128,256]{2,1,0:T(8,128)(2,1)}, u32[]{:S(2)}, u32[]{:S(2)}) collective-permute-start(bf16[2,128,256]{2,1,0:T(8,128)(2,1)} %returns.1), channel_id=1, source_target_pairs={{0,2},{2,0},{1,3},{3,1},{4,6},{6,4},{5,7},{7,5},{8,10},{10,8},{9,1... | collective-permute-start | bytes 393224 | tf_op jit(solution)/shard_map/ppermute | solution.py:326
  26.8 0.0 collective-permute-done.xo_ref
  26.8 0.0 collective-permute-done.4.refs_3_
  26.8 0.0 collective-permute-done.6.refs_5_
  26.8 0.0 collective-permute-done.5.refs_4_
  26.8 0.0 copy-start.7
  26.8 0.6 %copy-done.7 = bf16[2,256,128]{2,1,0:T(8,128)(2,1)} copy-done((bf16[2,256,128]{2,1,0:T(8,128)(2,1)}, bf16[2,256,128]{2,1,0:T(8,128)(2,1)S(1)}, u32[]{:S(2)}) %copy-start.7) | copy-done | bytes 131096
  27.5 0.0 copy-done.5
  27.5 0.0 copy-start.8
  27.5 0.9 %copy-done.8 = bf16[2,256,128]{2,1,0:T(8,128)(2,1)S(1)} copy-done((bf16[2,256,128]{2,1,0:T(8,128)(2,1)S(1)}, bf16[2,256,128]{2,1,0:T(8,128)(2,1)}, u32[]{:S(2)}) %copy-start.8) | copy-done | bytes 131096
  28.4 3.0 %scores.1 = (bf16[1,2,128,3060]{3,2,1,0:T(8,128)(2,1)S(1)}, f32[2,128,128]{2,1,0:T(8,128)S(1)}, bf16[2,128,128]{2,1,0:T(8,128)(2,1)}) custom-call(s32[2,9]{1,0:T(2,128)S(1)} %copy-done.4, s32[1,2]{1,0:T(1,128)S(1)} %copy-done.5, s32[2,256]{1,0:T(2,128)S(1)} %copy-done.3, bf16[128,256]{1,0:T(8,128)(2,1)S(1)} %copy-done.2, bf16[2,256,128]{2,1,0:T(8,128)(2,1)S(1)} %bitcast.4, ...), custom_call_target="tpu_custom_call" | custom-call | flops 1000000000 | bytes 4000000 | tf_op jit(solution)/shard_map/scores/pallas_call | solution.py:251
  31.3 0.0 copy-start.1
  31.3 0.6 %copy-done.1 = f32[2,128,128]{2,1,0:T(8,128)} copy-done((f32[2,128,128]{2,1,0:T(8,128)}, f32[2,128,128]{2,1,0:T(8,128)S(1)}, u32[]{:S(2)}) %copy-start.1) | copy-done | bytes 131096
  32.0 0.2 collective-permute-start.7
  32.2 2.9 %copy.9 = bf16[1,2,128,3060]{2,1,3,0:T(2,128)(2,1)} copy(bf16[1,2,128,3060]{3,2,1,0:T(8,128)(2,1)S(1)} %get-tuple-element.18) | data formatting | bytes 3133440
  35.0 0.0 collective-permute-done.7.other_ref
  35.0 0.0 copy-start.11
  35.0 0.0 collective-permute-done.11.refs_0_
  35.1 0.6 %copy-done.11 = bf16[2,128,128]{2,1,0:T(8,128)(2,1)} copy-done((bf16[2,128,128]{2,1,0:T(8,128)(2,1)}, bf16[2,128,128]{2,1,0:T(8,128)(2,1)S(1)}, u32[]{:S(2)}) %copy-start.11) | copy-done | bytes 65560
  35.7 1.9 %merge.1 = f32[1,2,256,128]{3,2,1,0:T(8,128)} custom-call(f32[2,128,128]{2,1,0:T(8,128)} %copy-done.1, bf16[2,128,128]{2,1,0:T(8,128)(2,1)} %copy-done.11, bf16[2,128,256]{2,1,0:T(8,128)(2,1)} %collective-permute-done.11.refs_0_), custom_call_target="tpu_custom_call" | custom-call | flops 100000 | bytes 700000 | tf_op jit(solution)/shard_map/merge/pallas_call | solution.py:287
Async XLA Ops:
  0.6 3.7 %copy-start.2 = (bf16[128,256]{1,0:T(8,128)(2,1)S(1)}, bf16[128,256]{1,0:T(8,128)(2,1)}, u32[]{:S(2)}) copy-start(bf16[128,256]{1,0:T(8,128)(2,1)} %constant.2.clone.pool_ref) | copy-start | bytes 196612
  0.6 3.7 %copy-start.3 = (s32[2,256]{1,0:T(2,128)S(1)}, s32[2,256]{1,0:T(2,128)}, u32[]{:S(2)}) copy-start(s32[2,256]{1,0:T(2,128)} %valid_ref.3) | copy-start | bytes 6148
  0.7 3.7 %copy-start.4 = (s32[2,9]{1,0:T(2,128)S(1)}, s32[2,9]{1,0:T(2,128)}, u32[]{:S(2)}) copy-start(s32[2,9]{1,0:T(2,128)} %neighbours_ref.3) | copy-start | bytes 220
  4.3 2.3 %copy-start.6 = (bf16[1,2,256,128]{3,2,1,0:T(8,128)(2,1)S(1)}, bf16[1,2,256,128]{3,2,1,0:T(8,128)(2,1)}, u32[]{:S(2)}) copy-start(bf16[1,2,256,128]{3,2,1,0:T(8,128)(2,1)} %param.6) | copy-start | bytes 393220
  4.3 23.1 %copy-start.5 = (s32[1,2]{1,0:T(1,128)S(1)}, s32[1,2]{1,0:T(1,128)}, u32[]{:S(2)}) copy-start(s32[1,2]{1,0:T(1,128)} %pairing_ref.3) | copy-start | bytes 28
  6.1 10.6 %collective-permute-start.8 = (bf16[2,5,128,256]{3,2,1,0:T(8,128)(2,1)S(1)}, bf16[2,5,128,256]{3,2,1,0:T(8,128)(2,1)S(1)}, u32[]{:S(2)}, u32[]{:S(2)}) collective-permute-start(bf16[2,5,128,256]{3,2,1,0:T(8,128)(2,1)S(1)} %get-tuple-element.14.mine_ref), channel_id=1, source_target_pairs={{0,1},{1,0},{2,3},{3,2},{4,5},{5,4},{6,7},{7,6},{8,9},{9,8},{10,11... | collective-permute-start | bytes 1966088 | tf_op jit(solution)/shard_map/ppermute | solution.py:313
  6.6 6.7 %collective-permute-start.1 = (bf16[2,256,128]{2,1,0:T(8,128)(2,1)S(1)}, bf16[2,256,128]{2,1,0:T(8,128)(2,1)S(1)}, u32[]{:S(2)}, u32[]{:S(2)}) collective-permute-start(bf16[2,256,128]{2,1,0:T(8,128)(2,1)S(1)} %bitcast.1), channel_id=1, source_target_pairs={{0,2},{2,0},{1,3},{3,1},{4,6},{6,4},{5,7},{7,5},{8,10},{10,8},{9,1... | collective-permute-start | bytes 393224 | tf_op jit(solution)/shard_map/ppermute | solution.py:316
  13.3 5.1 %collective-permute-start.3 = (bf16[2,256,128]{2,1,0:T(8,128)(2,1)S(1)}, bf16[2,256,128]{2,1,0:T(8,128)(2,1)S(1)}, u32[]{:S(2)}, u32[]{:S(2)}) collective-permute-start(bf16[2,256,128]{2,1,0:T(8,128)(2,1)S(1)} %collective-permute-done.1.refs_0_), channel_id=1, source_target_pairs={{4,8},{8,4},{5,9},{9,5},{0,1},{1,0},{12,13},{13,12},{6,10},{10,6},... | collective-permute-start | bytes 393224 | tf_op jit(solution)/shard_map/ppermute | solution.py:310
  13.3 7.1 %collective-permute-start.2 = (bf16[2,256,128]{2,1,0:T(8,128)(2,1)S(1)}, bf16[2,256,128]{2,1,0:T(8,128)(2,1)S(1)}, u32[]{:S(2)}, u32[]{:S(2)}) collective-permute-start(bf16[2,256,128]{2,1,0:T(8,128)(2,1)S(1)} %collective-permute-done.1.refs_0_), channel_id=1, source_target_pairs={{0,4},{4,0},{8,12},{12,8},{1,5},{5,1},{9,13},{13,9},{2,6},{6,2},{1... | collective-permute-start | bytes 393224 | tf_op jit(solution)/shard_map/ppermute | solution.py:307
  17.1 0.7 %copy-start = (f32[2,128,256]{2,1,0:T(8,128)}, f32[2,128,256]{2,1,0:T(8,128)S(1)}, u32[]{:S(2)}) copy-start(f32[2,128,256]{2,1,0:T(8,128)S(1)} %get-tuple-element.15.own_ref) | copy-start | bytes 786436
  17.8 5.0 %collective-permute-start.9 = (bf16[2,128,256]{2,1,0:T(8,128)(2,1)S(1)}, bf16[2,128,256]{2,1,0:T(8,128)(2,1)S(1)}, u32[]{:S(2)}, u32[]{:S(2)}) collective-permute-start(bf16[2,128,256]{2,1,0:T(8,128)(2,1)S(1)} %get-tuple-element.16), channel_id=1, source_target_pairs={{0,4},{4,0},{8,12},{12,8},{1,5},{5,1},{9,13},{13,9},{2,6},{6,2},{1... | collective-permute-start | bytes 393224 | tf_op jit(solution)/shard_map/ppermute | solution.py:307
  17.8 5.0 %collective-permute-start.10 = (bf16[2,128,256]{2,1,0:T(8,128)(2,1)S(1)}, bf16[2,128,256]{2,1,0:T(8,128)(2,1)S(1)}, u32[]{:S(2)}, u32[]{:S(2)}) collective-permute-start(bf16[2,128,256]{2,1,0:T(8,128)(2,1)S(1)} %get-tuple-element.17), channel_id=1, source_target_pairs={{4,8},{8,4},{5,9},{9,5},{0,1},{1,0},{12,13},{13,12},{6,10},{10,6},... | collective-permute-start | bytes 393224 | tf_op jit(solution)/shard_map/ppermute | solution.py:310
  17.8 8.9 %collective-permute-start = (bf16[2,256,128]{2,1,0:T(8,128)(2,1)S(1)}, bf16[2,256,128]{2,1,0:T(8,128)(2,1)S(1)}, u32[]{:S(2)}, u32[]{:S(2)}) collective-permute-start(bf16[2,256,128]{2,1,0:T(8,128)(2,1)S(1)} %bitcast.3), channel_id=1, source_target_pairs={{0,1},{1,0},{2,3},{3,2},{4,5},{5,4},{6,7},{7,6},{8,9},{9,8},{10,11... | collective-permute-start | bytes 393224 | tf_op jit(solution)/shard_map/ppermute | solution.py:313
  18.4 8.4 %collective-permute-start.4 = (bf16[2,256,128]{2,1,0:T(8,128)(2,1)S(1)}, bf16[2,256,128]{2,1,0:T(8,128)(2,1)S(1)}, u32[]{:S(2)}, u32[]{:S(2)}) collective-permute-start(bf16[2,256,128]{2,1,0:T(8,128)(2,1)S(1)} %collective-permute-done.1.refs_0_), channel_id=1, source_target_pairs={{0,1},{1,0},{2,3},{3,2},{4,5},{5,4},{6,7},{7,6},{8,9},{9,8},{10,11... | collective-permute-start | bytes 393224 | tf_op jit(solution)/shard_map/ppermute | solution.py:313
  20.4 6.4 %collective-permute-start.6 = (bf16[2,256,128]{2,1,0:T(8,128)(2,1)S(1)}, bf16[2,256,128]{2,1,0:T(8,128)(2,1)S(1)}, u32[]{:S(2)}, u32[]{:S(2)}) collective-permute-start(bf16[2,256,128]{2,1,0:T(8,128)(2,1)S(1)} %collective-permute-done.3.refs_2_), channel_id=1, source_target_pairs={{0,1},{1,0},{2,3},{3,2},{4,5},{5,4},{6,7},{7,6},{8,9},{9,8},{10,11... | collective-permute-start | bytes 393224 | tf_op jit(solution)/shard_map/ppermute | solution.py:313
  22.8 0.7 %copy-start.9 = (bf16[2,128,256]{2,1,0:T(8,128)(2,1)}, bf16[2,128,256]{2,1,0:T(8,128)(2,1)S(1)}, u32[]{:S(2)}) copy-start(bf16[2,128,256]{2,1,0:T(8,128)(2,1)S(1)} %collective-permute-done.9.even_ref) | copy-start | bytes 393220
  22.8 4.0 %collective-permute-start.5 = (bf16[2,256,128]{2,1,0:T(8,128)(2,1)S(1)}, bf16[2,256,128]{2,1,0:T(8,128)(2,1)S(1)}, u32[]{:S(2)}, u32[]{:S(2)}) collective-permute-start(bf16[2,256,128]{2,1,0:T(8,128)(2,1)S(1)} %collective-permute-done.2.refs_1_), channel_id=1, source_target_pairs={{0,1},{1,0},{2,3},{3,2},{4,5},{5,4},{6,7},{7,6},{8,9},{9,8},{10,11... | collective-permute-start | bytes 393224 | tf_op jit(solution)/shard_map/ppermute | solution.py:313
  22.8 0.7 %copy-start.10 = (bf16[2,128,256]{2,1,0:T(8,128)(2,1)}, bf16[2,128,256]{2,1,0:T(8,128)(2,1)S(1)}, u32[]{:S(2)}) copy-start(bf16[2,128,256]{2,1,0:T(8,128)(2,1)S(1)} %collective-permute-done.10.odd_ref) | copy-start | bytes 393220
  25.3 9.8 %collective-permute-start.11 = (bf16[2,128,256]{2,1,0:T(8,128)(2,1)}, bf16[2,128,256]{2,1,0:T(8,128)(2,1)}, u32[]{:S(2)}, u32[]{:S(2)}) collective-permute-start(bf16[2,128,256]{2,1,0:T(8,128)(2,1)} %returns.1), channel_id=1, source_target_pairs={{0,2},{2,0},{1,3},{3,1},{4,6},{6,4},{5,7},{7,5},{8,10},{10,8},{9,1... | collective-permute-start | bytes 393224 | tf_op jit(solution)/shard_map/ppermute | solution.py:326
  26.8 0.7 %copy-start.7 = (bf16[2,256,128]{2,1,0:T(8,128)(2,1)}, bf16[2,256,128]{2,1,0:T(8,128)(2,1)S(1)}, u32[]{:S(2)}) copy-start(bf16[2,256,128]{2,1,0:T(8,128)(2,1)S(1)} %collective-permute-done.5.refs_4_) | copy-start | bytes 393220
  27.5 0.9 %copy-start.8 = (bf16[2,256,128]{2,1,0:T(8,128)(2,1)S(1)}, bf16[2,256,128]{2,1,0:T(8,128)(2,1)}, u32[]{:S(2)}) copy-start(bf16[2,256,128]{2,1,0:T(8,128)(2,1)} %copy-done.7) | copy-start | bytes 393220
  31.3 0.6 %copy-start.1 = (f32[2,128,128]{2,1,0:T(8,128)}, f32[2,128,128]{2,1,0:T(8,128)S(1)}, u32[]{:S(2)}) copy-start(f32[2,128,128]{2,1,0:T(8,128)S(1)} %get-tuple-element.12.mine_ref) | copy-start | bytes 393220
  32.0 3.1 %collective-permute-start.7 = (bf16[2,128,128]{2,1,0:T(8,128)(2,1)}, bf16[2,128,128]{2,1,0:T(8,128)(2,1)S(1)}, u32[]{:S(2)}, u32[]{:S(2)}) collective-permute-start(bf16[2,128,128]{2,1,0:T(8,128)(2,1)} %get-tuple-element.13), channel_id=1, source_target_pairs={{0,1},{1,0},{2,3},{3,2},{4,5},{5,4},{6,7},{7,6},{8,9},{9,8},{10,11... | collective-permute-start | bytes 196616 | tf_op jit(solution)/shard_map/ppermute | solution.py:313
  35.0 0.6 %copy-start.11 = (bf16[2,128,128]{2,1,0:T(8,128)(2,1)}, bf16[2,128,128]{2,1,0:T(8,128)(2,1)S(1)}, u32[]{:S(2)}) copy-start(bf16[2,128,128]{2,1,0:T(8,128)(2,1)S(1)} %collective-permute-done.7.other_ref) | copy-start | bytes 196612

commit v2 on v0

v2 whole, which is shorter than its diff:
```python
import functools

import jax
import jax.numpy as jnp
from jax import lax
from jax.experimental import pallas as pl
from jax.experimental.pallas import tpu as pltpu
from jax.sharding import PartitionSpec as P

CHANNELS = 256
SIDE = 16
PIXELS = 256
LEVELS = 340
NEIGHBOURS = 9
REACH = 2
SPAN = 2 * REACH + 1
COARSE = LEVELS - PIXELS
MARGIN = 16
PAD = 128
WIDE = PIXELS + PAD

VMEM = pl.BlockSpec(memory_space=pltpu.VMEM)
HBM = pl.BlockSpec(memory_space=pltpu.HBM)


def even_pairs(count):
    pairs = []
    for i in range(0, count - 1, 2):
        pairs += [(i, i + 1), (i + 1, i)]
    if count % 2:
        pairs.append((count - 1, count - 1))
    return pairs


def odd_pairs(count, cores):
    pairs, paired = [], set()
    for i in range(1, count - 1, 2):
        paired |= {i, i + 1}
        for c in range(cores):
            pairs += [(i * cores + c, (i + 1) * cores + c), ((i + 1) * cores + c, i * cores + c)]
    for i in range(count):
        if i not in paired:
            pairs += [(i * cores + c, i * cores + (c + 1) % cores) for c in range(cores)]
    return pairs


def frame_links(count):
    if count == 2:
        swap = [(0, 1), (1, 0)]
        return [(swap, swap)]
    onward = [(i, i + 1) for i in range(count - 1)]
    back = [(i + 1, i) for i in range(count - 1)]
    return [(onward, back), (back, onward)]


def coarse_weights(shape, pixel_axis):
    pixel = lax.broadcasted_iota(jnp.int32, shape, pixel_axis)
    cell = lax.broadcasted_iota(jnp.int32, shape, 1 - pixel_axis)
    row, column = lax.shift_right_logical(pixel, 4), jnp.bitwise_and(pixel, SIDE - 1)
    table = jnp.zeros(shape, jnp.float32)
    base = 0
    for level, across in ((1, 8), (2, 4), (3, 2)):
        target = base + lax.shift_right_logical(row, level) * across + lax.shift_right_logical(column, level)
        table = jnp.where(cell == target, 0.25**level, table)
        base += across * across
    return table.astype(jnp.bfloat16)


def column_of(row):
    n = row.shape[1]
    diagonal = lax.broadcasted_iota(jnp.int32, (n, n), 0) == lax.broadcasted_iota(jnp.int32, (n, n), 1)
    return jnp.sum(jnp.where(diagonal, row, 0.0), axis=1, keepdims=True)


def valid_row(valid_ref, a, core, half):
    row = valid_ref[a : a + 1, :].astype(jnp.float32)
    return jnp.where(core == 0, row[:, :half], row[:, half:])


def relative(neighbours_ref, a, k, first):
    return neighbours_ref[a, k] - (first + a) + REACH


def gate(pairing_ref, j, partners):
    if partners == 1:
        column = 1 - lax.axis_index("frame")
    else:
        column = j
    return pairing_ref[0, column].astype(jnp.float32) / 16.0


def entry_pairs(tiles):
    rows = LEVELS * tiles
    for k in range(0, NEIGHBOURS, 2):
        entries = range(k, min(k + 2, NEIGHBOURS))
        yield entries, k * rows, len(entries) * rows


def in_hbm(*arrays):
    return [pltpu.with_memory_space_constraint(z, pltpu.HBM) for z in arrays]


def copies(sources, targets, sems):
    started = [pltpu.make_async_copy(s, t, sems.at[i]) for i, (s, t) in enumerate(zip(sources, targets, strict=True))]
    for copy in started:
        copy.start()
    return started


def side_bases(tiles):
    parity = lax.rem(lax.axis_index("tile"), 2)
    return (1 - parity) * 2 * tiles, parity * 2 * tiles


def shape_of(shape, dtype=jnp.bfloat16):
    return jax.ShapeDtypeStruct(shape, dtype)


def call(kernel, name, outs, in_specs, out_specs, scratch, vmem_mib):
    return pl.pallas_call(
        kernel,
        out_shape=outs,
        in_specs=in_specs,
        out_specs=out_specs,
        scratch_shapes=scratch,
        compiler_params=pltpu.CompilerParams(vmem_limit_bytes=vmem_mib * 2**20),
        name=name,
    )


def fold_kernel(tiles, half, neighbours_hbm, valid_hbm, cot_hbm, features_hbm, down_ref, *refs):
    x_ref, neighbours_ref, valid_ref, cot_ref, stage, total, sems = refs
    core = lax.axis_index("chan")
    first = lax.axis_index("tile") * tiles
    parts = list(entry_pairs(tiles))
    views = [pl.ds(start, size) for _, start, size in parts]
    waits = copies(
        [neighbours_hbm, valid_hbm] + [cot_hbm.at[v] for v in views] + [features_hbm.at[0]],
        [neighbours_ref, valid_ref] + [cot_ref.at[v] for v in views] + [x_ref],
        sems,
    )
    pool = coarse_weights((PIXELS, PAD), 0)
    total[...] = jnp.zeros_like(total)
    waits[0].wait()
    waits[1].wait()
    for (entries, start, size), copy in zip(parts, waits[2 : 2 + len(parts)], strict=True):
        copy.wait()
        stage[:size] = cot_ref[start : start + size, :].astype(jnp.float32)
        for i, k in enumerate(entries):
            for a in range(tiles):
                w = relative(neighbours_ref, a, k, first)
                total[a, w, :LEVELS] += stage[pl.ds(i * LEVELS * tiles + a, LEVELS, stride=tiles), :]
    for a in range(tiles):
        keep = valid_row(valid_ref, a, core, half)
        for w in range(SPAN):
            coarse = total[a, w, PIXELS:].astype(jnp.bfloat16)
            spread = jnp.dot(pool, coarse, preferred_element_type=jnp.float32)
            down_ref[a, w] = ((total[a, w, :PIXELS] + spread) * keep).astype(jnp.bfloat16)
    waits[-1].wait()


def fold(neighbours, valid, cotangent, features):
    rows, half = cotangent.shape
    _, tiles, pixels, channels = features.shape
    return call(
        functools.partial(fold_kernel, tiles, half),
        "fold",
        (shape_of((tiles, SPAN, PIXELS, half)), shape_of((tiles, pixels, channels))),
        [HBM] * 4,
        (VMEM,) * 2,
        [
            pltpu.SMEM(neighbours.shape, jnp.int32),
            pltpu.VMEM(valid.shape, jnp.int32),
            pltpu.VMEM((rows, half), jnp.bfloat16),
            pltpu.VMEM((2 * LEVELS * tiles, half), jnp.float32),
            pltpu.VMEM((tiles, SPAN, WIDE, half), jnp.float32),
            pltpu.SemaphoreType.DMA((3 + (NEIGHBOURS + 1) // 2,)),
        ],
        8,
    )(*in_hbm(neighbours, valid, cotangent, features))


def halves(core, half):
    here = pl.ds(pl.multiple_of(core * half, half), half)
    there = pl.ds(pl.multiple_of((1 - core) * half, half), half)
    return here, there


def keys_kernel(tiles, half, x_ref, mine_ref, other_ref, own_ref, even_ref, odd_ref, window):
    here, there = halves(lax.axis_index("chan"), half)
    for a in range(tiles):
        queries = jnp.concatenate([x_ref[a, here, :], x_ref[a, there, :]], axis=0)
        for w in range(SPAN):
            grads = jnp.concatenate([mine_ref[a, w], other_ref[a, w]], axis=1)
            term = jnp.dot(grads, queries, preferred_element_type=jnp.float32)
            slot = a + w
            if a == 0 or w == SPAN - 1:
                window[slot] = term
            else:
                window[slot] += term
    own_ref[...] = window[tiles : 2 * tiles]
    even, odd = side_bases(tiles)
    for a in range(tiles):
        even_ref[a] = window[even + a].astype(jnp.bfloat16)
        odd_ref[a] = window[odd + a].astype(jnp.bfloat16)


def keys(x, mine, other):
    tiles, half = x.shape[0], mine.shape[3]
    return call(
        functools.partial(keys_kernel, tiles, half),
        "keys",
        (shape_of(x.shape, jnp.float32), shape_of(x.shape), shape_of(x.shape)),
        [VMEM] * 3,
        (VMEM,) * 3,
        [pltpu.VMEM((3 * tiles,) + x.shape[1:], jnp.float32)],
        6,
    )(x, mine, other)


def returns_kernel(partners, pairing_hbm, own_ref, even_ref, odd_ref, *refs):
    out_refs, (pairing_ref, sems) = refs[:partners], refs[partners:]
    (copy,) = copies([pairing_hbm], [pairing_ref], sems)
    tile, count = lax.axis_index("tile"), lax.axis_size("tile")
    parity = lax.rem(tile, 2)
    has_even = jnp.logical_or(parity == 1, tile + 1 < count)
    has_odd = jnp.logical_or(jnp.logical_and(parity == 0, tile > 0), jnp.logical_and(parity == 1, tile + 1 < count))
    total = own_ref[...]
    rows = own_ref.shape[0] * own_ref.shape[1]
    total = total + jnp.where(has_even, even_ref[...].astype(jnp.float32), 0.0)
    total = total + jnp.where(has_odd, odd_ref[...].astype(jnp.float32), 0.0)
    copy.wait()
    for j in range(partners):
        out_refs[j][:rows] = (total * gate(pairing_ref, j, partners)).astype(jnp.bfloat16).reshape(rows, -1)
        out_refs[j][rows:] = jnp.zeros_like(out_refs[j][rows:])


def returns(partners, pairing, own, even, odd):
    return call(
        functools.partial(returns_kernel, partners),
        "returns",
        (shape_of((own.shape[0] * own.shape[1] + MARGIN, own.shape[2])),) * partners,
        [HBM] + [VMEM] * 3,
        (VMEM,) * partners,
        [pltpu.SMEM(pairing.shape, jnp.int32), pltpu.SemaphoreType.DMA((1,))],
        3,
    )(*in_hbm(pairing), own, even, odd)


def join(mine, other):
    core = lax.axis_index("chan")
    return jnp.concatenate([jnp.where(core == 0, mine, other), jnp.where(core == 0, other, mine)], axis=-1)


def multiply(left, right, contract):
    return lax.dot_general(left, right, ((contract[:1], contract[1:]), ((), ())), preferred_element_type=jnp.float32)


def query_grads(mine_ref, other_ref, a, w, level):
    return multiply(jnp.concatenate([mine_ref[a, w], other_ref[a, w]], axis=1), level, (0, 0))


def near_kernel(tiles, half, partners, pairing_hbm, valid_hbm, down_ref, down_other_ref, *refs):
    (x_ref, xo_ref), same, rest = refs[:2], refs[2 : 2 + 2 * partners], refs[2 + 2 * partners :]
    queries_ref, fine_ref, coarse_ref, grad_ref, pairing_ref, valid_ref, sems = rest
    waits = copies([pairing_hbm, valid_hbm], [pairing_ref, valid_ref], sems)
    core = lax.axis_index("chan")
    pool = coarse_weights((PAD, PIXELS), 1)
    here, _ = halves(core, half)
    for copy in waits:
        copy.wait()
    for a in range(tiles):
        keep = column_of(valid_row(valid_ref, a, core, half))
        row = join(x_ref[a, here, :], xo_ref[a, here, :]).astype(jnp.float32) * keep
        for j in range(partners):
            queries_ref[j, a * half : (a + 1) * half] = (row * gate(pairing_ref, j, partners)).astype(jnp.bfloat16)
    grad = [None] * tiles
    for s in range(tiles):
        for j in range(partners):
            level_mine, level_other = same[2 * j][s], same[2 * j + 1][s]
            level = join(level_mine, level_other)
            coarse = jnp.dot(pool, level, preferred_element_type=jnp.float32).astype(jnp.bfloat16)
            fine_term = multiply(level, queries_ref[j], (1, 1))
            coarse_term = multiply(coarse, queries_ref[j], (1, 1))
            fine_ref[s] = fine_term if j == 0 else fine_ref[s] + fine_term
            coarse_ref[s] = coarse_term if j == 0 else coarse_ref[s] + coarse_term
            for a in range(tiles):
                term = query_grads(down_ref, down_other_ref, a, tiles + s - a, level_mine)
                term = term * gate(pairing_ref, j, partners)
                grad[a] = term if grad[a] is None else grad[a] + term
    for a in range(tiles):
        grad_ref[a] = grad[a]


def near(partners, pairing, valid, down, down_other, x, xo, same):
    tiles, half, channels = x.shape[0], down.shape[3], x.shape[2]
    both = 2 * channels
    return call(
        functools.partial(near_kernel, tiles, half, partners),
        "near",
        (
            shape_of((partners, tiles * half, both)),
            shape_of((tiles, PIXELS, tiles * half), jnp.float32),
            shape_of((tiles, PAD, tiles * half), jnp.float32),
            shape_of((tiles, 2 * half, channels), jnp.float32),
        ),
        [HBM, HBM] + [VMEM] * (4 + len(same)),
        (VMEM,) * 4,
        [
            pltpu.SMEM(pairing.shape, jnp.int32),
            pltpu.VMEM(valid.shape, jnp.int32),
            pltpu.SemaphoreType.DMA((2,)),
        ],
        8,
    )(*in_hbm(pairing, valid), down, down_other, x, xo, *same)


def side_order(tiles):
    parity = lax.rem(lax.axis_index("tile"), 2)
    return (1 - parity) * tiles, parity * tiles


def sides_kernel(tiles, half, partners, pairing_hbm, down_ref, down_other_ref, near_ref, *refs):
    inputs, (grad_ref, levels, pairing_ref, sems) = refs[: 2 * partners], refs[2 * partners :]
    (copy,) = copies([pairing_hbm], [pairing_ref], sems)
    here, there = halves(lax.axis_index("chan"), half)
    even, odd = side_order(tiles)
    for j in range(partners):
        levels[j, pl.ds(even, tiles)] = inputs[2 * j][...]
        levels[j, pl.ds(odd, tiles)] = inputs[2 * j + 1][...]
    copy.wait()
    for a in range(tiles):
        grad = near_ref[a]
        for j in range(partners):
            term = None
            for w in range(SPAN):
                slot = a + w
                if tiles <= slot < 2 * tiles:
                    continue
                part = query_grads(down_ref, down_other_ref, a, w, levels[j, slot if slot < tiles else slot - tiles])
                term = part if term is None else term + part
            grad = grad + term * gate(pairing_ref, j, partners)
        grad_ref[a, here, :] = grad[:half]
        grad_ref[a, there, :] = grad[half:]


def sides(partners, pairing, down, down_other, near_grad, beside):
    tiles, rows, channels = near_grad.shape
    return call(
        functools.partial(sides_kernel, tiles, rows // 2, partners),
        "sides",
        shape_of(near_grad.shape, jnp.float32),
        [HBM] + [VMEM] * (3 + len(beside)),
        VMEM,
        [
            pltpu.VMEM((partners, 2 * tiles, PIXELS, channels), jnp.bfloat16),
            pltpu.SMEM(pairing.shape, jnp.int32),
            pltpu.SemaphoreType.DMA((1,)),
        ],
        6,
    )(*in_hbm(pairing), down, down_other, near_grad, *beside)


def volume_kernel(tiles, half, partners, neighbours_hbm, queries_ref, near_fine, near_coarse, *refs):
    inputs, rest = refs[: 4 * partners], refs[4 * partners :]
    volume_hbm, neighbours_ref, fine_table, coarse_table, stage, volume_ref, sems = rest
    (neighbours_copy,) = copies([neighbours_hbm], [neighbours_ref], sems)
    first = lax.axis_index("tile") * tiles
    pool = coarse_weights((PAD, PIXELS), 1)
    fine_table[tiles : 2 * tiles] = near_fine[...]
    coarse_table[tiles : 2 * tiles] = near_coarse[...]
    for part, base in enumerate(side_bases(tiles)):
        for a in range(tiles):
            fine, coarse = None, None
            for j in range(partners):
                level = join(inputs[4 * j + part][a], inputs[4 * j + 2 + part][a])
                cells = jnp.dot(pool, level, preferred_element_type=jnp.float32).astype(jnp.bfloat16)
                fine_term = multiply(level, queries_ref[j], (1, 1))
                coarse_term = multiply(cells, queries_ref[j], (1, 1))
                fine = fine_term if fine is None else fine + fine_term
                coarse = coarse_term if coarse is None else coarse + coarse_term
            fine_table[base + a] = fine
            coarse_table[base + a] = coarse
    neighbours_copy.wait()
    waits = []
    for i_part, (entries, start, size) in enumerate(entry_pairs(tiles)):
        for i, k in enumerate(entries):
            for a in range(tiles):
                slot = relative(neighbours_ref, a, k, first) + a
                lanes = slice(a * half, (a + 1) * half)
                base = i * LEVELS * tiles + a
                stage[pl.ds(base, PIXELS, stride=tiles), :] = fine_table[slot, :, lanes]
                stage[pl.ds(base + PIXELS * tiles, COARSE, stride=tiles), :] = coarse_table[slot, :COARSE, lanes]
        rows = pl.ds(start, size)
        volume_ref[rows, :] = stage[:size].astype(jnp.bfloat16)
        copy = pltpu.make_async_copy(volume_ref.at[rows], volume_hbm.at[rows], sems.at[1 + i_part])
        copy.start()
        waits.append(copy)
    for copy in waits:
        copy.wait()


def volumes(partners, neighbours, queries, near_fine, near_coarse, beside):
    tiles, half = near_fine.shape[0], near_fine.shape[2] // near_fine.shape[0]
    rows = NEIGHBOURS * LEVELS * tiles
    return call(
        functools.partial(volume_kernel, tiles, half, partners),
        "volume",
        shape_of((rows, half)),
        [HBM] + [VMEM] * (3 + len(beside)),
        HBM,
        [
            pltpu.SMEM(neighbours.shape, jnp.int32),
            pltpu.VMEM((3 * tiles, PIXELS, tiles * half), jnp.float32),
            pltpu.VMEM((3 * tiles, PAD, tiles * half), jnp.float32),
            pltpu.VMEM((2 * LEVELS * tiles, half), jnp.float32),
            pltpu.VMEM((rows, half), jnp.bfloat16),
            pltpu.SemaphoreType.DMA((1 + (NEIGHBOURS + 1) // 2,)),
        ],
        12,
    )(*in_hbm(neighbours), queries, near_fine, near_coarse, *beside)


def merge_kernel(partners, grad_ref, *refs):
    total = grad_ref[...]
    for j in range(partners):
        total = total + refs[j][: total.shape[0] * total.shape[1]].astype(jnp.float32).reshape(total.shape)
    refs[partners][0] = total


def merge(grad, returned):
    return call(
        functools.partial(merge_kernel, len(returned)),
        "merge",
        shape_of((1,) + grad.shape, jnp.float32),
        [VMEM] * (1 + len(returned)),
        VMEM,
        [],
        2,
    )(grad, *returned)


def after(value, earlier):
    return lax.optimization_barrier((value, earlier))[0]


def local(features, neighbours, pairing, valid_tiles, cotangent):
    count = lax.axis_size("tile")
    cores = lax.axis_size("chan")
    links = frame_links(lax.axis_size("frame"))
    partners = len(links)
    tiles, half = cotangent.shape[1:3]
    swap = [(c, (c + 1) % cores) for c in range(cores)]
    evens, odds = even_pairs(count), odd_pairs(count, cores)

    def over_even(z):
        return lax.ppermute(z, "tile", evens)

    def over_odd(z):
        return lax.ppermute(z, ("tile", "chan"), odds)

    def over_cores(z):
        return lax.ppermute(z, "chan", swap)

    upstream = jnp.transpose(cotangent[0], (2, 0, 1)).reshape(NEIGHBOURS * LEVELS * tiles, half)
    down, x = fold(neighbours, valid_tiles, upstream, features)
    down_other = over_cores(down)
    arrived = [lax.ppermute(x, "frame", ahead) for ahead, _ in links]
    xo = over_cores(x)
    own, to_even, to_odd = keys(x, down, down_other)
    arrived = [after(y, own) for y in arrived]
    beside = [(over_even(y), over_odd(y)) for y in arrived]
    sent = returns(partners, pairing, own, over_even(to_even), over_odd(to_odd))
    returned = [lax.ppermute(z, "frame", back) for z, (_, back) in zip(sent, links, strict=True)]
    same = []
    for y in arrived:
        same += [after(y, sent[0]), after(over_cores(y), sent[0])]
    queries, near_fine, near_coarse, near_grad = near(partners, pairing, valid_tiles, down, down_other, x, xo, same)
    mine, exchanged = [], []
    for even, odd in beside:
        even = after(even, near_grad)
        odd = after(odd, even)
        mine += [even, odd]
        exchanged += [even, odd, over_cores(even), over_cores(odd)]
    grad = sides(partners, pairing, down, down_other, near_grad, mine)
    exchanged = [after(z, grad) for z in exchanged]
    volume = volumes(partners, neighbours, queries, near_fine, near_coarse, exchanged)
    feature_grad = merge(grad, returned)
    volume = jnp.transpose(volume.reshape(NEIGHBOURS * LEVELS, tiles, half), (1, 2, 0))
    return volume[None], feature_grad


def solution(mesh):
    return jax.shard_map(
        local,
        mesh=mesh,
        in_specs=(
            P(("clip", "frame"), "tile", None, "chan"),
            P(("clip", "tile"), None),
            P(("clip", "frame"), None),
            P(("clip", "tile"), None),
            P(("clip", "frame"), "tile", "chan", None),
        ),
        out_specs=(
            P(("clip", "frame"), "tile", "chan", None),
            P(("clip", "frame"), "tile", None, "chan"),
        ),
        check_vma=False,
    )
```

time: 116 us -> 21.5 us (0.19)
  the two profiles are of different devices: /device:TPU:0 before, /device:TPU:13 now
where the time goes in v2:
time: 21.5 us; the launch traced here: 21.2 us
  starting transfers between devices  10.1 us (47%)
  Pallas kernels  8.63 us (40%)
  waiting for transfers between devices  1.76 us (8%)
  between operations  0.72 us (3%)
    ppermute x2, starting transfers between devices, over_odd(): return lax.ppermute(z, ('tile', 'chan'), odds)  3.92 us
    ppermute x5, starting transfers between devices, over_cores(): return lax.ppermute(z, 'chan', swap)  3.32 us
    pallas_call x1, Pallas kernels, volumes(): call(functools.partial(volume_kernel, tiles, half, partners), 'volume', s...  2.31 us
    pallas_call x1, Pallas kernels, fold(): call(functools.partial(fold_kernel, tiles, half), 'fold', (shape_of((tile...  1.97 us
    pallas_call x1, Pallas kernels, near(): call(functools.partial(near_kernel, tiles, half, partners), 'near', (shap...  1.3 us
    ppermute x1, starting transfers between devices, local(): lax.ppermute(z, 'frame', back)  1.28 us
    ppermute x1, starting transfers between devices, local(): arrived = [lax.ppermute(x, 'frame', ahead) for ahead, _ in links]  1.23 us
    pallas_call x1, Pallas kernels, sides(): call(functools.partial(sides_kernel, tiles, rows // 2, partners), 'sides'...  1.08 us
  transfers between devices with their start and end apart: 11, of which 4 were waited for; matrix products, arithmetic and copies ran while one was open for 0% of the time, Pallas kernels for 28%

profile of v2, /device:TPU:13, one launch (start us, length us, event | category | flops | bytes accessed | tf_op | source)
XLA Modules:
  0.0 21.2 jit_solution(5231922474463782414)
XLA Ops:
  0.6 2.0 %fold.1 = (bf16[2,5,256,128]{3,2,1,0:T(8,128)(2,1)S(1)}, bf16[2,256,128]{2,1,0:T(8,128)(2,1)S(1)}) custom-call(s32[2,9]{1,0:T(2,128)} %neighbours_hbm.3, s32[2,256]{1,0:T(2,128)} %valid_hbm.3, bf16[6120,128]{1,0:T(8,128)(2,1)} %bitcast.10, bf16[1,2,256,128]{3,2,1,0:T(8,128)(2,1)} %features_hbm.1), custom_call_target="tpu_custom_call" | custom-call | tf_op jit(solution)/shard_map/fold/pallas_call | solution.py:165
  2.6 0.7 %collective-permute-start = (bf16[2,5,256,128]{3,2,1,0:T(8,128)(2,1)S(1)}, bf16[2,5,256,128]{3,2,1,0:T(8,128)(2,1)S(1)}, u32[]{:S(2)}, u32[]{:S(2)}) collective-permute-start(bf16[2,5,256,128]{3,2,1,0:T(8,128)(2,1)S(1)} %get-tuple-element.20.mine_ref.down_ref), channel_id=1, source_target_pairs={{0,1},{1,0},{2,3},{3,2},{4,5},{5,4},{6,7},{7,6},{8,9},{9,8},{10,11... | collective-permute-start | bytes 1966088 | tf_op jit(solution)/shard_map/ppermute | solution.py:463
  3.3 1.2 %collective-permute-start.2 = (bf16[2,256,128]{2,1,0:T(8,128)(2,1)S(1)}, bf16[2,256,128]{2,1,0:T(8,128)(2,1)S(1)}, u32[]{:S(2)}, u32[]{:S(2)}) collective-permute-start(bf16[2,256,128]{2,1,0:T(8,128)(2,1)S(1)} %get-tuple-element.21.x_ref.refs_0_), channel_id=1, source_target_pairs={{0,2},{2,0},{1,3},{3,1},{4,6},{6,4},{5,7},{7,5},{8,10},{10,8},{9,1... | collective-permute-start | bytes 393224 | tf_op jit(solution)/shard_map/ppermute | solution.py:468
  4.6 0.5 %collective-permute-done.other_ref.down_other_ref = bf16[2,5,256,128]{3,2,1,0:T(8,128)(2,1)S(1)} collective-permute-done((bf16[2,5,256,128]{3,2,1,0:T(8,128)(2,1)S(1)}, bf16[2,5,256,128]{3,2,1,0:T(8,128)(2,1)S(1)}, u32[]{:S(2)}, u32[]{:S(2)}) %collective-permute-start) | collective-permute-done | bytes 655392 | tf_op jit(solution)/shard_map/ppermute | solution.py:463
  5.1 0.5 %keys.1 = (f32[2,256,128]{2,1,0:T(8,128)S(1)}, bf16[2,256,128]{2,1,0:T(8,128)(2,1)S(1)}, bf16[2,256,128]{2,1,0:T(8,128)(2,1)S(1)}) custom-call(bf16[2,256,128]{2,1,0:T(8,128)(2,1)S(1)} %get-tuple-element.21.x_ref.refs_0_, bf16[2,5,256,128]{3,2,1,0:T(8,128)(2,1)S(1)} %get-tuple-element.20.mine_ref.down_ref, ...), custom_call_target="tpu_custom_call" | custom-call | tf_op jit(solution)/shard_map/keys/pallas_call | solution.py:210
  5.6 0.2 %collective-permute-start.3 = (bf16[2,256,128]{2,1,0:T(8,128)(2,1)S(1)}, bf16[2,256,128]{2,1,0:T(8,128)(2,1)S(1)}, u32[]{:S(2)}, u32[]{:S(2)}) collective-permute-start(bf16[2,256,128]{2,1,0:T(8,128)(2,1)S(1)} %get-tuple-element.24), channel_id=1, source_target_pairs={{0,4},{4,0},{8,12},{12,8},{1,5},{5,1},{9,13},{13,9},{2,6},{6,2},{1... | collective-permute-start | bytes 393224 | tf_op jit(solution)/shard_map/ppermute | solution.py:457
  5.9 2.4 %collective-permute-start.4 = (bf16[2,256,128]{2,1,0:T(8,128)(2,1)S(1)}, bf16[2,256,128]{2,1,0:T(8,128)(2,1)S(1)}, u32[]{:S(2)}, u32[]{:S(2)}) collective-permute-start(bf16[2,256,128]{2,1,0:T(8,128)(2,1)S(1)} %get-tuple-element.25), channel_id=1, source_target_pairs={{4,8},{8,4},{5,9},{9,5},{0,1},{1,0},{12,13},{13,12},{6,10},{10,6},... | collective-permute-start | bytes 393224 | tf_op jit(solution)/shard_map/ppermute | solution.py:460
  8.3 0.1 collective-permute-done.2.refs_2_
  8.4 0.8 %collective-permute-start.5 = (bf16[2,256,128]{2,1,0:T(8,128)(2,1)S(1)}, bf16[2,256,128]{2,1,0:T(8,128)(2,1)S(1)}, u32[]{:S(2)}, u32[]{:S(2)}) collective-permute-start(bf16[2,256,128]{2,1,0:T(8,128)(2,1)S(1)} %collective-permute-done.2.refs_2_), channel_id=1, source_target_pairs={{0,1},{1,0},{2,3},{3,2},{4,5},{5,4},{6,7},{7,6},{8,9},{9,8},{10,11... | collective-permute-start | bytes 393224 | tf_op jit(solution)/shard_map/ppermute | solution.py:463
  9.3 0.0 collective-permute-start.1
  9.3 0.2 collective-permute-start.6
  9.4 0.9 %collective-permute-done.3.even_ref = bf16[2,256,128]{2,1,0:T(8,128)(2,1)S(1)} collective-permute-done((bf16[2,256,128]{2,1,0:T(8,128)(2,1)S(1)}, bf16[2,256,128]{2,1,0:T(8,128)(2,1)S(1)}, u32[]{:S(2)}, u32[]{:S(2)}) %collective-permute-start.3) | collective-permute-done | bytes 131104 | tf_op jit(solution)/shard_map/ppermute | solution.py:457
  10.4 1.5 %collective-permute-start.7 = (bf16[2,256,128]{2,1,0:T(8,128)(2,1)S(1)}, bf16[2,256,128]{2,1,0:T(8,128)(2,1)S(1)}, u32[]{:S(2)}, u32[]{:S(2)}) collective-permute-start(bf16[2,256,128]{2,1,0:T(8,128)(2,1)S(1)} %collective-permute-done.2.refs_2_), channel_id=1, source_target_pairs={{4,8},{8,4},{5,9},{9,5},{0,1},{1,0},{12,13},{13,12},{6,10},{10,6},... | collective-permute-start | bytes 393224 | tf_op jit(solution)/shard_map/ppermute | solution.py:460
  11.9 0.0 collective-permute-done.4.odd_ref
  11.9 0.7 %returns.1 = bf16[528,128]{1,0:T(8,128)(2,1)S(1)} custom-call(s32[1,2]{1,0:T(1,128)} %pairing_hbm.5, f32[2,256,128]{2,1,0:T(8,128)S(1)} %get-tuple-element.22.own_ref, bf16[2,256,128]{2,1,0:T(8,128)(2,1)S(1)} %collective-permute-done.3.even_ref, bf16[2,256,128]{2,1,0:T(8,128)(2,1)S(1)} %collective-permute-done.4.odd_ref), custom_call_target="tpu_custom_call" | custom-call | tf_op jit(solution)/shard_map/returns/pallas_call | solution.py:239
  12.6 1.3 %collective-permute-start.10 = (bf16[528,128]{1,0:T(8,128)(2,1)S(1)}, bf16[528,128]{1,0:T(8,128)(2,1)S(1)}, u32[]{:S(2)}, u32[]{:S(2)}) collective-permute-start(bf16[528,128]{1,0:T(8,128)(2,1)S(1)} %returns.1), channel_id=1, source_target_pairs={{0,2},{2,0},{1,3},{3,1},{4,6},{6,4},{5,7},{7,5},{8,10},{10,8},{9,1... | collective-permute-start | bytes 405512 | tf_op jit(solution)/shard_map/ppermute | solution.py:474
  13.9 0.0 collective-permute-done.5.refs_3_
  13.9 0.0 collective-permute-done.1.refs_1_
  13.9 1.3 %near.1 = (bf16[1,256,256]{2,1,0:T(8,128)(2,1)S(1)}, f32[2,256,256]{2,1,0:T(8,128)S(1)}, f32[2,128,256]{2,1,0:T(8,128)S(1)}, f32[2,256,128]{2,1,0:T(8,128)S(1)}) custom-call(s32[1,2]{1,0:T(1,128)} %pairing_hbm.5, s32[2,256]{1,0:T(2,128)} %valid_hbm.3, bf16[2,5,256,128]{3,2,1,0:T(8,128)(2,1)S(1)} %get-tuple-element.20.mine_ref.down_ref, ...), custom_call_target="tpu_custom_call" | custom-call | tf_op jit(solution)/shard_map/near/pallas_call | solution.py:298
  15.2 0.0 collective-permute-done.6.refs_0_
  15.2 0.0 collective-permute-done.7.refs_1_
  15.2 1.6 %collective-permute-start.9 = (bf16[2,256,128]{2,1,0:T(8,128)(2,1)S(1)}, bf16[2,256,128]{2,1,0:T(8,128)(2,1)S(1)}, u32[]{:S(2)}, u32[]{:S(2)}) collective-permute-start(bf16[2,256,128]{2,1,0:T(8,128)(2,1)S(1)} %collective-permute-done.7.refs_1_), channel_id=1, source_target_pairs={{0,1},{1,0},{2,3},{3,2},{4,5},{5,4},{6,7},{7,6},{8,9},{9,8},{10,11... | collective-permute-start | bytes 393224 | tf_op jit(solution)/shard_map/ppermute | solution.py:463
  16.8 0.1 collective-permute-start.8
  16.9 1.1 %sides.1.grad_ref = f32[2,256,128]{2,1,0:T(8,128)S(1)} custom-call(s32[1,2]{1,0:T(1,128)} %pairing_hbm.5, bf16[2,5,256,128]{3,2,1,0:T(8,128)(2,1)S(1)} %get-tuple-element.20.mine_ref.down_ref, bf16[2,5,256,128]{3,2,1,0:T(8,128)(2,1)S(1)} %collective-permute-done.other_ref.down_other_ref, f32[2,256,128]{2,1,0:T(8,128)S(1)} %get-tuple-element.31.near_ref, ...), custom_call_target="tpu_custom_call" | custom-call | tf_op jit(solution)/shard_map/sides/pallas_call | solution.py:349
  18.0 0.0 collective-permute-done.9.refs_3_
  18.0 0.2 collective-permute-done.8.refs_2_
  18.2 2.3 %volume.1 = bf16[6120,128]{1,0:T(8,128)(2,1)} custom-call(s32[2,9]{1,0:T(2,128)} %neighbours_hbm.3, bf16[1,256,256]{2,1,0:T(8,128)(2,1)S(1)} %get-tuple-element.28.queries_ref, f32[2,256,256]{2,1,0:T(8,128)S(1)} %get-tuple-element.29.near_fine, f32[2,128,256]{2,1,0:T(8,128)S(1)} %get-tuple-element.30.near_coarse, ...), custom_call_target="tpu_custom_call" | custom-call | tf_op jit(solution)/shard_map/volume/pallas_call | solution.py:406
  20.5 0.0 collective-permute-done.10.refs_0_
  20.5 0.7 %merge.1 = f32[1,2,256,128]{3,2,1,0:T(8,128)} custom-call(f32[2,256,128]{2,1,0:T(8,128)S(1)} %sides.1.grad_ref, bf16[528,128]{1,0:T(8,128)(2,1)S(1)} %collective-permute-done.10.refs_0_), custom_call_target="tpu_custom_call" | custom-call | tf_op jit(solution)/shard_map/merge/pallas_call | solution.py:432
Async XLA Ops:
  2.6 2.5 %collective-permute-start = (bf16[2,5,256,128]{3,2,1,0:T(8,128)(2,1)S(1)}, bf16[2,5,256,128]{3,2,1,0:T(8,128)(2,1)S(1)}, u32[]{:S(2)}, u32[]{:S(2)}) collective-permute-start(bf16[2,5,256,128]{3,2,1,0:T(8,128)(2,1)S(1)} %get-tuple-element.20.mine_ref.down_ref), channel_id=1, source_target_pairs={{0,1},{1,0},{2,3},{3,2},{4,5},{5,4},{6,7},{7,6},{8,9},{9,8},{10,11... | collective-permute-start | bytes 1966088 | tf_op jit(solution)/shard_map/ppermute | solution.py:463
  3.3 5.1 %collective-permute-start.2 = (bf16[2,256,128]{2,1,0:T(8,128)(2,1)S(1)}, bf16[2,256,128]{2,1,0:T(8,128)(2,1)S(1)}, u32[]{:S(2)}, u32[]{:S(2)}) collective-permute-start(bf16[2,256,128]{2,1,0:T(8,128)(2,1)S(1)} %get-tuple-element.21.x_ref.refs_0_), channel_id=1, source_target_pairs={{0,2},{2,0},{1,3},{3,1},{4,6},{6,4},{5,7},{7,5},{8,10},{10,8},{9,1... | collective-permute-start | bytes 393224 | tf_op jit(solution)/shard_map/ppermute | solution.py:468
  5.6 4.8 %collective-permute-start.3 = (bf16[2,256,128]{2,1,0:T(8,128)(2,1)S(1)}, bf16[2,256,128]{2,1,0:T(8,128)(2,1)S(1)}, u32[]{:S(2)}, u32[]{:S(2)}) collective-permute-start(bf16[2,256,128]{2,1,0:T(8,128)(2,1)S(1)} %get-tuple-element.24), channel_id=1, source_target_pairs={{0,4},{4,0},{8,12},{12,8},{1,5},{5,1},{9,13},{13,9},{2,6},{6,2},{1... | collective-permute-start | bytes 393224 | tf_op jit(solution)/shard_map/ppermute | solution.py:457
  5.9 6.0 %collective-permute-start.4 = (bf16[2,256,128]{2,1,0:T(8,128)(2,1)S(1)}, bf16[2,256,128]{2,1,0:T(8,128)(2,1)S(1)}, u32[]{:S(2)}, u32[]{:S(2)}) collective-permute-start(bf16[2,256,128]{2,1,0:T(8,128)(2,1)S(1)} %get-tuple-element.25), channel_id=1, source_target_pairs={{4,8},{8,4},{5,9},{9,5},{0,1},{1,0},{12,13},{13,12},{6,10},{10,6},... | collective-permute-start | bytes 393224 | tf_op jit(solution)/shard_map/ppermute | solution.py:460
  8.4 5.4 %collective-permute-start.5 = (bf16[2,256,128]{2,1,0:T(8,128)(2,1)S(1)}, bf16[2,256,128]{2,1,0:T(8,128)(2,1)S(1)}, u32[]{:S(2)}, u32[]{:S(2)}) collective-permute-start(bf16[2,256,128]{2,1,0:T(8,128)(2,1)S(1)} %collective-permute-done.2.refs_2_), channel_id=1, source_target_pairs={{0,1},{1,0},{2,3},{3,2},{4,5},{5,4},{6,7},{7,6},{8,9},{9,8},{10,11... | collective-permute-start | bytes 393224 | tf_op jit(solution)/shard_map/ppermute | solution.py:463
  9.3 4.6 %collective-permute-start.1 = (bf16[2,256,128]{2,1,0:T(8,128)(2,1)S(1)}, bf16[2,256,128]{2,1,0:T(8,128)(2,1)S(1)}, u32[]{:S(2)}, u32[]{:S(2)}) collective-permute-start(bf16[2,256,128]{2,1,0:T(8,128)(2,1)S(1)} %get-tuple-element.21.x_ref.refs_0_), channel_id=1, source_target_pairs={{0,1},{1,0},{2,3},{3,2},{4,5},{5,4},{6,7},{7,6},{8,9},{9,8},{10,11... | collective-permute-start | bytes 393224 | tf_op jit(solution)/shard_map/ppermute | solution.py:463
  9.3 5.9 %collective-permute-start.6 = (bf16[2,256,128]{2,1,0:T(8,128)(2,1)S(1)}, bf16[2,256,128]{2,1,0:T(8,128)(2,1)S(1)}, u32[]{:S(2)}, u32[]{:S(2)}) collective-permute-start(bf16[2,256,128]{2,1,0:T(8,128)(2,1)S(1)} %collective-permute-done.2.refs_2_), channel_id=1, source_target_pairs={{0,4},{4,0},{8,12},{12,8},{1,5},{5,1},{9,13},{13,9},{2,6},{6,2},{1... | collective-permute-start | bytes 393224 | tf_op jit(solution)/shard_map/ppermute | solution.py:457
  10.4 4.8 %collective-permute-start.7 = (bf16[2,256,128]{2,1,0:T(8,128)(2,1)S(1)}, bf16[2,256,128]{2,1,0:T(8,128)(2,1)S(1)}, u32[]{:S(2)}, u32[]{:S(2)}) collective-permute-start(bf16[2,256,128]{2,1,0:T(8,128)(2,1)S(1)} %collective-permute-done.2.refs_2_), channel_id=1, source_target_pairs={{4,8},{8,4},{5,9},{9,5},{0,1},{1,0},{12,13},{13,12},{6,10},{10,6},... | collective-permute-start | bytes 393224 | tf_op jit(solution)/shard_map/ppermute | solution.py:460
  12.6 7.9 %collective-permute-start.10 = (bf16[528,128]{1,0:T(8,128)(2,1)S(1)}, bf16[528,128]{1,0:T(8,128)(2,1)S(1)}, u32[]{:S(2)}, u32[]{:S(2)}) collective-permute-start(bf16[528,128]{1,0:T(8,128)(2,1)S(1)} %returns.1), channel_id=1, source_target_pairs={{0,2},{2,0},{1,3},{3,1},{4,6},{6,4},{5,7},{7,5},{8,10},{10,8},{9,1... | collective-permute-start | bytes 405512 | tf_op jit(solution)/shard_map/ppermute | solution.py:474
  15.2 2.8 %collective-permute-start.9 = (bf16[2,256,128]{2,1,0:T(8,128)(2,1)S(1)}, bf16[2,256,128]{2,1,0:T(8,128)(2,1)S(1)}, u32[]{:S(2)}, u32[]{:S(2)}) collective-permute-start(bf16[2,256,128]{2,1,0:T(8,128)(2,1)S(1)} %collective-permute-done.7.refs_1_), channel_id=1, source_target_pairs={{0,1},{1,0},{2,3},{3,2},{4,5},{5,4},{6,7},{7,6},{8,9},{9,8},{10,11... | collective-permute-start | bytes 393224 | tf_op jit(solution)/shard_map/ppermute | solution.py:463
  16.8 1.3 %collective-permute-start.8 = (bf16[2,256,128]{2,1,0:T(8,128)(2,1)S(1)}, bf16[2,256,128]{2,1,0:T(8,128)(2,1)S(1)}, u32[]{:S(2)}, u32[]{:S(2)}) collective-permute-start(bf16[2,256,128]{2,1,0:T(8,128)(2,1)S(1)} %collective-permute-done.6.refs_0_), channel_id=1, source_target_pairs={{0,1},{1,0},{2,3},{3,2},{4,5},{5,4},{6,7},{7,6},{8,9},{9,8},{10,11... | collective-permute-start | bytes 393224 | tf_op jit(solution)/shard_map/ppermute | solution.py:463

commit v3 on v2

v3 whole, which is shorter than its diff:
```python
import functools

import jax
import jax.numpy as jnp
from jax import lax
from jax.experimental import pallas as pl
from jax.experimental.pallas import tpu as pltpu
from jax.sharding import PartitionSpec as P

CHANNELS = 256
SIDE = 16
PIXELS = 256
LEVELS = 340
NEIGHBOURS = 9
REACH = 2
SPAN = 2 * REACH + 1
COARSE = LEVELS - PIXELS
MARGIN = 16
PAD = 128
WIDE = PIXELS + PAD

VMEM = pl.BlockSpec(memory_space=pltpu.VMEM)
HBM = pl.BlockSpec(memory_space=pltpu.HBM)


def even_pairs(count):
    pairs = []
    for i in range(0, count - 1, 2):
        pairs += [(i, i + 1), (i + 1, i)]
    if count % 2:
        pairs.append((count - 1, count - 1))
    return pairs


def odd_pairs(count, cores):
    pairs, paired = [], set()
    for i in range(1, count - 1, 2):
        paired |= {i, i + 1}
        for c in range(cores):
            pairs += [(i * cores + c, (i + 1) * cores + c), ((i + 1) * cores + c, i * cores + c)]
    for i in range(count):
        if i not in paired:
            pairs += [(i * cores + c, i * cores + (c + 1) % cores) for c in range(cores)]
    return pairs


def frame_links(count):
    if count == 2:
        swap = [(0, 1), (1, 0)]
        return [(swap, swap)]
    onward = [(i, i + 1) for i in range(count - 1)]
    back = [(i + 1, i) for i in range(count - 1)]
    return [(onward, back), (back, onward)]


def coarse_weights(shape, pixel_axis):
    pixel = lax.broadcasted_iota(jnp.int32, shape, pixel_axis)
    cell = lax.broadcasted_iota(jnp.int32, shape, 1 - pixel_axis)
    row, column = lax.shift_right_logical(pixel, 4), jnp.bitwise_and(pixel, SIDE - 1)
    table = jnp.zeros(shape, jnp.float32)
    base = 0
    for level, across in ((1, 8), (2, 4), (3, 2)):
        target = base + lax.shift_right_logical(row, level) * across + lax.shift_right_logical(column, level)
        table = jnp.where(cell == target, 0.25**level, table)
        base += across * across
    return table.astype(jnp.bfloat16)


def column_of(row):
    n = row.shape[1]
    diagonal = lax.broadcasted_iota(jnp.int32, (n, n), 0) == lax.broadcasted_iota(jnp.int32, (n, n), 1)
    return jnp.sum(jnp.where(diagonal, row, 0.0), axis=1, keepdims=True)


def valid_row(valid_ref, a, core, half):
    row = valid_ref[a : a + 1, :].astype(jnp.float32)
    return jnp.where(core == 0, row[:, :half], row[:, half:])


def relative(neighbours_ref, a, k, first):
    return neighbours_ref[a, k] - (first + a) + REACH


def gate(pairing_ref, j, partners):
    if partners == 1:
        column = 1 - lax.axis_index("frame")
    else:
        column = j
    return pairing_ref[0, column].astype(jnp.float32) / 16.0


def entry_pairs(tiles):
    rows = LEVELS * tiles
    for k in range(0, NEIGHBOURS, 2):
        entries = range(k, min(k + 2, NEIGHBOURS))
        yield entries, k * rows, len(entries) * rows


def in_hbm(*arrays):
    return [pltpu.with_memory_space_constraint(z, pltpu.HBM) for z in arrays]


def copies(sources, targets, sems):
    started = [pltpu.make_async_copy(s, t, sems.at[i]) for i, (s, t) in enumerate(zip(sources, targets, strict=True))]
    for copy in started:
        copy.start()
    return started


def side_bases(tiles):
    parity = lax.rem(lax.axis_index("tile"), 2)
    return (1 - parity) * 2 * tiles, parity * 2 * tiles


def shape_of(shape, dtype=jnp.bfloat16):
    return jax.ShapeDtypeStruct(shape, dtype)


def call(kernel, name, outs, in_specs, out_specs, scratch, vmem_mib):
    return pl.pallas_call(
        kernel,
        out_shape=outs,
        in_specs=in_specs,
        out_specs=out_specs,
        scratch_shapes=scratch,
        compiler_params=pltpu.CompilerParams(vmem_limit_bytes=vmem_mib * 2**20),
        name=name,
    )


def fold_kernel(tiles, half, partners, neighbours_hbm, valid_hbm, pairing_hbm, cot_hbm, features_hbm, *refs):
    folded_ref, x_ref, gates_ref, keep_ref, pool_ref, list_ref = refs[:6]
    neighbours_ref, valid_ref, pairing_ref, cot_ref, stage, total, sems = refs[6:]
    core = lax.axis_index("chan")
    first = lax.axis_index("tile") * tiles
    parts = list(entry_pairs(tiles))
    views = [pl.ds(start, size) for _, start, size in parts]
    small, (features_copy, list_copy, *waits) = split(
        copies(
            [neighbours_hbm, valid_hbm, pairing_hbm, features_hbm.at[0], neighbours_hbm] + [cot_hbm.at[v] for v in views],
            [neighbours_ref, valid_ref, pairing_ref, x_ref, list_ref] + [cot_ref.at[v] for v in views],
            sems,
        ),
        3,
    )
    pool_ref[...] = coarse_weights((PAD, PIXELS), 1)
    pool = coarse_weights((PIXELS, PAD), 0)
    total[...] = jnp.zeros_like(total)
    for copy in small:
        copy.wait()
    keep = [valid_row(valid_ref, a, core, half) for a in range(tiles)]
    columns = [jnp.broadcast_to(column_of(row), (half, half)) for row in keep]
    for j in range(partners):
        weight = gate(pairing_ref, j, partners)
        gates_ref[j] = jnp.full(gates_ref.shape[1:], weight, jnp.float32)
        for a in range(tiles):
            keep_ref[j, a * half : (a + 1) * half] = columns[a] * weight
    for (entries, start, size), copy in zip(parts, waits, strict=True):
        copy.wait()
        stage[:size] = cot_ref[start : start + size, :].astype(jnp.float32)
        for i, k in enumerate(entries):
            for a in range(tiles):
                w = relative(neighbours_ref, a, k, first)
                total[a, w, :LEVELS] += stage[pl.ds(i * LEVELS * tiles + a, LEVELS, stride=tiles), :]
    for a in range(tiles):
        for w in range(SPAN):
            coarse = total[a, w, PIXELS:].astype(jnp.bfloat16)
            spread = jnp.dot(pool, coarse, preferred_element_type=jnp.float32)
            folded_ref[fold_rows(a, w)] = ((total[a, w, :PIXELS] + spread) * keep[a]).astype(jnp.bfloat16)
    features_copy.wait()
    list_copy.wait()
    _, there = halves(core, half)
    for a in range(tiles):
        folded_ref[query_rows(tiles, half, a)] = x_ref[a, there, :]


def split(items, count):
    return items[:count], items[count:]


def fold_rows(a, w):
    start = (a * SPAN + w) * PIXELS
    return slice(start, start + PIXELS)


def query_rows(tiles, half, a):
    start = tiles * SPAN * PIXELS + a * half
    return slice(start, start + half)


def fold(partners, neighbours, valid, pairing, cotangent, features):
    rows, half = cotangent.shape
    _, tiles, pixels, channels = features.shape
    return call(
        functools.partial(fold_kernel, tiles, half, partners),
        "fold",
        (
            shape_of((tiles * SPAN * PIXELS + tiles * half, half)),
            shape_of((tiles, pixels, channels)),
            shape_of((partners, 8, channels), jnp.float32),
            shape_of((partners, tiles * half, channels), jnp.float32),
            shape_of((PAD, PIXELS)),
            shape_of(neighbours.shape, jnp.int32),
        ),
        [HBM] * 5,
        (VMEM,) * 6,
        [
            pltpu.SMEM(neighbours.shape, jnp.int32),
            pltpu.VMEM(valid.shape, jnp.int32),
            pltpu.SMEM(pairing.shape, jnp.int32),
            pltpu.VMEM((rows, half), jnp.bfloat16),
            pltpu.VMEM((2 * LEVELS * tiles, half), jnp.float32),
            pltpu.VMEM((tiles, SPAN, WIDE, half), jnp.float32),
            pltpu.SemaphoreType.DMA((5 + (NEIGHBOURS + 1) // 2,)),
        ],
        8,
    )(*in_hbm(neighbours, valid, pairing, cotangent, features))


def halves(core, half):
    here = pl.ds(pl.multiple_of(core * half, half), half)
    there = pl.ds(pl.multiple_of((1 - core) * half, half), half)
    return here, there


def keys_kernel(tiles, half, x_ref, mine_ref, other_ref, own_ref, even_ref, odd_ref, window):
    here, there = halves(lax.axis_index("chan"), half)
    for a in range(tiles):
        queries = jnp.concatenate([x_ref[a, here, :], x_ref[a, there, :]], axis=0)
        for w in range(SPAN):
            grads = jnp.concatenate([mine_ref[fold_rows(a, w)], other_ref[fold_rows(a, w)]], axis=1)
            term = jnp.dot(grads, queries, preferred_element_type=jnp.float32)
            slot = a + w
            if a == 0 or w == SPAN - 1:
                window[slot] = term
            else:
                window[slot] += term
    own_ref[...] = window[tiles : 2 * tiles]
    even, odd = side_bases(tiles)
    for a in range(tiles):
        even_ref[a] = window[even + a].astype(jnp.bfloat16)
        odd_ref[a] = window[odd + a].astype(jnp.bfloat16)


def keys(x, mine, other):
    tiles, half = x.shape[0], mine.shape[1]
    return call(
        functools.partial(keys_kernel, tiles, half),
        "keys",
        (shape_of(x.shape, jnp.float32), shape_of(x.shape), shape_of(x.shape)),
        [VMEM] * 3,
        (VMEM,) * 3,
        [pltpu.VMEM((3 * tiles,) + x.shape[1:], jnp.float32)],
        6,
    )(x, mine, other)


def returns_kernel(partners, gates_ref, own_ref, even_ref, odd_ref, *out_refs):
    tile, count = lax.axis_index("tile"), lax.axis_size("tile")
    parity = lax.rem(tile, 2)
    has_even = jnp.logical_or(parity == 1, tile + 1 < count)
    has_odd = jnp.logical_or(jnp.logical_and(parity == 0, tile > 0), jnp.logical_and(parity == 1, tile + 1 < count))
    tiles, pixels, _ = own_ref.shape
    for a in range(tiles):
        total = own_ref[a]
        total = total + jnp.where(has_even, even_ref[a].astype(jnp.float32), 0.0)
        total = total + jnp.where(has_odd, odd_ref[a].astype(jnp.float32), 0.0)
        for j in range(partners):
            out_refs[j][a * pixels : (a + 1) * pixels] = (total * gates_ref[j, :1]).astype(jnp.bfloat16)
    for j in range(partners):
        out_refs[j][tiles * pixels :] = jnp.zeros((MARGIN, out_refs[j].shape[1]), jnp.bfloat16)


def returns(partners, gates, own, even, odd):
    tiles, pixels, channels = own.shape
    return call(
        functools.partial(returns_kernel, partners),
        "returns",
        (shape_of((tiles * pixels + MARGIN, channels)),) * partners,
        [VMEM] * 4,
        (VMEM,) * partners,
        [],
        3,
    )(gates, own, even, odd)


def join(mine, other):
    core = lax.axis_index("chan")
    return jnp.concatenate([jnp.where(core == 0, mine, other), jnp.where(core == 0, other, mine)], axis=-1)


def multiply(left, right, contract):
    return lax.dot_general(left, right, ((contract[:1], contract[1:]), ((), ())), preferred_element_type=jnp.float32)


def window_slots(tiles):
    even, odd = side_bases(tiles)
    return tiles, even, odd


def sides_kernel(tiles, half, partners, gates_ref, folded_ref, other_ref, *refs):
    inputs, (grad_ref, levels) = refs[: 3 * partners], refs[3 * partners :]
    here, there = halves(lax.axis_index("chan"), half)
    for j in range(partners):
        for part, base in enumerate(window_slots(tiles)):
            levels[j, pl.ds(base, tiles)] = inputs[3 * j + part][...]
    for a in range(tiles):
        grad = None
        for j in range(partners):
            term = None
            for w in range(SPAN):
                both = jnp.concatenate([folded_ref[fold_rows(a, w)], other_ref[fold_rows(a, w)]], axis=1)
                part = multiply(both, levels[j, a + w], (0, 0))
                term = part if term is None else term + part
            term = term * gates_ref[j, :1]
            grad = term if grad is None else grad + term
        grad_ref[a, here, :] = grad[:half]
        grad_ref[a, there, :] = grad[half:]


def sides(partners, gates, folded, other, windows):
    tiles, pixels, channels = windows[0].shape
    return call(
        functools.partial(sides_kernel, tiles, pixels // 2, partners),
        "sides",
        shape_of(windows[0].shape, jnp.float32),
        [VMEM] * (3 + len(windows)),
        VMEM,
        [pltpu.VMEM((partners, 3 * tiles, pixels, channels), jnp.bfloat16)],
        6,
    )(gates, folded, other, *windows)


def near_kernel(tiles, half, partners, keep_ref, pool_ref, x_ref, other_ref, *refs):
    same, (queries_ref, fine_ref, coarse_ref) = refs[: 2 * partners], refs[2 * partners :]
    here, _ = halves(lax.axis_index("chan"), half)
    mine = jnp.concatenate([x_ref[a, here, :] for a in range(tiles)], axis=0).astype(jnp.float32)
    other = jnp.concatenate([other_ref[query_rows(tiles, half, a)] for a in range(tiles)], axis=0).astype(jnp.float32)
    pool = pool_ref[...]
    for j in range(partners):
        queries_ref[j] = join(mine * keep_ref[j], other * keep_ref[j]).T.astype(jnp.bfloat16)
    for s in range(tiles):
        fine, coarse = None, None
        for j in range(partners):
            level = join(same[2 * j][s], same[2 * j + 1][s])
            cells = jnp.dot(pool, level, preferred_element_type=jnp.float32).astype(jnp.bfloat16)
            fine_term = multiply(level, queries_ref[j], (1, 0))
            coarse_term = multiply(cells, queries_ref[j], (1, 0))
            fine = fine_term if fine is None else fine + fine_term
            coarse = coarse_term if coarse is None else coarse + coarse_term
        fine_ref[s] = fine
        coarse_ref[s] = coarse


def near(partners, keep, pool, x, other, same):
    tiles, pixels, channels = x.shape
    return call(
        functools.partial(near_kernel, tiles, pixels // 2, partners),
        "near",
        (
            shape_of((partners, 2 * channels, tiles * pixels // 2)),
            shape_of((tiles, pixels, tiles * pixels // 2), jnp.float32),
            shape_of((tiles, PAD, tiles * pixels // 2), jnp.float32),
        ),
        [VMEM] * (4 + len(same)),
        (VMEM,) * 3,
        [],
        6,
    )(keep, pool, x, other, *same)


def volume_kernel(tiles, half, partners, list_ref, queries_ref, near_fine, near_coarse, pool_ref, part_ref, *refs):
    inputs, returned, rest = refs[: 4 * partners], refs[4 * partners : 5 * partners], refs[5 * partners :]
    volume_hbm, grad_hbm, neighbours_ref, levels, cells, fine_table, coarse_table = rest[:7]
    stage, volume_ref, grad_ref, sems = rest[7:]
    (neighbours_copy,) = copies([list_ref], [neighbours_ref], sems)
    first = lax.axis_index("tile") * tiles
    pixels = grad_ref.shape[1]
    for a in range(tiles):
        total = part_ref[a]
        for j in range(partners):
            total = total + returned[j][a * pixels : (a + 1) * pixels].astype(jnp.float32)
        grad_ref[a] = total
    waits = [pltpu.make_async_copy(grad_ref, grad_hbm.at[0], sems.at[1])]
    waits[0].start()
    pool = pool_ref[...]
    for j in range(partners):
        for part in range(2):
            for a in range(tiles):
                level = join(inputs[4 * j + part][a], inputs[4 * j + 2 + part][a])
                at = part * tiles + a
                levels[j, at * PIXELS : (at + 1) * PIXELS] = level
                cells[j, at * PAD : (at + 1) * PAD] = jnp.dot(
                    pool, level, preferred_element_type=jnp.float32
                ).astype(jnp.bfloat16)
    fine_table[tiles : 2 * tiles] = near_fine[...]
    coarse_table[tiles : 2 * tiles] = near_coarse[...]
    for keys_at, table in ((levels, fine_table), (cells, coarse_table)):
        total = multiply(keys_at[0], queries_ref[0], (1, 0))
        for j in range(1, partners):
            total = total + multiply(keys_at[j], queries_ref[j], (1, 0))
        total = total.reshape(2, tiles, table.shape[1], tiles * half)
        for part, base in enumerate(side_bases(tiles)):
            table[pl.ds(base, tiles)] = total[part]
    neighbours_copy.wait()
    for i_part, (entries, start, size) in enumerate(entry_pairs(tiles)):
        for i, k in enumerate(entries):
            for a in range(tiles):
                slot = relative(neighbours_ref, a, k, first) + a
                lanes = slice(a * half, (a + 1) * half)
                base = i * LEVELS * tiles + a
                stage[pl.ds(base, PIXELS, stride=tiles), :] = fine_table[slot, :, lanes]
                stage[pl.ds(base + PIXELS * tiles, COARSE, stride=tiles), :] = coarse_table[slot, :COARSE, lanes]
        rows = pl.ds(start, size)
        volume_ref[rows, :] = stage[:size].astype(jnp.bfloat16)
        copy = pltpu.make_async_copy(volume_ref.at[rows], volume_hbm.at[rows], sems.at[2 + i_part])
        copy.start()
        waits.append(copy)
    for copy in waits:
        copy.wait()


def volumes(partners, neighbours, queries, near_fine, near_coarse, pool, grad, beside, returned):
    tiles, pixels, channels = grad.shape
    half = pixels // 2
    rows = NEIGHBOURS * LEVELS * tiles
    return call(
        functools.partial(volume_kernel, tiles, half, partners),
        "volume",
        (shape_of((rows, half)), shape_of((1,) + grad.shape, jnp.float32)),
        [VMEM] * (6 + len(beside) + len(returned)),
        (HBM, HBM),
        [
            pltpu.SMEM(neighbours.shape, jnp.int32),
            pltpu.VMEM((partners, 2 * tiles * PIXELS, 2 * channels), jnp.bfloat16),
            pltpu.VMEM((partners, 2 * tiles * PAD, 2 * channels), jnp.bfloat16),
            pltpu.VMEM((3 * tiles, PIXELS, tiles * half), jnp.float32),
            pltpu.VMEM((3 * tiles, PAD, tiles * half), jnp.float32),
            pltpu.VMEM((2 * LEVELS * tiles, half), jnp.float32),
            pltpu.VMEM((rows, half), jnp.bfloat16),
            pltpu.VMEM(grad.shape, jnp.float32),
            pltpu.SemaphoreType.DMA((2 + (NEIGHBOURS + 1) // 2,)),
        ],
        12,
    )(neighbours, queries, near_fine, near_coarse, pool, grad, *beside, *returned)


def after(value, earlier):
    return lax.optimization_barrier((value, earlier))[0]


def local(features, neighbours, pairing, valid_tiles, cotangent):
    count = lax.axis_size("tile")
    cores = lax.axis_size("chan")
    links = frame_links(lax.axis_size("frame"))
    partners = len(links)
    tiles, half = cotangent.shape[1:3]
    swap = [(c, (c + 1) % cores) for c in range(cores)]
    evens, odds = even_pairs(count), odd_pairs(count, cores)

    def over_even(z):
        return lax.ppermute(z, "tile", evens)

    def over_odd(z):
        return lax.ppermute(z, ("tile", "chan"), odds)

    def over_cores(z):
        return lax.ppermute(z, "chan", swap)

    upstream = jnp.transpose(cotangent[0], (2, 0, 1)).reshape(NEIGHBOURS * LEVELS * tiles, half)
    folded, x, gates, keep, pool, listed = fold(partners, neighbours, valid_tiles, pairing, upstream, features)
    other = over_cores(folded)
    arrived = [lax.ppermute(x, "frame", ahead) for ahead, _ in links]
    own, to_even, to_odd = keys(x, folded, other)
    arrived = [after(y, own) for y in arrived]
    beside = [(over_even(y), over_odd(y)) for y in arrived]
    from_odd = over_odd(to_odd)
    from_even = after(over_even(to_even), from_odd)
    sent = returns(partners, gates, own, from_even, from_odd)
    returned = [lax.ppermute(z, "frame", back) for z, (_, back) in zip(sent, links, strict=True)]
    same = []
    for y in arrived:
        same += [after(y, sent[0]), after(over_cores(y), sent[0])]
    queries, near_fine, near_coarse = near(partners, keep, pool, x, other, same)
    mine, exchanged = [], []
    for y, (even, odd) in zip(arrived, beside, strict=True):
        even = after(even, near_fine)
        odd = after(odd, even)
        mine += [y, even, odd]
        exchanged += [even, odd, over_cores(even), over_cores(odd)]
    grad = sides(partners, gates, folded, other, mine)
    exchanged = [after(z, grad) for z in exchanged]
    volume, feature_grad = volumes(
        partners, listed, queries, near_fine, near_coarse, pool, grad, exchanged, returned
    )
    volume = jnp.transpose(volume.reshape(NEIGHBOURS * LEVELS, tiles, half), (1, 2, 0))
    return volume[None], feature_grad


def solution(mesh):
    return jax.shard_map(
        local,
        mesh=mesh,
        in_specs=(
            P(("clip", "frame"), "tile", None, "chan"),
            P(("clip", "tile"), None),
            P(("clip", "frame"), None),
            P(("clip", "tile"), None),
            P(("clip", "frame"), "tile", "chan", None),
        ),
        out_specs=(
            P(("clip", "frame"), "tile", "chan", None),
            P(("clip", "frame"), "tile", None, "chan"),
        ),
        check_vma=False,
    )
```

time: 21.5 us -> 20.1 us (0.935)
  the two profiles are of different devices: /device:TPU:13 before, /device:TPU:0 now
where the time goes in v3:
time: 20.1 us; the launch traced here: 19.9 us
  starting transfers between devices  9.69 us (48%)
  Pallas kernels  5.75 us (29%)
  waiting for transfers between devices  3.79 us (19%)
  between operations  0.67 us (3%)
    ppermute x2, starting transfers between devices, over_even(): return lax.ppermute(z, 'tile', evens)  4.14 us
    ppermute x1, starting transfers between devices, local(): arrived = [lax.ppermute(x, 'frame', ahead) for ahead, _ in links]  2.56 us
    pallas_call x1, Pallas kernels, fold(): call(functools.partial(fold_kernel, tiles, half, partners), 'fold', (shap...  2.08 us
    pallas_call x1, Pallas kernels, volumes(): call(functools.partial(volume_kernel, tiles, half, partners), 'volume', (...  1.96 us
    ppermute x1, starting transfers between devices, local(): lax.ppermute(z, 'frame', back)  1.73 us
    ppermute x2, waiting for transfers between devices, over_even(): return lax.ppermute(z, 'tile', evens)  1.64 us
    ppermute x1, waiting for transfers between devices, local(): arrived = [lax.ppermute(x, 'frame', ahead) for ahead, _ in links]  1.27 us
    ppermute x4, starting transfers between devices, over_cores(): return lax.ppermute(z, 'chan', swap)  1.03 us
  transfers between devices with their start and end apart: 10, of which 6 were waited for; matrix products, arithmetic and copies ran while one was open for 0% of the time, Pallas kernels for 9%

profile of v3, /device:TPU:0, one launch (start us, length us, event | category | flops | bytes accessed | tf_op | source)
XLA Modules:
  0.0 19.9 jit_solution(13347541126088747662)
XLA Ops:
  0.6 2.1 %fold.1 = (bf16[2816,128]{1,0:T(8,128)(2,1)S(1)}, bf16[2,256,128]{2,1,0:T(8,128)(2,1)S(1)}, f32[1,8,128]{2,1,0:T(8,128)S(1)}, f32[1,256,128]{2,1,0:T(8,128)S(1)}...) custom-call(s32[2,9]{1,0:T(2,128)} %neighbours_hbm.1, s32[2,256]{1,0:T(2,128)} %valid_hbm.1, s32[1,2]{1,0:T(1,128)} %pairing_hbm.1, ...), custom_call_target="tpu_custom_call" | custom-call | tf_op jit(solution)/shard_map/fold/pallas_call | solution.py:194
  2.7 0.5 %collective-permute-start = (bf16[2816,128]{1,0:T(8,128)(2,1)S(1)}, bf16[2816,128]{1,0:T(8,128)(2,1)S(1)}, u32[]{:S(2)}, u32[]{:S(2)}) collective-permute-start(bf16[2816,128]{1,0:T(8,128)(2,1)S(1)} %get-tuple-element.30.mine_ref.folded_ref), channel_id=1, source_target_pairs={{0,1},{1,0},{2,3},{3,2},{4,5},{5,4},{6,7},{7,6},{8,9},{9,8},{10,11... | collective-permute-start | bytes 2162696 | tf_op jit(solution)/shard_map/ppermute | solution.py:468
  3.2 2.6 %collective-permute-start.1 = (bf16[2,256,128]{2,1,0:T(8,128)(2,1)S(1)}, bf16[2,256,128]{2,1,0:T(8,128)(2,1)S(1)}, u32[]{:S(2)}, u32[]{:S(2)}) collective-permute-start(bf16[2,256,128]{2,1,0:T(8,128)(2,1)S(1)} %get-tuple-element.29.x_ref), channel_id=1, source_target_pairs={{0,2},{2,0},{1,3},{3,1},{4,6},{6,4},{5,7},{7,5},{8,10},{10,8},{9,1... | collective-permute-start | bytes 393224 | tf_op jit(solution)/shard_map/ppermute | solution.py:473
  5.8 0.0 collective-permute-done.other_ref
  5.8 0.5 %keys.1 = (f32[2,256,128]{2,1,0:T(8,128)S(1)}, bf16[2,256,128]{2,1,0:T(8,128)(2,1)S(1)}, bf16[2,256,128]{2,1,0:T(8,128)(2,1)S(1)}) custom-call(bf16[2,256,128]{2,1,0:T(8,128)(2,1)S(1)} %get-tuple-element.29.x_ref, bf16[2816,128]{1,0:T(8,128)(2,1)S(1)} %get-tuple-element.30.mine_ref.folded_ref, bf16[2816,128]{1,0:T(8,128)(2,1)S(1)} %collective-permute-done.other_ref), custom_call_target="tpu_custom_call" | custom-call | tf_op jit(solution)/shard_map/keys/pallas_call | solution.py:247
  6.4 2.3 %collective-permute-start.2 = (bf16[2,256,128]{2,1,0:T(8,128)(2,1)S(1)}, bf16[2,256,128]{2,1,0:T(8,128)(2,1)S(1)}, u32[]{:S(2)}, u32[]{:S(2)}) collective-permute-start(bf16[2,256,128]{2,1,0:T(8,128)(2,1)S(1)} %get-tuple-element.34), channel_id=1, source_target_pairs={{0,4},{4,0},{8,12},{12,8},{1,5},{5,1},{9,13},{13,9},{2,6},{6,2},{1... | collective-permute-start | bytes 393224 | tf_op jit(solution)/shard_map/ppermute | solution.py:462
  8.6 0.0 collective-permute-start.3
  8.6 1.3 %collective-permute-done.1.refs_0_ = bf16[2,256,128]{2,1,0:T(8,128)(2,1)S(1)} collective-permute-done((bf16[2,256,128]{2,1,0:T(8,128)(2,1)S(1)}, bf16[2,256,128]{2,1,0:T(8,128)(2,1)S(1)}, u32[]{:S(2)}, u32[]{:S(2)}) %collective-permute-start.1) | collective-permute-done | bytes 131104 | tf_op jit(solution)/shard_map/ppermute | solution.py:473
  9.9 0.0 collective-permute-start.4
  9.9 1.9 %collective-permute-start.5 = (bf16[2,256,128]{2,1,0:T(8,128)(2,1)S(1)}, bf16[2,256,128]{2,1,0:T(8,128)(2,1)S(1)}, u32[]{:S(2)}, u32[]{:S(2)}) collective-permute-start(bf16[2,256,128]{2,1,0:T(8,128)(2,1)S(1)} %collective-permute-done.1.refs_0_), channel_id=1, source_target_pairs={{0,4},{4,0},{8,12},{12,8},{1,5},{5,1},{9,13},{13,9},{2,6},{6,2},{1... | collective-permute-start | bytes 393224 | tf_op jit(solution)/shard_map/ppermute | solution.py:462
  11.8 0.2 %collective-permute-start.6 = (bf16[2,256,128]{2,1,0:T(8,128)(2,1)S(1)}, bf16[2,256,128]{2,1,0:T(8,128)(2,1)S(1)}, u32[]{:S(2)}, u32[]{:S(2)}) collective-permute-start(bf16[2,256,128]{2,1,0:T(8,128)(2,1)S(1)} %collective-permute-done.1.refs_0_), channel_id=1, source_target_pairs={{4,8},{8,4},{5,9},{9,5},{0,1},{1,0},{12,13},{13,12},{6,10},{10,6},... | collective-permute-start | bytes 393224 | tf_op jit(solution)/shard_map/ppermute | solution.py:465
  12.0 0.4 %collective-permute-done.2.even_ref = bf16[2,256,128]{2,1,0:T(8,128)(2,1)S(1)} collective-permute-done((bf16[2,256,128]{2,1,0:T(8,128)(2,1)S(1)}, bf16[2,256,128]{2,1,0:T(8,128)(2,1)S(1)}, u32[]{:S(2)}, u32[]{:S(2)}) %collective-permute-start.2) | collective-permute-done | bytes 131104 | tf_op jit(solution)/shard_map/ppermute | solution.py:462
  12.4 0.0 collective-permute-done.3.odd_ref
  12.4 0.1 returns.1
  12.5 1.7 %collective-permute-start.9 = (bf16[528,128]{1,0:T(8,128)(2,1)S(1)}, bf16[528,128]{1,0:T(8,128)(2,1)S(1)}, u32[]{:S(2)}, u32[]{:S(2)}) collective-permute-start(bf16[528,128]{1,0:T(8,128)(2,1)S(1)} %returns.1), channel_id=1, source_target_pairs={{0,2},{2,0},{1,3},{3,1},{4,6},{6,4},{5,7},{7,5},{8,10},{10,8},{9,1... | collective-permute-start | bytes 405512 | tf_op jit(solution)/shard_map/ppermute | solution.py:480
  14.2 0.0 collective-permute-done.4.refs_1_
  14.2 0.5 %near.1 = (bf16[1,256,256]{2,1,0:T(8,128)(2,1)S(1)}, f32[2,256,256]{2,1,0:T(8,128)S(1)}, f32[2,128,256]{2,1,0:T(8,128)S(1)}) custom-call(f32[1,256,128]{2,1,0:T(8,128)S(1)} %get-tuple-element.27.keep_ref, bf16[128,256]{1,0:T(8,128)(2,1)S(1)} %get-tuple-element.28.pool_ref, bf16[2,256,128]{2,1,0:T(8,128)(2,1)S(1)} %get-tuple-element.29.x_ref, ...), custom_call_target="tpu_custom_call" | custom-call | tf_op jit(solution)/shard_map/near/pallas_call | solution.py:357
  14.7 1.2 %collective-permute-done.5.refs_1_.refs_0_ = bf16[2,256,128]{2,1,0:T(8,128)(2,1)S(1)} collective-permute-done((bf16[2,256,128]{2,1,0:T(8,128)(2,1)S(1)}, bf16[2,256,128]{2,1,0:T(8,128)(2,1)S(1)}, u32[]{:S(2)}, u32[]{:S(2)}) %collective-permute-start.5) | collective-permute-done | bytes 131104 | tf_op jit(solution)/shard_map/ppermute | solution.py:462
  15.9 0.0 collective-permute-done.6.refs_2_.refs_1_
  15.9 0.0 collective-permute-start.8
  15.9 0.5 %collective-permute-start.7 = (bf16[2,256,128]{2,1,0:T(8,128)(2,1)S(1)}, bf16[2,256,128]{2,1,0:T(8,128)(2,1)S(1)}, u32[]{:S(2)}, u32[]{:S(2)}) collective-permute-start(bf16[2,256,128]{2,1,0:T(8,128)(2,1)S(1)} %collective-permute-done.5.refs_1_.refs_0_), channel_id=1, source_target_pairs={{0,1},{1,0},{2,3},{3,2},{4,5},{5,4},{6,7},{7,6},{8,9},{9,8},{10,11... | collective-permute-start | bytes 393224 | tf_op jit(solution)/shard_map/ppermute | solution.py:468
  16.5 0.6 %sides.1.part_ref = f32[2,256,128]{2,1,0:T(8,128)S(1)} custom-call(f32[1,8,128]{2,1,0:T(8,128)S(1)} %get-tuple-element.33.gates_ref, bf16[2816,128]{1,0:T(8,128)(2,1)S(1)} %get-tuple-element.30.mine_ref.folded_ref, bf16[2816,128]{1,0:T(8,128)(2,1)S(1)} %collective-permute-done.other_ref, bf16[2,256,128]{2,1,0:T(8,128)(2,1)S(1)} %collective-permute-done.1.refs_0_, ...), custom_call_target="tpu_custom_call" | custom-call | tf_op jit(solution)/shard_map/sides/pallas_call | solution.py:323
  17.1 0.2 %collective-permute-done.8.refs_3_ = bf16[2,256,128]{2,1,0:T(8,128)(2,1)S(1)} collective-permute-done((bf16[2,256,128]{2,1,0:T(8,128)(2,1)S(1)}, bf16[2,256,128]{2,1,0:T(8,128)(2,1)S(1)}, u32[]{:S(2)}, u32[]{:S(2)}) %collective-permute-start.8) | collective-permute-done | bytes 131104 | tf_op jit(solution)/shard_map/ppermute | solution.py:468
  17.3 0.2 collective-permute-done.7.refs_2_
  17.5 0.5 %collective-permute-done.9.refs_4_ = bf16[528,128]{1,0:T(8,128)(2,1)S(1)} collective-permute-done((bf16[528,128]{1,0:T(8,128)(2,1)S(1)}, bf16[528,128]{1,0:T(8,128)(2,1)S(1)}, u32[]{:S(2)}, u32[]{:S(2)}) %collective-permute-start.9) | collective-permute-done | bytes 135200 | tf_op jit(solution)/shard_map/ppermute | solution.py:480
  17.9 2.0 %volume.1 = (bf16[6120,128]{1,0:T(8,128)(2,1)}, f32[1,2,256,128]{3,2,1,0:T(8,128)}) custom-call(s32[2,9]{1,0:T(2,128)S(1)} %get-tuple-element.26.list_ref, bf16[1,256,256]{2,1,0:T(8,128)(2,1)S(1)} %get-tuple-element.39.queries_ref, f32[2,256,256]{2,1,0:T(8,128)S(1)} %get-tuple-element.40.near_fine, f32[2,128,256]{2,1,0:T(8,128)S(1)} %get-tuple-element.41.near_coarse, ...), custom_call_target="tpu_custom_call" | custom-call | tf_op jit(solution)/shard_map/volume/pallas_call | solution.py:427
Async XLA Ops:
  2.7 3.1 %collective-permute-start = (bf16[2816,128]{1,0:T(8,128)(2,1)S(1)}, bf16[2816,128]{1,0:T(8,128)(2,1)S(1)}, u32[]{:S(2)}, u32[]{:S(2)}) collective-permute-start(bf16[2816,128]{1,0:T(8,128)(2,1)S(1)} %get-tuple-element.30.mine_ref.folded_ref), channel_id=1, source_target_pairs={{0,1},{1,0},{2,3},{3,2},{4,5},{5,4},{6,7},{7,6},{8,9},{9,8},{10,11... | collective-permute-start | bytes 2162696 | tf_op jit(solution)/shard_map/ppermute | solution.py:468
  3.2 6.7 %collective-permute-start.1 = (bf16[2,256,128]{2,1,0:T(8,128)(2,1)S(1)}, bf16[2,256,128]{2,1,0:T(8,128)(2,1)S(1)}, u32[]{:S(2)}, u32[]{:S(2)}) collective-permute-start(bf16[2,256,128]{2,1,0:T(8,128)(2,1)S(1)} %get-tuple-element.29.x_ref), channel_id=1, source_target_pairs={{0,2},{2,0},{1,3},{3,1},{4,6},{6,4},{5,7},{7,5},{8,10},{10,8},{9,1... | collective-permute-start | bytes 393224 | tf_op jit(solution)/shard_map/ppermute | solution.py:473
  6.4 6.1 %collective-permute-start.2 = (bf16[2,256,128]{2,1,0:T(8,128)(2,1)S(1)}, bf16[2,256,128]{2,1,0:T(8,128)(2,1)S(1)}, u32[]{:S(2)}, u32[]{:S(2)}) collective-permute-start(bf16[2,256,128]{2,1,0:T(8,128)(2,1)S(1)} %get-tuple-element.34), channel_id=1, source_target_pairs={{0,4},{4,0},{8,12},{12,8},{1,5},{5,1},{9,13},{13,9},{2,6},{6,2},{1... | collective-permute-start | bytes 393224 | tf_op jit(solution)/shard_map/ppermute | solution.py:462
  8.6 3.8 %collective-permute-start.3 = (bf16[2,256,128]{2,1,0:T(8,128)(2,1)S(1)}, bf16[2,256,128]{2,1,0:T(8,128)(2,1)S(1)}, u32[]{:S(2)}, u32[]{:S(2)}) collective-permute-start(bf16[2,256,128]{2,1,0:T(8,128)(2,1)S(1)} %get-tuple-element.35), channel_id=1, source_target_pairs={{4,8},{8,4},{5,9},{9,5},{0,1},{1,0},{12,13},{13,12},{6,10},{10,6},... | collective-permute-start | bytes 393224 | tf_op jit(solution)/shard_map/ppermute | solution.py:465
  9.9 4.3 %collective-permute-start.4 = (bf16[2,256,128]{2,1,0:T(8,128)(2,1)S(1)}, bf16[2,256,128]{2,1,0:T(8,128)(2,1)S(1)}, u32[]{:S(2)}, u32[]{:S(2)}) collective-permute-start(bf16[2,256,128]{2,1,0:T(8,128)(2,1)S(1)} %collective-permute-done.1.refs_0_), channel_id=1, source_target_pairs={{0,1},{1,0},{2,3},{3,2},{4,5},{5,4},{6,7},{7,6},{8,9},{9,8},{10,11... | collective-permute-start | bytes 393224 | tf_op jit(solution)/shard_map/ppermute | solution.py:468
  9.9 6.0 %collective-permute-start.5 = (bf16[2,256,128]{2,1,0:T(8,128)(2,1)S(1)}, bf16[2,256,128]{2,1,0:T(8,128)(2,1)S(1)}, u32[]{:S(2)}, u32[]{:S(2)}) collective-permute-start(bf16[2,256,128]{2,1,0:T(8,128)(2,1)S(1)} %collective-permute-done.1.refs_0_), channel_id=1, source_target_pairs={{0,4},{4,0},{8,12},{12,8},{1,5},{5,1},{9,13},{13,9},{2,6},{6,2},{1... | collective-permute-start | bytes 393224 | tf_op jit(solution)/shard_map/ppermute | solution.py:462
  11.8 4.2 %collective-permute-start.6 = (bf16[2,256,128]{2,1,0:T(8,128)(2,1)S(1)}, bf16[2,256,128]{2,1,0:T(8,128)(2,1)S(1)}, u32[]{:S(2)}, u32[]{:S(2)}) collective-permute-start(bf16[2,256,128]{2,1,0:T(8,128)(2,1)S(1)} %collective-permute-done.1.refs_0_), channel_id=1, source_target_pairs={{4,8},{8,4},{5,9},{9,5},{0,1},{1,0},{12,13},{13,12},{6,10},{10,6},... | collective-permute-start | bytes 393224 | tf_op jit(solution)/shard_map/ppermute | solution.py:465
  12.5 5.4 %collective-permute-start.9 = (bf16[528,128]{1,0:T(8,128)(2,1)S(1)}, bf16[528,128]{1,0:T(8,128)(2,1)S(1)}, u32[]{:S(2)}, u32[]{:S(2)}) collective-permute-start(bf16[528,128]{1,0:T(8,128)(2,1)S(1)} %returns.1), channel_id=1, source_target_pairs={{0,2},{2,0},{1,3},{3,1},{4,6},{6,4},{5,7},{7,5},{8,10},{10,8},{9,1... | collective-permute-start | bytes 405512 | tf_op jit(solution)/shard_map/ppermute | solution.py:480
  15.9 1.3 %collective-permute-start.8 = (bf16[2,256,128]{2,1,0:T(8,128)(2,1)S(1)}, bf16[2,256,128]{2,1,0:T(8,128)(2,1)S(1)}, u32[]{:S(2)}, u32[]{:S(2)}) collective-permute-start(bf16[2,256,128]{2,1,0:T(8,128)(2,1)S(1)} %collective-permute-done.6.refs_2_.refs_1_), channel_id=1, source_target_pairs={{0,1},{1,0},{2,3},{3,2},{4,5},{5,4},{6,7},{7,6},{8,9},{9,8},{10,11... | collective-permute-start | bytes 393224 | tf_op jit(solution)/shard_map/ppermute | solution.py:468
  15.9 1.5 %collective-permute-start.7 = (bf16[2,256,128]{2,1,0:T(8,128)(2,1)S(1)}, bf16[2,256,128]{2,1,0:T(8,128)(2,1)S(1)}, u32[]{:S(2)}, u32[]{:S(2)}) collective-permute-start(bf16[2,256,128]{2,1,0:T(8,128)(2,1)S(1)} %collective-permute-done.5.refs_1_.refs_0_), channel_id=1, source_target_pairs={{0,1},{1,0},{2,3},{3,2},{4,5},{5,4},{6,7},{7,6},{8,9},{9,8},{10,11... | collective-permute-start | bytes 393224 | tf_op jit(solution)/shard_map/ppermute | solution.py:468

commit v4 on v3

--- a/solution.py
+++ b/solution.py
@@ -16,6 +16,7 @@
 SPAN = 2 * REACH + 1
 COARSE = LEVELS - PIXELS
 MARGIN = 16
+STAGES = 9
 PAD = 128
 WIDE = PIXELS + PAD
 
@@ -116,13 +117,14 @@
     return jax.ShapeDtypeStruct(shape, dtype)
 
 
-def call(kernel, name, outs, in_specs, out_specs, scratch, vmem_mib):
+def call(kernel, name, outs, in_specs, out_specs, scratch, vmem_mib, aliases=None):
     return pl.pallas_call(
         kernel,
         out_shape=outs,
         in_specs=in_specs,
         out_specs=out_specs,
         scratch_shapes=scratch,
+        input_output_aliases=aliases or {},
         compiler_params=pltpu.CompilerParams(vmem_limit_bytes=vmem_mib * 2**20),
         name=name,
     )
@@ -130,22 +132,21 @@
 
 def fold_kernel(tiles, half, partners, neighbours_hbm, valid_hbm, pairing_hbm, cot_hbm, features_hbm, *refs):
     folded_ref, x_ref, gates_ref, keep_ref, pool_ref, list_ref = refs[:6]
-    neighbours_ref, valid_ref, pairing_ref, cot_ref, stage, total, sems = refs[6:]
+    neighbours_ref, valid_ref, pairing_ref, cot_ref, stage, sems, *totals = refs[6:]
     core = lax.axis_index("chan")
     first = lax.axis_index("tile") * tiles
-    parts = list(entry_pairs(tiles))
-    views = [pl.ds(start, size) for _, start, size in parts]
     small, (features_copy, list_copy, *waits) = split(
         copies(
-            [neighbours_hbm, valid_hbm, pairing_hbm, features_hbm.at[0], neighbours_hbm] + [cot_hbm.at[v] for v in views],
-            [neighbours_ref, valid_ref, pairing_ref, x_ref, list_ref] + [cot_ref.at[v] for v in views],
+            [neighbours_hbm, valid_hbm, pairing_hbm, features_hbm.at[0], neighbours_hbm] + [cot_hbm.at[k] for k in range(NEIGHBOURS)],
+            [neighbours_ref, valid_ref, pairing_ref, x_ref, list_ref] + [cot_ref.at[k] for k in range(NEIGHBOURS)],
             sems,
         ),
         3,
     )
     pool_ref[...] = coarse_weights((PAD, PIXELS), 1)
     pool = coarse_weights((PIXELS, PAD), 0)
-    total[...] = jnp.zeros_like(total)
+    for total in totals:
+        total[...] = jnp.zeros_like(total)
     for copy in small:
         copy.wait()
     keep = [valid_row(valid_ref, a, core, half) for a in range(tiles)]
@@ -155,18 +156,17 @@
         gates_ref[j] = jnp.full(gates_ref.shape[1:], weight, jnp.float32)
         for a in range(tiles):
             keep_ref[j, a * half : (a + 1) * half] = columns[a] * weight
-    for (entries, start, size), copy in zip(parts, waits, strict=True):
+    for k, copy in enumerate(waits):
         copy.wait()
-        stage[:size] = cot_ref[start : start + size, :].astype(jnp.float32)
-        for i, k in enumerate(entries):
-            for a in range(tiles):
-                w = relative(neighbours_ref, a, k, first)
-                total[a, w, :LEVELS] += stage[pl.ds(i * LEVELS * tiles + a, LEVELS, stride=tiles), :]
+        stage[k % STAGES] = cot_ref[k].astype(jnp.float32).reshape(LEVELS * tiles, half)
+        for a in range(tiles):
+            w = relative(neighbours_ref, a, k, first)
+            totals[a][w, :LEVELS] += stage[k % STAGES, pl.ds(a, LEVELS, stride=tiles), :]
     for a in range(tiles):
         for w in range(SPAN):
-            coarse = total[a, w, PIXELS:].astype(jnp.bfloat16)
+            coarse = totals[a][w, PIXELS:].astype(jnp.bfloat16)
             spread = jnp.dot(pool, coarse, preferred_element_type=jnp.float32)
-            folded_ref[fold_rows(a, w)] = ((total[a, w, :PIXELS] + spread) * keep[a]).astype(jnp.bfloat16)
+            folded_ref[fold_rows(a, w)] = ((totals[a][w, :PIXELS] + spread) * keep[a]).astype(jnp.bfloat16)
     features_copy.wait()
     list_copy.wait()
     _, there = halves(core, half)
@@ -189,7 +189,7 @@
 
 
 def fold(partners, neighbours, valid, pairing, cotangent, features):
-    rows, half = cotangent.shape
+    half = cotangent.shape[-1]
     _, tiles, pixels, channels = features.shape
     return call(
         functools.partial(fold_kernel, tiles, half, partners),
@@ -208,12 +208,12 @@
             pltpu.SMEM(neighbours.shape, jnp.int32),
             pltpu.VMEM(valid.shape, jnp.int32),
             pltpu.SMEM(pairing.shape, jnp.int32),
-            pltpu.VMEM((rows, half), jnp.bfloat16),
-            pltpu.VMEM((2 * LEVELS * tiles, half), jnp.float32),
-            pltpu.VMEM((tiles, SPAN, WIDE, half), jnp.float32),
-            pltpu.SemaphoreType.DMA((5 + (NEIGHBOURS + 1) // 2,)),
-        ],
-        8,
+            pltpu.VMEM(cotangent.shape, jnp.bfloat16),
+            pltpu.VMEM((STAGES, LEVELS * tiles, half), jnp.float32),
+            pltpu.SemaphoreType.DMA((5 + NEIGHBOURS,)),
+        ]
+        + [pltpu.VMEM((SPAN, WIDE, half), jnp.float32)] * tiles,
+        10,
     )(*in_hbm(neighbours, valid, pairing, cotangent, features))
 
 
@@ -223,23 +223,26 @@
     return here, there
 
 
-def keys_kernel(tiles, half, x_ref, mine_ref, other_ref, own_ref, even_ref, odd_ref, window):
+def keys_kernel(tiles, half, x_ref, mine_ref, other_ref, own_ref, even_ref, odd_ref):
     here, there = halves(lax.axis_index("chan"), half)
+    queries = [jnp.concatenate([x_ref[a, here, :], x_ref[a, there, :]], axis=0) for a in range(tiles)]
+
+    def of_slot(slot):
+        users = [a for a in range(tiles) if 0 <= slot - a < SPAN]
+        blocks = [ref[fold_rows(a, slot - a)] for a in users for ref in (mine_ref, other_ref)]
+        return jnp.dot(
+            jnp.concatenate(blocks, axis=1),
+            jnp.concatenate([queries[a] for a in users], axis=0),
+            preferred_element_type=jnp.float32,
+        )
+
+    parity = lax.rem(lax.axis_index("tile"), 2)
     for a in range(tiles):
-        queries = jnp.concatenate([x_ref[a, here, :], x_ref[a, there, :]], axis=0)
-        for w in range(SPAN):
-            grads = jnp.concatenate([mine_ref[fold_rows(a, w)], other_ref[fold_rows(a, w)]], axis=1)
-            term = jnp.dot(grads, queries, preferred_element_type=jnp.float32)
-            slot = a + w
-            if a == 0 or w == SPAN - 1:
-                window[slot] = term
-            else:
-                window[slot] += term
-    own_ref[...] = window[tiles : 2 * tiles]
-    even, odd = side_bases(tiles)
-    for a in range(tiles):
-        even_ref[a] = window[even + a].astype(jnp.bfloat16)
-        odd_ref[a] = window[odd + a].astype(jnp.bfloat16)
+        below = of_slot(a).astype(jnp.bfloat16)
+        above = of_slot(2 * tiles + a).astype(jnp.bfloat16)
+        even_ref[a] = jnp.where(parity == 0, above, below)
+        odd_ref[a] = jnp.where(parity == 0, below, above)
+        own_ref[a] = of_slot(tiles + a)
 
 
 def keys(x, mine, other):
@@ -250,8 +253,8 @@
         (shape_of(x.shape, jnp.float32), shape_of(x.shape), shape_of(x.shape)),
         [VMEM] * 3,
         (VMEM,) * 3,
-        [pltpu.VMEM((3 * tiles,) + x.shape[1:], jnp.float32)],
-        6,
+        [],
+        4,
     )(x, mine, other)
 
 
@@ -298,8 +301,31 @@
     return tiles, even, odd
 
 
-def sides_kernel(tiles, half, partners, gates_ref, folded_ref, other_ref, *refs):
-    inputs, (grad_ref, levels) = refs[: 3 * partners], refs[3 * partners :]
+def beside_groups(tiles):
+    return slice(0, tiles), slice(2 * tiles, 3 * tiles)
+
+
+def add_scores(tiles, partners, channels, pool, queries_ref, levels, fine_ref, coarse_ref, first):
+    for group in beside_groups(tiles):
+        fine, coarse = None, None
+        for j in range(partners):
+            queries = queries_ref[j, channels, :]
+            level = levels[j, group]
+            width = level.shape[2]
+            cells = [jnp.dot(pool, level[a], preferred_element_type=jnp.float32) for a in range(tiles)]
+            cells = jnp.concatenate(cells, axis=0).astype(jnp.bfloat16)
+            fine_term = multiply(level.reshape(tiles * PIXELS, width), queries, (1, 0))
+            coarse_term = multiply(cells, queries, (1, 0))
+            fine = fine_term if fine is None else fine + fine_term
+            coarse = coarse_term if coarse is None else coarse + coarse_term
+        fine = fine.reshape(tiles, PIXELS, fine.shape[1])
+        coarse = coarse.reshape(tiles, PAD, coarse.shape[1])
+        fine_ref[group] = fine if first else fine_ref[group] + fine
+        coarse_ref[group] = coarse if first else coarse_ref[group] + coarse
+
+
+def sides_kernel(tiles, half, partners, gates_ref, folded_ref, other_ref, pool_ref, queries_ref, near_fine, near_coarse, *refs):
+    inputs, (grad_ref, fine_ref, coarse_ref, levels) = refs[: 3 * partners], refs[3 * partners :]
     here, there = halves(lax.axis_index("chan"), half)
     for j in range(partners):
         for part, base in enumerate(window_slots(tiles)):
@@ -316,19 +342,22 @@
             grad = term if grad is None else grad + term
         grad_ref[a, here, :] = grad[:half]
         grad_ref[a, there, :] = grad[half:]
-
-
-def sides(partners, gates, folded, other, windows):
+    mine, _ = halves(lax.axis_index("chan"), grad_ref.shape[2])
+    add_scores(tiles, partners, mine, pool_ref[...], queries_ref, levels, fine_ref, coarse_ref, True)
+
+
+def sides(partners, gates, folded, other, pool, queries, fine, coarse, windows):
     tiles, pixels, channels = windows[0].shape
     return call(
         functools.partial(sides_kernel, tiles, pixels // 2, partners),
         "sides",
-        shape_of(windows[0].shape, jnp.float32),
-        [VMEM] * (3 + len(windows)),
-        VMEM,
+        (shape_of(windows[0].shape, jnp.float32), shape_of(fine.shape, jnp.float32), shape_of(coarse.shape, jnp.float32)),
+        [VMEM] * (7 + len(windows)),
+        (VMEM,) * 3,
         [pltpu.VMEM((partners, 3 * tiles, pixels, channels), jnp.bfloat16)],
         6,
-    )(gates, folded, other, *windows)
+        {5: 1, 6: 2},
+    )(gates, folded, other, pool, queries, fine, coarse, *windows)
 
 
 def near_kernel(tiles, half, partners, keep_ref, pool_ref, x_ref, other_ref, *refs):
@@ -348,8 +377,8 @@
             coarse_term = multiply(cells, queries_ref[j], (1, 0))
             fine = fine_term if fine is None else fine + fine_term
             coarse = coarse_term if coarse is None else coarse + coarse_term
-        fine_ref[s] = fine
-        coarse_ref[s] = coarse
+        fine_ref[tiles + s] = fine
+        coarse_ref[tiles + s] = coarse
 
 
 def near(partners, keep, pool, x, other, same):
@@ -359,8 +388,8 @@
         "near",
         (
             shape_of((partners, 2 * channels, tiles * pixels // 2)),
-            shape_of((tiles, pixels, tiles * pixels // 2), jnp.float32),
-            shape_of((tiles, PAD, tiles * pixels // 2), jnp.float32),
+            shape_of((3 * tiles, pixels, tiles * pixels // 2), jnp.float32),
+            shape_of((3 * tiles, PAD, tiles * pixels // 2), jnp.float32),
         ),
         [VMEM] * (4 + len(same)),
         (VMEM,) * 3,
@@ -369,80 +398,67 @@
     )(keep, pool, x, other, *same)
 
 
-def volume_kernel(tiles, half, partners, list_ref, queries_ref, near_fine, near_coarse, pool_ref, part_ref, *refs):
-    inputs, returned, rest = refs[: 4 * partners], refs[4 * partners : 5 * partners], refs[5 * partners :]
-    volume_hbm, grad_hbm, neighbours_ref, levels, cells, fine_table, coarse_table = rest[:7]
-    stage, volume_ref, grad_ref, sems = rest[7:]
-    (neighbours_copy,) = copies([list_ref], [neighbours_ref], sems)
+def volume_kernel(tiles, half, partners, list_ref, queries_ref, pool_ref, part_ref, near_fine, near_coarse, *refs):
+    inputs, returned, rest = refs[: 2 * partners], refs[2 * partners : 3 * partners], refs[3 * partners :]
+    volume_hbm, grad_hbm, fine_table, coarse_table, levels, stage, volume_ref, grad_ref, sems = rest
     first = lax.axis_index("tile") * tiles
-    pixels = grad_ref.shape[1]
+    listed = list_ref[...]
+    pixels, channels = grad_ref.shape[1:]
     for a in range(tiles):
-        total = part_ref[a]
+        summed = part_ref[a]
         for j in range(partners):
-            total = total + returned[j][a * pixels : (a + 1) * pixels].astype(jnp.float32)
-        grad_ref[a] = total
-    waits = [pltpu.make_async_copy(grad_ref, grad_hbm.at[0], sems.at[1])]
+            summed = summed + returned[j][a * pixels : (a + 1) * pixels].astype(jnp.float32)
+        grad_ref[a] = summed
+    waits = [pltpu.make_async_copy(grad_ref, grad_hbm.at[0], sems.at[0])]
     waits[0].start()
-    pool = pool_ref[...]
     for j in range(partners):
-        for part in range(2):
-            for a in range(tiles):
-                level = join(inputs[4 * j + part][a], inputs[4 * j + 2 + part][a])
-                at = part * tiles + a
-                levels[j, at * PIXELS : (at + 1) * PIXELS] = level
-                cells[j, at * PAD : (at + 1) * PAD] = jnp.dot(
-                    pool, level, preferred_element_type=jnp.float32
-                ).astype(jnp.bfloat16)
-    fine_table[tiles : 2 * tiles] = near_fine[...]
-    coarse_table[tiles : 2 * tiles] = near_coarse[...]
-    for keys_at, table in ((levels, fine_table), (cells, coarse_table)):
-        total = multiply(keys_at[0], queries_ref[0], (1, 0))
-        for j in range(1, partners):
-            total = total + multiply(keys_at[j], queries_ref[j], (1, 0))
-        total = total.reshape(2, tiles, table.shape[1], tiles * half)
         for part, base in enumerate(side_bases(tiles)):
-            table[pl.ds(base, tiles)] = total[part]
-    neighbours_copy.wait()
+            levels[j, pl.ds(base, tiles)] = inputs[2 * j + part][...]
+    _, other = halves(lax.axis_index("chan"), channels)
+    add_scores(tiles, partners, other, pool_ref[...], queries_ref, levels, fine_table, coarse_table, False)
     for i_part, (entries, start, size) in enumerate(entry_pairs(tiles)):
         for i, k in enumerate(entries):
             for a in range(tiles):
-                slot = relative(neighbours_ref, a, k, first) + a
+                slot = relative(listed, a, k, first) + a
                 lanes = slice(a * half, (a + 1) * half)
                 base = i * LEVELS * tiles + a
                 stage[pl.ds(base, PIXELS, stride=tiles), :] = fine_table[slot, :, lanes]
                 stage[pl.ds(base + PIXELS * tiles, COARSE, stride=tiles), :] = coarse_table[slot, :COARSE, lanes]
         rows = pl.ds(start, size)
         volume_ref[rows, :] = stage[:size].astype(jnp.bfloat16)
-        copy = pltpu.make_async_copy(volume_ref.at[rows], volume_hbm.at[rows], sems.at[2 + i_part])
+        copy = pltpu.make_async_copy(volume_ref.at[rows], volume_hbm.at[rows], sems.at[1 + i_part])
         copy.start()
         waits.append(copy)
     for copy in waits:
         copy.wait()
 
 
-def volumes(partners, neighbours, queries, near_fine, near_coarse, pool, grad, beside, returned):
+def volumes(partners, neighbours, queries, pool, grad, fine, coarse, beside, returned):
     tiles, pixels, channels = grad.shape
     half = pixels // 2
     rows = NEIGHBOURS * LEVELS * tiles
-    return call(
+    volume, feature_grad, _, _ = call(
         functools.partial(volume_kernel, tiles, half, partners),
         "volume",
-        (shape_of((rows, half)), shape_of((1,) + grad.shape, jnp.float32)),
+        (
+            shape_of((rows, half)),
+            shape_of((1,) + grad.shape, jnp.float32),
+            shape_of(fine.shape, jnp.float32),
+            shape_of(coarse.shape, jnp.float32),
+        ),
         [VMEM] * (6 + len(beside) + len(returned)),
-        (HBM, HBM),
+        (HBM, HBM, VMEM, VMEM),
         [
-            pltpu.SMEM(neighbours.shape, jnp.int32),
-            pltpu.VMEM((partners, 2 * tiles * PIXELS, 2 * channels), jnp.bfloat16),
-            pltpu.VMEM((partners, 2 * tiles * PAD, 2 * channels), jnp.bfloat16),
-            pltpu.VMEM((3 * tiles, PIXELS, tiles * half), jnp.float32),
-            pltpu.VMEM((3 * tiles, PAD, tiles * half), jnp.float32),
+            pltpu.VMEM((partners, 3 * tiles, pixels, channels), jnp.bfloat16),
             pltpu.VMEM((2 * LEVELS * tiles, half), jnp.float32),
             pltpu.VMEM((rows, half), jnp.bfloat16),
             pltpu.VMEM(grad.shape, jnp.float32),
-            pltpu.SemaphoreType.DMA((2 + (NEIGHBOURS + 1) // 2,)),
+            pltpu.SemaphoreType.DMA((1 + (NEIGHBOURS + 1) // 2,)),
         ],
-        12,
-    )(neighbours, queries, near_fine, near_coarse, pool, grad, *beside, *returned)
+        8,
+        {4: 2, 5: 3},
+    )(neighbours, queries, pool, grad, fine, coarse, *beside, *returned)
+    return volume, feature_grad
 
 
 def after(value, earlier):
@@ -467,7 +483,7 @@
     def over_cores(z):
         return lax.ppermute(z, "chan", swap)
 
-    upstream = jnp.transpose(cotangent[0], (2, 0, 1)).reshape(NEIGHBOURS * LEVELS * tiles, half)
+    upstream = jnp.transpose(cotangent[0], (2, 0, 1)).reshape(NEIGHBOURS, LEVELS * tiles // 8, 8, half)
     folded, x, gates, keep, pool, listed = fold(partners, neighbours, valid_tiles, pairing, upstream, features)
     other = over_cores(folded)
     arrived = [lax.ppermute(x, "frame", ahead) for ahead, _ in links]
@@ -481,18 +497,15 @@
     same = []
     for y in arrived:
         same += [after(y, sent[0]), after(over_cores(y), sent[0])]
-    queries, near_fine, near_coarse = near(partners, keep, pool, x, other, same)
+    queries, fine, coarse = near(partners, keep, pool, x, other, same)
     mine, exchanged = [], []
     for y, (even, odd) in zip(arrived, beside, strict=True):
-        even = after(even, near_fine)
-        odd = after(odd, even)
+        even, odd = after(even, fine), after(odd, fine)
         mine += [y, even, odd]
-        exchanged += [even, odd, over_cores(even), over_cores(odd)]
-    grad = sides(partners, gates, folded, other, mine)
+        exchanged += [over_cores(even), over_cores(odd)]
+    grad, fine, coarse = sides(partners, gates, folded, other, pool, queries, fine, coarse, mine)
     exchanged = [after(z, grad) for z in exchanged]
-    volume, feature_grad = volumes(
-        partners, listed, queries, near_fine, near_coarse, pool, grad, exchanged, returned
-    )
+    volume, feature_grad = volumes(partners, listed, queries, pool, grad, fine, coarse, exchanged, returned)
     volume = jnp.transpose(volume.reshape(NEIGHBOURS * LEVELS, tiles, half), (1, 2, 0))
     return volume[None], feature_grad
 

time: 20.1 us -> 19.8 us (0.985)
  waiting for transfers between devices: 3.79 us -> 3.53 us
    ppermute x4, waiting for transfers between devices: 0.42 us -> 0.08 us  [over_cores(): return lax.ppermute(z, 'chan', swap)]
    pallas_call x1, Pallas kernels: 0.61 us -> 0.93 us  [sides(): call(functools.partial(sides_kernel, tiles, pixels // 2, partners), 'side...]
  transfers between devices with their start and end apart: 10 -> 10, of which waited for: 6 -> 5; matrix products, arithmetic and copies ran while one was open for 0% -> 0% of each run, Pallas kernels for 9% -> 10%
where the time goes in v4:
time: 19.8 us; the launch traced here: 19.7 us
  starting transfers between devices  9.64 us (49%)
  Pallas kernels  5.85 us (30%)
  waiting for transfers between devices  3.53 us (18%)
  between operations  0.67 us (3%)
    ppermute x2, starting transfers between devices, over_even(): return lax.ppermute(z, 'tile', evens)  4.1 us
    ppermute x1, starting transfers between devices, local(): arrived = [lax.ppermute(x, 'frame', ahead) for ahead, _ in links]  2.56 us
    pallas_call x1, Pallas kernels, fold(): call(functools.partial(fold_kernel, tiles, half, partners), 'fold', (shap...  2.05 us
    pallas_call x1, Pallas kernels, volumes(): call(functools.partial(volume_kernel, tiles, half, partners), 'volume', (...  1.82 us
    ppermute x1, starting transfers between devices, local(): lax.ppermute(z, 'frame', back)  1.72 us
    ppermute x2, waiting for transfers between devices, over_even(): return lax.ppermute(z, 'tile', evens)  1.66 us
    ppermute x1, waiting for transfers between devices, local(): arrived = [lax.ppermute(x, 'frame', ahead) for ahead, _ in links]  1.33 us
    ppermute x4, starting transfers between devices, over_cores(): return lax.ppermute(z, 'chan', swap)  1.03 us
  transfers between devices with their start and end apart: 10, of which 5 were waited for; matrix products, arithmetic and copies ran while one was open for 0% of the time, Pallas kernels for 10%

profile of v4, /device:TPU:0, one launch (start us, length us, event | category | flops | bytes accessed | tf_op | source)
XLA Modules:
  0.0 19.7 jit_solution(9390302038357165859)
XLA Ops:
  0.6 2.1 %fold.1 = (bf16[2816,128]{1,0:T(8,128)(2,1)S(1)}, bf16[2,256,128]{2,1,0:T(8,128)(2,1)S(1)}, f32[1,8,128]{2,1,0:T(8,128)S(1)}, f32[1,256,128]{2,1,0:T(8,128)S(1)}...) custom-call(s32[2,9]{1,0:T(2,128)} %neighbours_hbm.1, s32[2,256]{1,0:T(2,128)} %valid_hbm.1, s32[1,2]{1,0:T(1,128)} %pairing_hbm.1, ...), custom_call_target="tpu_custom_call" | custom-call | tf_op jit(solution)/shard_map/fold/pallas_call | solution.py:194
  2.7 0.5 %collective-permute-start = (bf16[2816,128]{1,0:T(8,128)(2,1)S(1)}, bf16[2816,128]{1,0:T(8,128)(2,1)S(1)}, u32[]{:S(2)}, u32[]{:S(2)}) collective-permute-start(bf16[2816,128]{1,0:T(8,128)(2,1)S(1)} %get-tuple-element.31.mine_ref.folded_ref), channel_id=1, source_target_pairs={{0,1},{1,0},{2,3},{3,2},{4,5},{5,4},{6,7},{7,6},{8,9},{9,8},{10,11... | collective-permute-start | bytes 2162696 | tf_op jit(solution)/shard_map/ppermute | solution.py:484
  3.2 2.6 %collective-permute-start.1 = (bf16[2,256,128]{2,1,0:T(8,128)(2,1)S(1)}, bf16[2,256,128]{2,1,0:T(8,128)(2,1)S(1)}, u32[]{:S(2)}, u32[]{:S(2)}) collective-permute-start(bf16[2,256,128]{2,1,0:T(8,128)(2,1)S(1)} %get-tuple-element.30.x_ref), channel_id=1, source_target_pairs={{0,2},{2,0},{1,3},{3,1},{4,6},{6,4},{5,7},{7,5},{8,10},{10,8},{9,1... | collective-permute-start | bytes 393224 | tf_op jit(solution)/shard_map/ppermute | solution.py:489
  5.8 0.0 collective-permute-done.other_ref
  5.8 0.5 %keys.1 = (f32[2,256,128]{2,1,0:T(8,128)S(1)}, bf16[2,256,128]{2,1,0:T(8,128)(2,1)S(1)}, bf16[2,256,128]{2,1,0:T(8,128)(2,1)S(1)}) custom-call(bf16[2,256,128]{2,1,0:T(8,128)(2,1)S(1)} %get-tuple-element.30.x_ref, bf16[2816,128]{1,0:T(8,128)(2,1)S(1)} %get-tuple-element.31.mine_ref.folded_ref, bf16[2816,128]{1,0:T(8,128)(2,1)S(1)} %collective-permute-done.other_ref), custom_call_target="tpu_custom_call" | custom-call | tf_op jit(solution)/shard_map/keys/pallas_call | solution.py:250
  6.3 2.3 %collective-permute-start.2 = (bf16[2,256,128]{2,1,0:T(8,128)(2,1)S(1)}, bf16[2,256,128]{2,1,0:T(8,128)(2,1)S(1)}, u32[]{:S(2)}, u32[]{:S(2)}) collective-permute-start(bf16[2,256,128]{2,1,0:T(8,128)(2,1)S(1)} %get-tuple-element.35), channel_id=1, source_target_pairs={{0,4},{4,0},{8,12},{12,8},{1,5},{5,1},{9,13},{13,9},{2,6},{6,2},{1... | collective-permute-start | bytes 393224 | tf_op jit(solution)/shard_map/ppermute | solution.py:478
  8.5 0.0 collective-permute-start.3
  8.5 1.3 %collective-permute-done.1.refs_0_ = bf16[2,256,128]{2,1,0:T(8,128)(2,1)S(1)} collective-permute-done((bf16[2,256,128]{2,1,0:T(8,128)(2,1)S(1)}, bf16[2,256,128]{2,1,0:T(8,128)(2,1)S(1)}, u32[]{:S(2)}, u32[]{:S(2)}) %collective-permute-start.1) | collective-permute-done | bytes 131104 | tf_op jit(solution)/shard_map/ppermute | solution.py:489
  9.9 0.0 collective-permute-start.4
  9.9 1.8 %collective-permute-start.5 = (bf16[2,256,128]{2,1,0:T(8,128)(2,1)S(1)}, bf16[2,256,128]{2,1,0:T(8,128)(2,1)S(1)}, u32[]{:S(2)}, u32[]{:S(2)}) collective-permute-start(bf16[2,256,128]{2,1,0:T(8,128)(2,1)S(1)} %collective-permute-done.1.refs_0_), channel_id=1, source_target_pairs={{0,4},{4,0},{8,12},{12,8},{1,5},{5,1},{9,13},{13,9},{2,6},{6,2},{1... | collective-permute-start | bytes 393224 | tf_op jit(solution)/shard_map/ppermute | solution.py:478
  11.7 0.2 %collective-permute-start.6 = (bf16[2,256,128]{2,1,0:T(8,128)(2,1)S(1)}, bf16[2,256,128]{2,1,0:T(8,128)(2,1)S(1)}, u32[]{:S(2)}, u32[]{:S(2)}) collective-permute-start(bf16[2,256,128]{2,1,0:T(8,128)(2,1)S(1)} %collective-permute-done.1.refs_0_), channel_id=1, source_target_pairs={{4,8},{8,4},{5,9},{9,5},{0,1},{1,0},{12,13},{13,12},{6,10},{10,6},... | collective-permute-start | bytes 393224 | tf_op jit(solution)/shard_map/ppermute | solution.py:481
  11.9 0.4 %collective-permute-done.2.even_ref = bf16[2,256,128]{2,1,0:T(8,128)(2,1)S(1)} collective-permute-done((bf16[2,256,128]{2,1,0:T(8,128)(2,1)S(1)}, bf16[2,256,128]{2,1,0:T(8,128)(2,1)S(1)}, u32[]{:S(2)}, u32[]{:S(2)}) %collective-permute-start.2) | collective-permute-done | bytes 131104 | tf_op jit(solution)/shard_map/ppermute | solution.py:478
  12.3 0.0 collective-permute-done.3.odd_ref
  12.3 0.1 returns.1
  12.4 1.7 %collective-permute-start.9 = (bf16[528,128]{1,0:T(8,128)(2,1)S(1)}, bf16[528,128]{1,0:T(8,128)(2,1)S(1)}, u32[]{:S(2)}, u32[]{:S(2)}) collective-permute-start(bf16[528,128]{1,0:T(8,128)(2,1)S(1)} %returns.1), channel_id=1, source_target_pairs={{0,2},{2,0},{1,3},{3,1},{4,6},{6,4},{5,7},{7,5},{8,10},{10,8},{9,1... | collective-permute-start | bytes 405512 | tf_op jit(solution)/shard_map/ppermute | solution.py:496
  14.1 0.0 collective-permute-done.4.refs_1_
  14.1 0.5 %near.1 = (bf16[1,256,256]{2,1,0:T(8,128)(2,1)S(1)}, f32[6,256,256]{2,1,0:T(8,128)S(1)}, f32[6,128,256]{2,1,0:T(8,128)S(1)}) custom-call(f32[1,256,128]{2,1,0:T(8,128)S(1)} %get-tuple-element.28.keep_ref, bf16[128,256]{1,0:T(8,128)(2,1)S(1)} %get-tuple-element.29.pool_ref, bf16[2,256,128]{2,1,0:T(8,128)(2,1)S(1)} %get-tuple-element.30.x_ref, ...), custom_call_target="tpu_custom_call" | custom-call | tf_op jit(solution)/shard_map/near/pallas_call | solution.py:386
  14.6 1.3 %collective-permute-done.5.refs_1_ = bf16[2,256,128]{2,1,0:T(8,128)(2,1)S(1)} collective-permute-done((bf16[2,256,128]{2,1,0:T(8,128)(2,1)S(1)}, bf16[2,256,128]{2,1,0:T(8,128)(2,1)S(1)}, u32[]{:S(2)}, u32[]{:S(2)}) %collective-permute-start.5) | collective-permute-done | bytes 131104 | tf_op jit(solution)/shard_map/ppermute | solution.py:478
  15.9 0.0 collective-permute-start.7
  15.9 0.0 collective-permute-done.6.refs_2_
  15.9 0.5 %collective-permute-start.8 = (bf16[2,256,128]{2,1,0:T(8,128)(2,1)S(1)}, bf16[2,256,128]{2,1,0:T(8,128)(2,1)S(1)}, u32[]{:S(2)}, u32[]{:S(2)}) collective-permute-start(bf16[2,256,128]{2,1,0:T(8,128)(2,1)S(1)} %collective-permute-done.6.refs_2_), channel_id=1, source_target_pairs={{0,1},{1,0},{2,3},{3,2},{4,5},{5,4},{6,7},{7,6},{8,9},{9,8},{10,11... | collective-permute-start | bytes 393224 | tf_op jit(solution)/shard_map/ppermute | solution.py:484
  16.4 0.9 %sides.1 = (f32[2,256,128]{2,1,0:T(8,128)S(1)}, f32[6,256,256]{2,1,0:T(8,128)S(1)}, f32[6,128,256]{2,1,0:T(8,128)S(1)}) custom-call(f32[1,8,128]{2,1,0:T(8,128)S(1)} %get-tuple-element.34.gates_ref, bf16[2816,128]{1,0:T(8,128)(2,1)S(1)} %get-tuple-element.31.mine_ref.folded_ref, ...), custom_call_target="tpu_custom_call", output_to_operand_aliasing={{1}: (5, {}), {2}: (6, {})} | custom-call | tf_op jit(solution)/shard_map/sides/pallas_call | solution.py:351
  17.3 0.0 collective-permute-done.7.refs_0_
  17.3 0.1 collective-permute-done.8.refs_1_
  17.4 0.5 %collective-permute-done.9.refs_2_ = bf16[528,128]{1,0:T(8,128)(2,1)S(1)} collective-permute-done((bf16[528,128]{1,0:T(8,128)(2,1)S(1)}, bf16[528,128]{1,0:T(8,128)(2,1)S(1)}, u32[]{:S(2)}, u32[]{:S(2)}) %collective-permute-start.9) | collective-permute-done | bytes 135200 | tf_op jit(solution)/shard_map/ppermute | solution.py:496
  17.9 1.8 %volume.1 = (bf16[6120,128]{1,0:T(8,128)(2,1)}, f32[1,2,256,128]{3,2,1,0:T(8,128)}, f32[6,256,256]{2,1,0:T(8,128)S(1)}, f32[6,128,256]{2,1,0:T(8,128)S(1)}) custom-call(s32[2,9]{1,0:T(2,128)S(1)} %get-tuple-element.27.list_ref, bf16[1,256,256]{2,1,0:T(8,128)(2,1)S(1)} %get-tuple-element.40.queries_ref, ...), custom_call_target="tpu_custom_call", output_to_operand_aliasing={{2}: (4, {}), {3}: (5, {})} | custom-call | tf_op jit(solution)/shard_map/volume/pallas_call | solution.py:440
Async XLA Ops:
  2.7 3.1 %collective-permute-start = (bf16[2816,128]{1,0:T(8,128)(2,1)S(1)}, bf16[2816,128]{1,0:T(8,128)(2,1)S(1)}, u32[]{:S(2)}, u32[]{:S(2)}) collective-permute-start(bf16[2816,128]{1,0:T(8,128)(2,1)S(1)} %get-tuple-element.31.mine_ref.folded_ref), channel_id=1, source_target_pairs={{0,1},{1,0},{2,3},{3,2},{4,5},{5,4},{6,7},{7,6},{8,9},{9,8},{10,11... | collective-permute-start | bytes 2162696 | tf_op jit(solution)/shard_map/ppermute | solution.py:484
  3.2 6.7 %collective-permute-start.1 = (bf16[2,256,128]{2,1,0:T(8,128)(2,1)S(1)}, bf16[2,256,128]{2,1,0:T(8,128)(2,1)S(1)}, u32[]{:S(2)}, u32[]{:S(2)}) collective-permute-start(bf16[2,256,128]{2,1,0:T(8,128)(2,1)S(1)} %get-tuple-element.30.x_ref), channel_id=1, source_target_pairs={{0,2},{2,0},{1,3},{3,1},{4,6},{6,4},{5,7},{7,5},{8,10},{10,8},{9,1... | collective-permute-start | bytes 393224 | tf_op jit(solution)/shard_map/ppermute | solution.py:489
  6.3 6.1 %collective-permute-start.2 = (bf16[2,256,128]{2,1,0:T(8,128)(2,1)S(1)}, bf16[2,256,128]{2,1,0:T(8,128)(2,1)S(1)}, u32[]{:S(2)}, u32[]{:S(2)}) collective-permute-start(bf16[2,256,128]{2,1,0:T(8,128)(2,1)S(1)} %get-tuple-element.35), channel_id=1, source_target_pairs={{0,4},{4,0},{8,12},{12,8},{1,5},{5,1},{9,13},{13,9},{2,6},{6,2},{1... | collective-permute-start | bytes 393224 | tf_op jit(solution)/shard_map/ppermute | solution.py:478
  8.5 3.8 %collective-permute-start.3 = (bf16[2,256,128]{2,1,0:T(8,128)(2,1)S(1)}, bf16[2,256,128]{2,1,0:T(8,128)(2,1)S(1)}, u32[]{:S(2)}, u32[]{:S(2)}) collective-permute-start(bf16[2,256,128]{2,1,0:T(8,128)(2,1)S(1)} %get-tuple-element.36), channel_id=1, source_target_pairs={{4,8},{8,4},{5,9},{9,5},{0,1},{1,0},{12,13},{13,12},{6,10},{10,6},... | collective-permute-start | bytes 393224 | tf_op jit(solution)/shard_map/ppermute | solution.py:481
  9.9 4.3 %collective-permute-start.4 = (bf16[2,256,128]{2,1,0:T(8,128)(2,1)S(1)}, bf16[2,256,128]{2,1,0:T(8,128)(2,1)S(1)}, u32[]{:S(2)}, u32[]{:S(2)}) collective-permute-start(bf16[2,256,128]{2,1,0:T(8,128)(2,1)S(1)} %collective-permute-done.1.refs_0_), channel_id=1, source_target_pairs={{0,1},{1,0},{2,3},{3,2},{4,5},{5,4},{6,7},{7,6},{8,9},{9,8},{10,11... | collective-permute-start | bytes 393224 | tf_op jit(solution)/shard_map/ppermute | solution.py:484
  9.9 6.0 %collective-permute-start.5 = (bf16[2,256,128]{2,1,0:T(8,128)(2,1)S(1)}, bf16[2,256,128]{2,1,0:T(8,128)(2,1)S(1)}, u32[]{:S(2)}, u32[]{:S(2)}) collective-permute-start(bf16[2,256,128]{2,1,0:T(8,128)(2,1)S(1)} %collective-permute-done.1.refs_0_), channel_id=1, source_target_pairs={{0,4},{4,0},{8,12},{12,8},{1,5},{5,1},{9,13},{13,9},{2,6},{6,2},{1... | collective-permute-start | bytes 393224 | tf_op jit(solution)/shard_map/ppermute | solution.py:478
  11.7 4.2 %collective-permute-start.6 = (bf16[2,256,128]{2,1,0:T(8,128)(2,1)S(1)}, bf16[2,256,128]{2,1,0:T(8,128)(2,1)S(1)}, u32[]{:S(2)}, u32[]{:S(2)}) collective-permute-start(bf16[2,256,128]{2,1,0:T(8,128)(2,1)S(1)} %collective-permute-done.1.refs_0_), channel_id=1, source_target_pairs={{4,8},{8,4},{5,9},{9,5},{0,1},{1,0},{12,13},{13,12},{6,10},{10,6},... | collective-permute-start | bytes 393224 | tf_op jit(solution)/shard_map/ppermute | solution.py:481
  12.4 5.4 %collective-permute-start.9 = (bf16[528,128]{1,0:T(8,128)(2,1)S(1)}, bf16[528,128]{1,0:T(8,128)(2,1)S(1)}, u32[]{:S(2)}, u32[]{:S(2)}) collective-permute-start(bf16[528,128]{1,0:T(8,128)(2,1)S(1)} %returns.1), channel_id=1, source_target_pairs={{0,2},{2,0},{1,3},{3,1},{4,6},{6,4},{5,7},{7,5},{8,10},{10,8},{9,1... | collective-permute-start | bytes 405512 | tf_op jit(solution)/shard_map/ppermute | solution.py:496
  15.9 1.5 %collective-permute-start.7 = (bf16[2,256,128]{2,1,0:T(8,128)(2,1)S(1)}, bf16[2,256,128]{2,1,0:T(8,128)(2,1)S(1)}, u32[]{:S(2)}, u32[]{:S(2)}) collective-permute-start(bf16[2,256,128]{2,1,0:T(8,128)(2,1)S(1)} %collective-permute-done.5.refs_1_), channel_id=1, source_target_pairs={{0,1},{1,0},{2,3},{3,2},{4,5},{5,4},{6,7},{7,6},{8,9},{9,8},{10,11... | collective-permute-start | bytes 393224 | tf_op jit(solution)/shard_map/ppermute | solution.py:484
  15.9 1.5 %collective-permute-start.8 = (bf16[2,256,128]{2,1,0:T(8,128)(2,1)S(1)}, bf16[2,256,128]{2,1,0:T(8,128)(2,1)S(1)}, u32[]{:S(2)}, u32[]{:S(2)}) collective-permute-start(bf16[2,256,128]{2,1,0:T(8,128)(2,1)S(1)} %collective-permute-done.6.refs_2_), channel_id=1, source_target_pairs={{0,1},{1,0},{2,3},{3,2},{4,5},{5,4},{6,7},{7,6},{8,9},{9,8},{10,11... | collective-permute-start | bytes 393224 | tf_op jit(solution)/shard_map/ppermute | solution.py:484

commit v5 on v4

--- a/solution.py
+++ b/solution.py
@@ -223,18 +223,42 @@
     return here, there
 
 
-def keys_kernel(tiles, half, x_ref, mine_ref, other_ref, own_ref, even_ref, odd_ref):
-    here, there = halves(lax.axis_index("chan"), half)
-    queries = [jnp.concatenate([x_ref[a, here, :], x_ref[a, there, :]], axis=0) for a in range(tiles)]
+def window_grad(tiles, slot, queries, folded_ref):
+    users = [a for a in range(tiles) if 0 <= slot - a < SPAN]
+    blocks = [folded_ref[fold_rows(a, slot - a)] for a in users]
+    return jnp.dot(
+        jnp.concatenate(blocks, axis=1),
+        jnp.concatenate([queries[a] for a in users], axis=0),
+        preferred_element_type=jnp.float32,
+    )
+
+
+def early_kernel(tiles, half, x_ref, mine_ref, part_ref):
+    here, _ = halves(lax.axis_index("chan"), half)
+    queries = [x_ref[a, here, :] for a in range(tiles)]
+    for slot in range(3 * tiles):
+        part_ref[slot] = window_grad(tiles, slot, queries, mine_ref)
+
+
+def early(x, mine):
+    tiles, pixels, channels = x.shape
+    return call(
+        functools.partial(early_kernel, tiles, mine.shape[1]),
+        "early",
+        shape_of((3 * tiles, pixels, channels), jnp.float32),
+        [VMEM] * 2,
+        VMEM,
+        [],
+        4,
+    )(x, mine)
+
+
+def keys_kernel(tiles, half, x_ref, part_ref, other_ref, own_ref, even_ref, odd_ref):
+    _, there = halves(lax.axis_index("chan"), half)
+    queries = [x_ref[a, there, :] for a in range(tiles)]
 
     def of_slot(slot):
-        users = [a for a in range(tiles) if 0 <= slot - a < SPAN]
-        blocks = [ref[fold_rows(a, slot - a)] for a in users for ref in (mine_ref, other_ref)]
-        return jnp.dot(
-            jnp.concatenate(blocks, axis=1),
-            jnp.concatenate([queries[a] for a in users], axis=0),
-            preferred_element_type=jnp.float32,
-        )
+        return part_ref[slot] + window_grad(tiles, slot, queries, other_ref)
 
     parity = lax.rem(lax.axis_index("tile"), 2)
     for a in range(tiles):
@@ -245,8 +269,8 @@
         own_ref[a] = of_slot(tiles + a)
 
 
-def keys(x, mine, other):
-    tiles, half = x.shape[0], mine.shape[1]
+def keys(x, part, other):
+    tiles, half = x.shape[0], other.shape[1]
     return call(
         functools.partial(keys_kernel, tiles, half),
         "keys",
@@ -255,7 +279,7 @@
         (VMEM,) * 3,
         [],
         4,
-    )(x, mine, other)
+    )(x, part, other)
 
 
 def returns_kernel(partners, gates_ref, own_ref, even_ref, odd_ref, *out_refs):
@@ -296,78 +320,84 @@
     return lax.dot_general(left, right, ((contract[:1], contract[1:]), ((), ())), preferred_element_type=jnp.float32)
 
 
-def window_slots(tiles):
-    even, odd = side_bases(tiles)
-    return tiles, even, odd
-
-
-def beside_groups(tiles):
-    return slice(0, tiles), slice(2 * tiles, 3 * tiles)
-
-
-def add_scores(tiles, partners, channels, pool, queries_ref, levels, fine_ref, coarse_ref, first):
-    for group in beside_groups(tiles):
-        fine, coarse = None, None
-        for j in range(partners):
-            queries = queries_ref[j, channels, :]
-            level = levels[j, group]
-            width = level.shape[2]
-            cells = [jnp.dot(pool, level[a], preferred_element_type=jnp.float32) for a in range(tiles)]
-            cells = jnp.concatenate(cells, axis=0).astype(jnp.bfloat16)
-            fine_term = multiply(level.reshape(tiles * PIXELS, width), queries, (1, 0))
-            coarse_term = multiply(cells, queries, (1, 0))
-            fine = fine_term if fine is None else fine + fine_term
-            coarse = coarse_term if coarse is None else coarse + coarse_term
-        fine = fine.reshape(tiles, PIXELS, fine.shape[1])
-        coarse = coarse.reshape(tiles, PAD, coarse.shape[1])
-        fine_ref[group] = fine if first else fine_ref[group] + fine
-        coarse_ref[group] = coarse if first else coarse_ref[group] + coarse
-
-
-def sides_kernel(tiles, half, partners, gates_ref, folded_ref, other_ref, pool_ref, queries_ref, near_fine, near_coarse, *refs):
-    inputs, (grad_ref, fine_ref, coarse_ref, levels) = refs[: 3 * partners], refs[3 * partners :]
-    here, there = halves(lax.axis_index("chan"), half)
-    for j in range(partners):
-        for part, base in enumerate(window_slots(tiles)):
-            levels[j, pl.ds(base, tiles)] = inputs[3 * j + part][...]
+def query_grads(gates_ref, folded_ref, other_ref, tiles, partners, level_of, slots):
+    grads = []
     for a in range(tiles):
         grad = None
         for j in range(partners):
             term = None
-            for w in range(SPAN):
-                both = jnp.concatenate([folded_ref[fold_rows(a, w)], other_ref[fold_rows(a, w)]], axis=1)
-                part = multiply(both, levels[j, a + w], (0, 0))
-                term = part if term is None else term + part
+            for slot in slots:
+                if 0 <= slot - a < SPAN:
+                    rows = fold_rows(a, slot - a)
+                    both = jnp.concatenate([folded_ref[rows], other_ref[rows]], axis=1)
+                    part = multiply(both, level_of(j, slot), (0, 0))
+                    term = part if term is None else term + part
             term = term * gates_ref[j, :1]
             grad = term if grad is None else grad + term
-        grad_ref[a, here, :] = grad[:half]
-        grad_ref[a, there, :] = grad[half:]
-    mine, _ = halves(lax.axis_index("chan"), grad_ref.shape[2])
-    add_scores(tiles, partners, mine, pool_ref[...], queries_ref, levels, fine_ref, coarse_ref, True)
-
-
-def sides(partners, gates, folded, other, pool, queries, fine, coarse, windows):
-    tiles, pixels, channels = windows[0].shape
-    return call(
-        functools.partial(sides_kernel, tiles, pixels // 2, partners),
-        "sides",
-        (shape_of(windows[0].shape, jnp.float32), shape_of(fine.shape, jnp.float32), shape_of(coarse.shape, jnp.float32)),
-        [VMEM] * (7 + len(windows)),
-        (VMEM,) * 3,
-        [pltpu.VMEM((partners, 3 * tiles, pixels, channels), jnp.bfloat16)],
-        6,
-        {5: 1, 6: 2},
-    )(gates, folded, other, pool, queries, fine, coarse, *windows)
-
-
-def near_kernel(tiles, half, partners, keep_ref, pool_ref, x_ref, other_ref, *refs):
-    same, (queries_ref, fine_ref, coarse_ref) = refs[: 2 * partners], refs[2 * partners :]
+        grads.append(grad)
+    return grads
+
+
+def ready_kernel(tiles, half, partners, gates_ref, keep_ref, x_ref, folded_ref, other_ref, *refs):
+    same, (queries_ref, grad_ref) = refs[:partners], refs[partners:]
     here, _ = halves(lax.axis_index("chan"), half)
     mine = jnp.concatenate([x_ref[a, here, :] for a in range(tiles)], axis=0).astype(jnp.float32)
     other = jnp.concatenate([other_ref[query_rows(tiles, half, a)] for a in range(tiles)], axis=0).astype(jnp.float32)
-    pool = pool_ref[...]
     for j in range(partners):
         queries_ref[j] = join(mine * keep_ref[j], other * keep_ref[j]).T.astype(jnp.bfloat16)
+    slots = range(tiles, 2 * tiles)
+    grads = query_grads(
+        gates_ref, folded_ref, other_ref, tiles, partners, lambda j, slot: same[j][slot - tiles], slots
+    )
+    for a in range(tiles):
+        grad_ref[a] = grads[a]
+
+
+def ready(partners, gates, keep, x, folded, other, same):
+    tiles, pixels, channels = x.shape
+    return call(
+        functools.partial(ready_kernel, tiles, pixels // 2, partners),
+        "ready",
+        (shape_of((partners, 2 * channels, tiles * pixels // 2)), shape_of(x.shape, jnp.float32)),
+        [VMEM] * (5 + len(same)),
+        (VMEM,) * 2,
+        [],
+        6,
+    )(gates, keep, x, folded, other, *same)
+
+
+def sides_kernel(tiles, half, partners, gates_ref, folded_ref, other_ref, part_ref, *refs):
+    inputs, (grad_ref, levels) = refs[: 2 * partners], refs[2 * partners :]
+    here, there = halves(lax.axis_index("chan"), half)
+    for j in range(partners):
+        for part, base in enumerate(side_bases(tiles)):
+            levels[j, pl.ds(base, tiles)] = inputs[2 * j + part][...]
+    slots = [slot for slot in range(3 * tiles) if not tiles <= slot < 2 * tiles]
+    grads = query_grads(
+        gates_ref, folded_ref, other_ref, tiles, partners, lambda j, slot: levels[j, slot], slots
+    )
+    for a in range(tiles):
+        grad = part_ref[a] + grads[a]
+        grad_ref[a, here, :] = grad[:half]
+        grad_ref[a, there, :] = grad[half:]
+
+
+def sides(partners, gates, folded, other, part, windows):
+    tiles, pixels, channels = windows[0].shape
+    return call(
+        functools.partial(sides_kernel, tiles, pixels // 2, partners),
+        "sides",
+        shape_of(windows[0].shape, jnp.float32),
+        [VMEM] * (4 + len(windows)),
+        VMEM,
+        [pltpu.VMEM((partners, 3 * tiles, pixels, channels), jnp.bfloat16)],
+        6,
+    )(gates, folded, other, part, *windows)
+
+
+def near_kernel(tiles, partners, queries_ref, pool_ref, *refs):
+    same, (fine_ref, coarse_ref) = refs[: 2 * partners], refs[2 * partners :]
+    pool = pool_ref[...]
     for s in range(tiles):
         fine, coarse = None, None
         for j in range(partners):
@@ -381,26 +411,62 @@
         coarse_ref[tiles + s] = coarse
 
 
-def near(partners, keep, pool, x, other, same):
-    tiles, pixels, channels = x.shape
-    return call(
-        functools.partial(near_kernel, tiles, pixels // 2, partners),
+def near(partners, queries, pool, same):
+    tiles, pixels, _ = same[0].shape
+    return call(
+        functools.partial(near_kernel, tiles, partners),
         "near",
         (
-            shape_of((partners, 2 * channels, tiles * pixels // 2)),
             shape_of((3 * tiles, pixels, tiles * pixels // 2), jnp.float32),
             shape_of((3 * tiles, PAD, tiles * pixels // 2), jnp.float32),
         ),
-        [VMEM] * (4 + len(same)),
-        (VMEM,) * 3,
+        [VMEM] * (2 + len(same)),
+        (VMEM,) * 2,
         [],
         6,
-    )(keep, pool, x, other, *same)
-
-
-def volume_kernel(tiles, half, partners, list_ref, queries_ref, pool_ref, part_ref, near_fine, near_coarse, *refs):
-    inputs, returned, rest = refs[: 2 * partners], refs[2 * partners : 3 * partners], refs[3 * partners :]
-    volume_hbm, grad_hbm, fine_table, coarse_table, levels, stage, volume_ref, grad_ref, sems = rest
+    )(queries, pool, *same)
+
+
+def tables_kernel(tiles, partners, queries_ref, pool_ref, near_fine, near_coarse, *refs):
+    inputs, (fine_table, coarse_table, levels, cells) = refs[: 4 * partners], refs[4 * partners :]
+    pool = pool_ref[...]
+    for j in range(partners):
+        for part in range(2):
+            for a in range(tiles):
+                level = join(inputs[4 * j + part][a], inputs[4 * j + 2 + part][a])
+                at = part * tiles + a
+                levels[j, at * PIXELS : (at + 1) * PIXELS] = level
+                cells[j, at * PAD : (at + 1) * PAD] = jnp.dot(
+                    pool, level, preferred_element_type=jnp.float32
+                ).astype(jnp.bfloat16)
+    for keys_at, table in ((levels, fine_table), (cells, coarse_table)):
+        scores = multiply(keys_at[0], queries_ref[0], (1, 0))
+        for j in range(1, partners):
+            scores = scores + multiply(keys_at[j], queries_ref[j], (1, 0))
+        scores = scores.reshape(2, tiles, table.shape[1], table.shape[2])
+        for part, base in enumerate(side_bases(tiles)):
+            table[pl.ds(base, tiles)] = scores[part]
+
+
+def tables(partners, queries, pool, fine, coarse, beside):
+    tiles, pixels, channels = beside[0].shape
+    return call(
+        functools.partial(tables_kernel, tiles, partners),
+        "tables",
+        (shape_of(fine.shape, jnp.float32), shape_of(coarse.shape, jnp.float32)),
+        [VMEM] * (4 + len(beside)),
+        (VMEM,) * 2,
+        [
+            pltpu.VMEM((partners, 2 * tiles * pixels, 2 * channels), jnp.bfloat16),
+            pltpu.VMEM((partners, 2 * tiles * PAD, 2 * channels), jnp.bfloat16),
+        ],
+        6,
+        {2: 0, 3: 1},
+    )(queries, pool, fine, coarse, *beside)
+
+
+def volume_kernel(tiles, half, partners, list_ref, part_ref, fine_table, coarse_table, *refs):
+    returned, (volume_hbm, grad_hbm, stage, volume_ref, grad_ref, sems) = refs[:partners], refs[partners:]
     first = lax.axis_index("tile") * tiles
     listed = list_ref[...]
     pixels, channels = grad_ref.shape[1:]
@@ -411,11 +477,6 @@
         grad_ref[a] = summed
     waits = [pltpu.make_async_copy(grad_ref, grad_hbm.at[0], sems.at[0])]
     waits[0].start()
-    for j in range(partners):
-        for part, base in enumerate(side_bases(tiles)):
-            levels[j, pl.ds(base, tiles)] = inputs[2 * j + part][...]
-    _, other = halves(lax.axis_index("chan"), channels)
-    add_scores(tiles, partners, other, pool_ref[...], queries_ref, levels, fine_table, coarse_table, False)
     for i_part, (entries, start, size) in enumerate(entry_pairs(tiles)):
         for i, k in enumerate(entries):
             for a in range(tiles):
@@ -433,32 +494,24 @@
         copy.wait()
 
 
-def volumes(partners, neighbours, queries, pool, grad, fine, coarse, beside, returned):
-    tiles, pixels, channels = grad.shape
+def volumes(partners, neighbours, grad, fine, coarse, returned):
+    tiles, pixels, _ = grad.shape
     half = pixels // 2
     rows = NEIGHBOURS * LEVELS * tiles
-    volume, feature_grad, _, _ = call(
+    return call(
         functools.partial(volume_kernel, tiles, half, partners),
         "volume",
-        (
-            shape_of((rows, half)),
-            shape_of((1,) + grad.shape, jnp.float32),
-            shape_of(fine.shape, jnp.float32),
-            shape_of(coarse.shape, jnp.float32),
-        ),
-        [VMEM] * (6 + len(beside) + len(returned)),
-        (HBM, HBM, VMEM, VMEM),
+        (shape_of((rows, half)), shape_of((1,) + grad.shape, jnp.float32)),
+        [VMEM] * (4 + len(returned)),
+        (HBM, HBM),
         [
-            pltpu.VMEM((partners, 3 * tiles, pixels, channels), jnp.bfloat16),
             pltpu.VMEM((2 * LEVELS * tiles, half), jnp.float32),
             pltpu.VMEM((rows, half), jnp.bfloat16),
             pltpu.VMEM(grad.shape, jnp.float32),
             pltpu.SemaphoreType.DMA((1 + (NEIGHBOURS + 1) // 2,)),
         ],
         8,
-        {4: 2, 5: 3},
-    )(neighbours, queries, pool, grad, fine, coarse, *beside, *returned)
-    return volume, feature_grad
+    )(neighbours, grad, fine, coarse, *returned)
 
 
 def after(value, earlier):
@@ -487,25 +540,26 @@
     folded, x, gates, keep, pool, listed = fold(partners, neighbours, valid_tiles, pairing, upstream, features)
     other = over_cores(folded)
     arrived = [lax.ppermute(x, "frame", ahead) for ahead, _ in links]
-    own, to_even, to_odd = keys(x, folded, other)
+    own, to_even, to_odd = keys(x, early(x, folded), other)
     arrived = [after(y, own) for y in arrived]
     beside = [(over_even(y), over_odd(y)) for y in arrived]
     from_odd = over_odd(to_odd)
     from_even = after(over_even(to_even), from_odd)
     sent = returns(partners, gates, own, from_even, from_odd)
     returned = [lax.ppermute(z, "frame", back) for z, (_, back) in zip(sent, links, strict=True)]
-    same = []
-    for y in arrived:
-        same += [after(y, sent[0]), after(over_cores(y), sent[0])]
-    queries, fine, coarse = near(partners, keep, pool, x, other, same)
-    mine, exchanged = [], []
+    queries, part = ready(partners, gates, keep, x, folded, other, [after(y, sent[0]) for y in arrived])
+    same, mine, exchanged = [], [], []
     for y, (even, odd) in zip(arrived, beside, strict=True):
-        even, odd = after(even, fine), after(odd, fine)
-        mine += [y, even, odd]
-        exchanged += [over_cores(even), over_cores(odd)]
-    grad, fine, coarse = sides(partners, gates, folded, other, pool, queries, fine, coarse, mine)
-    exchanged = [after(z, grad) for z in exchanged]
-    volume, feature_grad = volumes(partners, listed, queries, pool, grad, fine, coarse, exchanged, returned)
+        even, odd = after(even, part), after(odd, part)
+        same += [after(y, odd), after(over_cores(y), odd)]
+        mine += [even, odd]
+        exchanged += [even, odd, over_cores(even), over_cores(odd)]
+    grad = sides(partners, gates, folded, other, part, mine)
+    fine, coarse = near(partners, queries, pool, [after(z, grad) for z in same])
+    exchanged = [after(after(z, grad), fine) for z in exchanged]
+    fine, coarse = tables(partners, queries, pool, fine, coarse, exchanged)
+    returned = [after(z, fine) for z in returned]
+    volume, feature_grad = volumes(partners, listed, grad, fine, coarse, returned)
     volume = jnp.transpose(volume.reshape(NEIGHBOURS * LEVELS, tiles, half), (1, 2, 0))
     return volume[None], feature_grad
 

time: 19.8 us -> 19.6 us (0.990)
  starting transfers between devices: 9.64 us -> 9.09 us
  Pallas kernels: 5.85 us -> 6.09 us
    pallas_call x1 -> x4, Pallas kernels: 0.47 us -> 1.6 us  [the longest x1 0.47 us: near(): call(functools.partial(near_kernel, tiles, partners), 'near', (shape_of((...]
    pallas_call x1, Pallas kernels: 0.93 us -> 0.48 us  [sides(): call(functools.partial(sides_kernel, tiles, pixels // 2, partners), 'side...]
    ppermute x2, waiting for transfers between devices: 1.66 us -> 1.24 us  [over_even(): return lax.ppermute(z, 'tile', evens)]
    ppermute x2, starting transfers between devices: 4.1 us -> 3.77 us  [over_even(): return lax.ppermute(z, 'tile', evens)]
    ppermute x1, waiting for transfers between devices: 0.46 us -> 0.75 us  [local(): lax.ppermute(z, 'frame', back)]
    pallas_call x1, Pallas kernels: 1.82 us -> 1.55 us  [volumes(): call(functools.partial(volume_kernel, tiles, half, partners), 'volume', (...]
    ppermute x2, starting transfers between devices: 0.23 us -> 0.01 us  [over_odd(): return lax.ppermute(z, ('tile', 'chan'), odds)]
  transfers between devices with their start and end apart: 10 -> 10, of which waited for: 5 -> 4; matrix products, arithmetic and copies ran while one was open for 0% -> 0% of each run, Pallas kernels for 10% -> 13%
where the time goes in v5:
time: 19.6 us; the launch traced here: 19.4 us
  starting transfers between devices  9.09 us (46%)
  Pallas kernels  6.09 us (31%)
  waiting for transfers between devices  3.53 us (18%)
  between operations  0.71 us (4%)
    ppermute x2, starting transfers between devices, over_even(): return lax.ppermute(z, 'tile', evens)  3.77 us
    ppermute x1, starting transfers between devices, local(): arrived = [lax.ppermute(x, 'frame', ahead) for ahead, _ in links]  2.56 us
    pallas_call x1, Pallas kernels, fold(): call(functools.partial(fold_kernel, tiles, half, partners), 'fold', (shap...  2.05 us
    ppermute x1, starting transfers between devices, local(): lax.ppermute(z, 'frame', back)  1.72 us
    pallas_call x1, Pallas kernels, volumes(): call(functools.partial(volume_kernel, tiles, half, partners), 'volume', (...  1.55 us
    ppermute x1, waiting for transfers between devices, local(): arrived = [lax.ppermute(x, 'frame', ahead) for ahead, _ in links]  1.48 us
    ppermute x2, waiting for transfers between devices, over_even(): return lax.ppermute(z, 'tile', evens)  1.24 us
    ppermute x4, starting transfers between devices, over_cores(): return lax.ppermute(z, 'chan', swap)  1.03 us
  transfers between devices with their start and end apart: 10, of which 4 were waited for; matrix products, arithmetic and copies ran while one was open for 0% of the time, Pallas kernels for 13%

profile of v5, /device:TPU:0, one launch (start us, length us, event | category | flops | bytes accessed | tf_op | source)
XLA Modules:
  0.0 19.4 jit_solution(12062133280806797118)
XLA Ops:
  0.6 2.1 %fold.1 = (bf16[2816,128]{1,0:T(8,128)(2,1)S(1)}, bf16[2,256,128]{2,1,0:T(8,128)(2,1)S(1)}, f32[1,8,128]{2,1,0:T(8,128)S(1)}, f32[1,256,128]{2,1,0:T(8,128)S(1)}...) custom-call(s32[2,9]{1,0:T(2,128)} %neighbours_hbm.1, s32[2,256]{1,0:T(2,128)} %valid_hbm.1, s32[1,2]{1,0:T(1,128)} %pairing_hbm.1, ...), custom_call_target="tpu_custom_call" | custom-call | tf_op jit(solution)/shard_map/fold/pallas_call | solution.py:194
  2.7 0.5 %collective-permute-start = (bf16[2816,128]{1,0:T(8,128)(2,1)S(1)}, bf16[2816,128]{1,0:T(8,128)(2,1)S(1)}, u32[]{:S(2)}, u32[]{:S(2)}) collective-permute-start(bf16[2816,128]{1,0:T(8,128)(2,1)S(1)} %get-tuple-element.39.mine_ref.folded_ref), channel_id=1, source_target_pairs={{0,1},{1,0},{2,3},{3,2},{4,5},{5,4},{6,7},{7,6},{8,9},{9,8},{10,11... | collective-permute-start | bytes 2162696 | tf_op jit(solution)/shard_map/ppermute | solution.py:537
  3.2 2.6 %collective-permute-start.1 = (bf16[2,256,128]{2,1,0:T(8,128)(2,1)S(1)}, bf16[2,256,128]{2,1,0:T(8,128)(2,1)S(1)}, u32[]{:S(2)}, u32[]{:S(2)}) collective-permute-start(bf16[2,256,128]{2,1,0:T(8,128)(2,1)S(1)} %get-tuple-element.41.x_ref), channel_id=1, source_target_pairs={{0,2},{2,0},{1,3},{3,1},{4,6},{6,4},{5,7},{7,5},{8,10},{10,8},{9,1... | collective-permute-start | bytes 393224 | tf_op jit(solution)/shard_map/ppermute | solution.py:542
  5.8 0.3 %early.1.part_ref = f32[6,256,128]{2,1,0:T(8,128)S(1)} custom-call(bf16[2,256,128]{2,1,0:T(8,128)(2,1)S(1)} %get-tuple-element.41.x_ref, bf16[2816,128]{1,0:T(8,128)(2,1)S(1)} %get-tuple-element.39.mine_ref.folded_ref), custom_call_target="tpu_custom_call" | custom-call | tf_op jit(solution)/shard_map/early/pallas_call | solution.py:245
  6.1 0.0 collective-permute-done.other_ref
  6.1 0.3 %keys.1 = (f32[2,256,128]{2,1,0:T(8,128)S(1)}, bf16[2,256,128]{2,1,0:T(8,128)(2,1)S(1)}, bf16[2,256,128]{2,1,0:T(8,128)(2,1)S(1)}) custom-call(bf16[2,256,128]{2,1,0:T(8,128)(2,1)S(1)} %get-tuple-element.41.x_ref, f32[6,256,128]{2,1,0:T(8,128)S(1)} %early.1.part_ref, bf16[2816,128]{1,0:T(8,128)(2,1)S(1)} %collective-permute-done.other_ref), custom_call_target="tpu_custom_call" | custom-call | tf_op jit(solution)/shard_map/keys/pallas_call | solution.py:274
  6.5 1.9 %collective-permute-start.2 = (bf16[2,256,128]{2,1,0:T(8,128)(2,1)S(1)}, bf16[2,256,128]{2,1,0:T(8,128)(2,1)S(1)}, u32[]{:S(2)}, u32[]{:S(2)}) collective-permute-start(bf16[2,256,128]{2,1,0:T(8,128)(2,1)S(1)} %get-tuple-element.44), channel_id=1, source_target_pairs={{0,4},{4,0},{8,12},{12,8},{1,5},{5,1},{9,13},{13,9},{2,6},{6,2},{1... | collective-permute-start | bytes 393224 | tf_op jit(solution)/shard_map/ppermute | solution.py:531
  8.4 0.0 collective-permute-start.3
  8.4 1.5 %collective-permute-done.1.refs_0_ = bf16[2,256,128]{2,1,0:T(8,128)(2,1)S(1)} collective-permute-done((bf16[2,256,128]{2,1,0:T(8,128)(2,1)S(1)}, bf16[2,256,128]{2,1,0:T(8,128)(2,1)S(1)}, u32[]{:S(2)}, u32[]{:S(2)}) %collective-permute-start.1) | collective-permute-done | bytes 131104 | tf_op jit(solution)/shard_map/ppermute | solution.py:542
  9.9 1.8 %collective-permute-start.4 = (bf16[2,256,128]{2,1,0:T(8,128)(2,1)S(1)}, bf16[2,256,128]{2,1,0:T(8,128)(2,1)S(1)}, u32[]{:S(2)}, u32[]{:S(2)}) collective-permute-start(bf16[2,256,128]{2,1,0:T(8,128)(2,1)S(1)} %collective-permute-done.1.refs_0_), channel_id=1, source_target_pairs={{0,4},{4,0},{8,12},{12,8},{1,5},{5,1},{9,13},{13,9},{2,6},{6,2},{1... | collective-permute-start | bytes 393224 | tf_op jit(solution)/shard_map/ppermute | solution.py:531
  11.7 0.0 collective-permute-start.5
  11.7 0.5 %collective-permute-done.2.even_ref = bf16[2,256,128]{2,1,0:T(8,128)(2,1)S(1)} collective-permute-done((bf16[2,256,128]{2,1,0:T(8,128)(2,1)S(1)}, bf16[2,256,128]{2,1,0:T(8,128)(2,1)S(1)}, u32[]{:S(2)}, u32[]{:S(2)}) %collective-permute-start.2) | collective-permute-done | bytes 131104 | tf_op jit(solution)/shard_map/ppermute | solution.py:531
  12.2 0.0 collective-permute-done.3.odd_ref
  12.2 0.1 returns.1
  12.3 1.7 %collective-permute-start.9 = (bf16[528,128]{1,0:T(8,128)(2,1)S(1)}, bf16[528,128]{1,0:T(8,128)(2,1)S(1)}, u32[]{:S(2)}, u32[]{:S(2)}) collective-permute-start(bf16[528,128]{1,0:T(8,128)(2,1)S(1)} %returns.1), channel_id=1, source_target_pairs={{0,2},{2,0},{1,3},{3,1},{4,6},{6,4},{5,7},{7,5},{8,10},{10,8},{9,1... | collective-permute-start | bytes 405512 | tf_op jit(solution)/shard_map/ppermute | solution.py:549
  14.0 0.0 collective-permute-start.6
  14.0 0.3 %ready.1 = (bf16[1,256,256]{2,1,0:T(8,128)(2,1)S(1)}, f32[2,256,128]{2,1,0:T(8,128)S(1)}) custom-call(f32[1,8,128]{2,1,0:T(8,128)S(1)} %get-tuple-element.38.gates_ref, f32[1,256,128]{2,1,0:T(8,128)S(1)} %get-tuple-element.40.keep_ref, bf16[2,256,128]{2,1,0:T(8,128)(2,1)S(1)} %get-tuple-element.41.x_ref, ...), custom_call_target="tpu_custom_call" | custom-call | tf_op jit(solution)/shard_map/ready/pallas_call | solution.py:358
  14.3 0.8 %collective-permute-done.4.refs_0_ = bf16[2,256,128]{2,1,0:T(8,128)(2,1)S(1)} collective-permute-done((bf16[2,256,128]{2,1,0:T(8,128)(2,1)S(1)}, bf16[2,256,128]{2,1,0:T(8,128)(2,1)S(1)}, u32[]{:S(2)}, u32[]{:S(2)}) %collective-permute-start.4) | collective-permute-done | bytes 131104 | tf_op jit(solution)/shard_map/ppermute | solution.py:531
  15.1 0.0 collective-permute-start.7
  15.1 0.0 collective-permute-done.5.refs_1_
  15.1 0.5 %collective-permute-start.8 = (bf16[2,256,128]{2,1,0:T(8,128)(2,1)S(1)}, bf16[2,256,128]{2,1,0:T(8,128)(2,1)S(1)}, u32[]{:S(2)}, u32[]{:S(2)}) collective-permute-start(bf16[2,256,128]{2,1,0:T(8,128)(2,1)S(1)} %collective-permute-done.5.refs_1_), channel_id=1, source_target_pairs={{0,1},{1,0},{2,3},{3,2},{4,5},{5,4},{6,7},{7,6},{8,9},{9,8},{10,11... | collective-permute-start | bytes 393224 | tf_op jit(solution)/shard_map/ppermute | solution.py:537
  15.6 0.5 %sides.1.part_ref = f32[2,256,128]{2,1,0:T(8,128)S(1)} custom-call(f32[1,8,128]{2,1,0:T(8,128)S(1)} %get-tuple-element.38.gates_ref, bf16[2816,128]{1,0:T(8,128)(2,1)S(1)} %get-tuple-element.39.mine_ref.folded_ref, bf16[2816,128]{1,0:T(8,128)(2,1)S(1)} %collective-permute-done.other_ref, f32[2,256,128]{2,1,0:T(8,128)S(1)} %get-tuple-element.48.part_ref, ...), custom_call_target="tpu_custom_call" | custom-call | tf_op jit(solution)/shard_map/sides/pallas_call | solution.py:387
  16.1 0.0 collective-permute-done.6.refs_1_
  16.1 0.5 %near.1 = (f32[6,256,256]{2,1,0:T(8,128)S(1)}, f32[6,128,256]{2,1,0:T(8,128)S(1)}) custom-call(bf16[1,256,256]{2,1,0:T(8,128)(2,1)S(1)} %get-tuple-element.51.queries_ref, bf16[128,256]{1,0:T(8,128)(2,1)S(1)} %get-tuple-element.52.pool_ref, bf16[2,256,128]{2,1,0:T(8,128)(2,1)S(1)} %collective-permute-done.1.refs_0_, ...), custom_call_target="tpu_custom_call" | custom-call | tf_op jit(solution)/shard_map/near/pallas_call | solution.py:416
  16.6 0.0 collective-permute-done.7.refs_2_
  16.6 0.0 collective-permute-done.8.refs_3_
  16.7 0.5 %tables.1 = (f32[6,256,256]{2,1,0:T(8,128)S(1)}, f32[6,128,256]{2,1,0:T(8,128)S(1)}) custom-call(bf16[1,256,256]{2,1,0:T(8,128)(2,1)S(1)} %get-tuple-element.51.queries_ref, bf16[128,256]{1,0:T(8,128)(2,1)S(1)} %get-tuple-element.52.pool_ref, f32[6,256,256]{2,1,0:T(8,128)S(1)} %get-tuple-element.57.near_fine, ...), custom_call_target="tpu_custom_call", output_to_operand_aliasing={{0}: (2, {}), {1}: (3, {})} | custom-call | tf_op jit(solution)/shard_map/tables/pallas_call | solution.py:453
  17.1 0.7 %collective-permute-done.9.refs_0_ = bf16[528,128]{1,0:T(8,128)(2,1)S(1)} collective-permute-done((bf16[528,128]{1,0:T(8,128)(2,1)S(1)}, bf16[528,128]{1,0:T(8,128)(2,1)S(1)}, u32[]{:S(2)}, u32[]{:S(2)}) %collective-permute-start.9) | collective-permute-done | bytes 135200 | tf_op jit(solution)/shard_map/ppermute | solution.py:549
  17.9 1.5 %volume.1 = (bf16[6120,128]{1,0:T(8,128)(2,1)}, f32[1,2,256,128]{3,2,1,0:T(8,128)}) custom-call(s32[2,9]{1,0:T(2,128)S(1)} %get-tuple-element.37.list_ref, f32[2,256,128]{2,1,0:T(8,128)S(1)} %sides.1.part_ref, f32[6,256,256]{2,1,0:T(8,128)S(1)} %get-tuple-element.67.fine_table, f32[6,128,256]{2,1,0:T(8,128)S(1)} %get-tuple-element.68.coarse_table, ...), custom_call_target="tpu_custom_call" | custom-call | tf_op jit(solution)/shard_map/volume/pallas_call | solution.py:501
Async XLA Ops:
  2.7 3.4 %collective-permute-start = (bf16[2816,128]{1,0:T(8,128)(2,1)S(1)}, bf16[2816,128]{1,0:T(8,128)(2,1)S(1)}, u32[]{:S(2)}, u32[]{:S(2)}) collective-permute-start(bf16[2816,128]{1,0:T(8,128)(2,1)S(1)} %get-tuple-element.39.mine_ref.folded_ref), channel_id=1, source_target_pairs={{0,1},{1,0},{2,3},{3,2},{4,5},{5,4},{6,7},{7,6},{8,9},{9,8},{10,11... | collective-permute-start | bytes 2162696 | tf_op jit(solution)/shard_map/ppermute | solution.py:537
  3.2 6.7 %collective-permute-start.1 = (bf16[2,256,128]{2,1,0:T(8,128)(2,1)S(1)}, bf16[2,256,128]{2,1,0:T(8,128)(2,1)S(1)}, u32[]{:S(2)}, u32[]{:S(2)}) collective-permute-start(bf16[2,256,128]{2,1,0:T(8,128)(2,1)S(1)} %get-tuple-element.41.x_ref), channel_id=1, source_target_pairs={{0,2},{2,0},{1,3},{3,1},{4,6},{6,4},{5,7},{7,5},{8,10},{10,8},{9,1... | collective-permute-start | bytes 393224 | tf_op jit(solution)/shard_map/ppermute | solution.py:542
  6.5 5.7 %collective-permute-start.2 = (bf16[2,256,128]{2,1,0:T(8,128)(2,1)S(1)}, bf16[2,256,128]{2,1,0:T(8,128)(2,1)S(1)}, u32[]{:S(2)}, u32[]{:S(2)}) collective-permute-start(bf16[2,256,128]{2,1,0:T(8,128)(2,1)S(1)} %get-tuple-element.44), channel_id=1, source_target_pairs={{0,4},{4,0},{8,12},{12,8},{1,5},{5,1},{9,13},{13,9},{2,6},{6,2},{1... | collective-permute-start | bytes 393224 | tf_op jit(solution)/shard_map/ppermute | solution.py:531
  8.4 3.8 %collective-permute-start.3 = (bf16[2,256,128]{2,1,0:T(8,128)(2,1)S(1)}, bf16[2,256,128]{2,1,0:T(8,128)(2,1)S(1)}, u32[]{:S(2)}, u32[]{:S(2)}) collective-permute-start(bf16[2,256,128]{2,1,0:T(8,128)(2,1)S(1)} %get-tuple-element.45), channel_id=1, source_target_pairs={{4,8},{8,4},{5,9},{9,5},{0,1},{1,0},{12,13},{13,12},{6,10},{10,6},... | collective-permute-start | bytes 393224 | tf_op jit(solution)/shard_map/ppermute | solution.py:534
  9.9 5.3 %collective-permute-start.4 = (bf16[2,256,128]{2,1,0:T(8,128)(2,1)S(1)}, bf16[2,256,128]{2,1,0:T(8,128)(2,1)S(1)}, u32[]{:S(2)}, u32[]{:S(2)}) collective-permute-start(bf16[2,256,128]{2,1,0:T(8,128)(2,1)S(1)} %collective-permute-done.1.refs_0_), channel_id=1, source_target_pairs={{0,4},{4,0},{8,12},{12,8},{1,5},{5,1},{9,13},{13,9},{2,6},{6,2},{1... | collective-permute-start | bytes 393224 | tf_op jit(solution)/shard_map/ppermute | solution.py:531
  11.7 3.4 %collective-permute-start.5 = (bf16[2,256,128]{2,1,0:T(8,128)(2,1)S(1)}, bf16[2,256,128]{2,1,0:T(8,128)(2,1)S(1)}, u32[]{:S(2)}, u32[]{:S(2)}) collective-permute-start(bf16[2,256,128]{2,1,0:T(8,128)(2,1)S(1)} %collective-permute-done.1.refs_0_), channel_id=1, source_target_pairs={{4,8},{8,4},{5,9},{9,5},{0,1},{1,0},{12,13},{13,12},{6,10},{10,6},... | collective-permute-start | bytes 393224 | tf_op jit(solution)/shard_map/ppermute | solution.py:534
  12.3 5.6 %collective-permute-start.9 = (bf16[528,128]{1,0:T(8,128)(2,1)S(1)}, bf16[528,128]{1,0:T(8,128)(2,1)S(1)}, u32[]{:S(2)}, u32[]{:S(2)}) collective-permute-start(bf16[528,128]{1,0:T(8,128)(2,1)S(1)} %returns.1), channel_id=1, source_target_pairs={{0,2},{2,0},{1,3},{3,1},{4,6},{6,4},{5,7},{7,5},{8,10},{10,8},{9,1... | collective-permute-start | bytes 405512 | tf_op jit(solution)/shard_map/ppermute | solution.py:549
  14.0 2.1 %collective-permute-start.6 = (bf16[2,256,128]{2,1,0:T(8,128)(2,1)S(1)}, bf16[2,256,128]{2,1,0:T(8,128)(2,1)S(1)}, u32[]{:S(2)}, u32[]{:S(2)}) collective-permute-start(bf16[2,256,128]{2,1,0:T(8,128)(2,1)S(1)} %collective-permute-done.1.refs_0_), channel_id=1, source_target_pairs={{0,1},{1,0},{2,3},{3,2},{4,5},{5,4},{6,7},{7,6},{8,9},{9,8},{10,11... | collective-permute-start | bytes 393224 | tf_op jit(solution)/shard_map/ppermute | solution.py:537
  15.1 1.5 %collective-permute-start.7 = (bf16[2,256,128]{2,1,0:T(8,128)(2,1)S(1)}, bf16[2,256,128]{2,1,0:T(8,128)(2,1)S(1)}, u32[]{:S(2)}, u32[]{:S(2)}) collective-permute-start(bf16[2,256,128]{2,1,0:T(8,128)(2,1)S(1)} %collective-permute-done.4.refs_0_), channel_id=1, source_target_pairs={{0,1},{1,0},{2,3},{3,2},{4,5},{5,4},{6,7},{7,6},{8,9},{9,8},{10,11... | collective-permute-start | bytes 393224 | tf_op jit(solution)/shard_map/ppermute | solution.py:537
  15.1 1.5 %collective-permute-start.8 = (bf16[2,256,128]{2,1,0:T(8,128)(2,1)S(1)}, bf16[2,256,128]{2,1,0:T(8,128)(2,1)S(1)}, u32[]{:S(2)}, u32[]{:S(2)}) collective-permute-start(bf16[2,256,128]{2,1,0:T(8,128)(2,1)S(1)} %collective-permute-done.5.refs_1_), channel_id=1, source_target_pairs={{0,1},{1,0},{2,3},{3,2},{4,5},{5,4},{6,7},{7,6},{8,9},{9,8},{10,11... | collective-permute-start | bytes 393224 | tf_op jit(solution)/shard_map/ppermute | solution.py:537

commit v6 on v5

--- a/solution.py
+++ b/solution.py
@@ -117,14 +117,13 @@
     return jax.ShapeDtypeStruct(shape, dtype)
 
 
-def call(kernel, name, outs, in_specs, out_specs, scratch, vmem_mib, aliases=None):
+def call(kernel, name, outs, in_specs, out_specs, scratch, vmem_mib):
     return pl.pallas_call(
         kernel,
         out_shape=outs,
         in_specs=in_specs,
         out_specs=out_specs,
         scratch_shapes=scratch,
-        input_output_aliases=aliases or {},
         compiler_params=pltpu.CompilerParams(vmem_limit_bytes=vmem_mib * 2**20),
         name=name,
     )
@@ -407,8 +406,8 @@
             coarse_term = multiply(cells, queries_ref[j], (1, 0))
             fine = fine_term if fine is None else fine + fine_term
             coarse = coarse_term if coarse is None else coarse + coarse_term
-        fine_ref[tiles + s] = fine
-        coarse_ref[tiles + s] = coarse
+        fine_ref[s] = fine
+        coarse_ref[s] = coarse
 
 
 def near(partners, queries, pool, same):
@@ -417,8 +416,8 @@
         functools.partial(near_kernel, tiles, partners),
         "near",
         (
-            shape_of((3 * tiles, pixels, tiles * pixels // 2), jnp.float32),
-            shape_of((3 * tiles, PAD, tiles * pixels // 2), jnp.float32),
+            shape_of((tiles, pixels, tiles * pixels // 2), jnp.float32),
+            shape_of((tiles, PAD, tiles * pixels // 2), jnp.float32),
         ),
         [VMEM] * (2 + len(same)),
         (VMEM,) * 2,
@@ -429,6 +428,8 @@
 
 def tables_kernel(tiles, partners, queries_ref, pool_ref, near_fine, near_coarse, *refs):
     inputs, (fine_table, coarse_table, levels, cells) = refs[: 4 * partners], refs[4 * partners :]
+    fine_table[tiles : 2 * tiles] = near_fine[...]
+    coarse_table[tiles : 2 * tiles] = near_coarse[...]
     pool = pool_ref[...]
     for j in range(partners):
         for part in range(2):
@@ -453,15 +454,14 @@
     return call(
         functools.partial(tables_kernel, tiles, partners),
         "tables",
-        (shape_of(fine.shape, jnp.float32), shape_of(coarse.shape, jnp.float32)),
+        tuple(shape_of((3 * tiles,) + near.shape[1:], jnp.float32) for near in (fine, coarse)),
         [VMEM] * (4 + len(beside)),
         (VMEM,) * 2,
         [
             pltpu.VMEM((partners, 2 * tiles * pixels, 2 * channels), jnp.bfloat16),
             pltpu.VMEM((partners, 2 * tiles * PAD, 2 * channels), jnp.bfloat16),
         ],
-        6,
-        {2: 0, 3: 1},
+        7,
     )(queries, pool, fine, coarse, *beside)
 
 

time: 19.6 us -> 19.6 us (level)
  transfers between devices with their start and end apart: 10 -> 10, of which waited for: 4 -> 5; matrix products, arithmetic and copies ran while one was open for 0% -> 0% of each run, Pallas kernels for 13% -> 13%
where the time goes in v6:
time: 19.6 us; the launch traced here: 19.4 us
  starting transfers between devices  9.08 us (46%)
  Pallas kernels  6.11 us (31%)
  waiting for transfers between devices  3.51 us (18%)
  between operations  0.71 us (4%)
    ppermute x2, starting transfers between devices, over_even(): return lax.ppermute(z, 'tile', evens)  3.76 us
    ppermute x1, starting transfers between devices, local(): arrived = [lax.ppermute(x, 'frame', ahead) for ahead, _ in links]  2.56 us
    pallas_call x1, Pallas kernels, fold(): call(functools.partial(fold_kernel, tiles, half, partners), 'fold', (shap...  2.05 us
    ppermute x1, starting transfers between devices, local(): lax.ppermute(z, 'frame', back)  1.72 us
    pallas_call x1, Pallas kernels, volumes(): call(functools.partial(volume_kernel, tiles, half, partners), 'volume', (...  1.55 us
    ppermute x1, waiting for transfers between devices, local(): arrived = [lax.ppermute(x, 'frame', ahead) for ahead, _ in links]  1.49 us
    ppermute x2, waiting for transfers between devices, over_even(): return lax.ppermute(z, 'tile', evens)  1.24 us
    ppermute x4, starting transfers between devices, over_cores(): return lax.ppermute(z, 'chan', swap)  1.03 us
  transfers between devices with their start and end apart: 10, of which 5 were waited for; matrix products, arithmetic and copies ran while one was open for 0% of the time, Pallas kernels for 13%

profile of v6, /device:TPU:0, one launch (start us, length us, event | category | flops | bytes accessed | tf_op | source)
XLA Modules:
  0.0 19.4 jit_solution(652830226773831760)
XLA Ops:
  0.6 2.1 %fold.1 = (bf16[2816,128]{1,0:T(8,128)(2,1)S(1)}, bf16[2,256,128]{2,1,0:T(8,128)(2,1)S(1)}, f32[1,8,128]{2,1,0:T(8,128)S(1)}, f32[1,256,128]{2,1,0:T(8,128)S(1)}...) custom-call(s32[2,9]{1,0:T(2,128)} %neighbours_hbm.1, s32[2,256]{1,0:T(2,128)} %valid_hbm.1, s32[1,2]{1,0:T(1,128)} %pairing_hbm.1, ...), custom_call_target="tpu_custom_call" | custom-call | tf_op jit(solution)/shard_map/fold/pallas_call | solution.py:193
  2.7 0.5 %collective-permute-start = (bf16[2816,128]{1,0:T(8,128)(2,1)S(1)}, bf16[2816,128]{1,0:T(8,128)(2,1)S(1)}, u32[]{:S(2)}, u32[]{:S(2)}) collective-permute-start(bf16[2816,128]{1,0:T(8,128)(2,1)S(1)} %get-tuple-element.39.mine_ref.folded_ref), channel_id=1, source_target_pairs={{0,1},{1,0},{2,3},{3,2},{4,5},{5,4},{6,7},{7,6},{8,9},{9,8},{10,11... | collective-permute-start | bytes 2162696 | tf_op jit(solution)/shard_map/ppermute | solution.py:537
  3.2 2.6 %collective-permute-start.1 = (bf16[2,256,128]{2,1,0:T(8,128)(2,1)S(1)}, bf16[2,256,128]{2,1,0:T(8,128)(2,1)S(1)}, u32[]{:S(2)}, u32[]{:S(2)}) collective-permute-start(bf16[2,256,128]{2,1,0:T(8,128)(2,1)S(1)} %get-tuple-element.41.x_ref), channel_id=1, source_target_pairs={{0,2},{2,0},{1,3},{3,1},{4,6},{6,4},{5,7},{7,5},{8,10},{10,8},{9,1... | collective-permute-start | bytes 393224 | tf_op jit(solution)/shard_map/ppermute | solution.py:542
  5.8 0.3 %early.1.part_ref = f32[6,256,128]{2,1,0:T(8,128)S(1)} custom-call(bf16[2,256,128]{2,1,0:T(8,128)(2,1)S(1)} %get-tuple-element.41.x_ref, bf16[2816,128]{1,0:T(8,128)(2,1)S(1)} %get-tuple-element.39.mine_ref.folded_ref), custom_call_target="tpu_custom_call" | custom-call | tf_op jit(solution)/shard_map/early/pallas_call | solution.py:244
  6.1 0.0 collective-permute-done.other_ref
  6.1 0.3 %keys.1 = (f32[2,256,128]{2,1,0:T(8,128)S(1)}, bf16[2,256,128]{2,1,0:T(8,128)(2,1)S(1)}, bf16[2,256,128]{2,1,0:T(8,128)(2,1)S(1)}) custom-call(bf16[2,256,128]{2,1,0:T(8,128)(2,1)S(1)} %get-tuple-element.41.x_ref, f32[6,256,128]{2,1,0:T(8,128)S(1)} %early.1.part_ref, bf16[2816,128]{1,0:T(8,128)(2,1)S(1)} %collective-permute-done.other_ref), custom_call_target="tpu_custom_call" | custom-call | tf_op jit(solution)/shard_map/keys/pallas_call | solution.py:273
  6.5 1.9 %collective-permute-start.2 = (bf16[2,256,128]{2,1,0:T(8,128)(2,1)S(1)}, bf16[2,256,128]{2,1,0:T(8,128)(2,1)S(1)}, u32[]{:S(2)}, u32[]{:S(2)}) collective-permute-start(bf16[2,256,128]{2,1,0:T(8,128)(2,1)S(1)} %get-tuple-element.44), channel_id=1, source_target_pairs={{0,4},{4,0},{8,12},{12,8},{1,5},{5,1},{9,13},{13,9},{2,6},{6,2},{1... | collective-permute-start | bytes 393224 | tf_op jit(solution)/shard_map/ppermute | solution.py:531
  8.4 0.0 collective-permute-start.3
  8.4 1.5 %collective-permute-done.1.refs_0_ = bf16[2,256,128]{2,1,0:T(8,128)(2,1)S(1)} collective-permute-done((bf16[2,256,128]{2,1,0:T(8,128)(2,1)S(1)}, bf16[2,256,128]{2,1,0:T(8,128)(2,1)S(1)}, u32[]{:S(2)}, u32[]{:S(2)}) %collective-permute-start.1) | collective-permute-done | bytes 131104 | tf_op jit(solution)/shard_map/ppermute | solution.py:542
  9.9 1.8 %collective-permute-start.4 = (bf16[2,256,128]{2,1,0:T(8,128)(2,1)S(1)}, bf16[2,256,128]{2,1,0:T(8,128)(2,1)S(1)}, u32[]{:S(2)}, u32[]{:S(2)}) collective-permute-start(bf16[2,256,128]{2,1,0:T(8,128)(2,1)S(1)} %collective-permute-done.1.refs_0_), channel_id=1, source_target_pairs={{0,4},{4,0},{8,12},{12,8},{1,5},{5,1},{9,13},{13,9},{2,6},{6,2},{1... | collective-permute-start | bytes 393224 | tf_op jit(solution)/shard_map/ppermute | solution.py:531
  11.7 0.0 collective-permute-start.5
  11.7 0.5 %collective-permute-done.2.even_ref = bf16[2,256,128]{2,1,0:T(8,128)(2,1)S(1)} collective-permute-done((bf16[2,256,128]{2,1,0:T(8,128)(2,1)S(1)}, bf16[2,256,128]{2,1,0:T(8,128)(2,1)S(1)}, u32[]{:S(2)}, u32[]{:S(2)}) %collective-permute-start.2) | collective-permute-done | bytes 131104 | tf_op jit(solution)/shard_map/ppermute | solution.py:531
  12.2 0.0 collective-permute-done.3.odd_ref
  12.2 0.1 returns.1
  12.3 1.7 %collective-permute-start.9 = (bf16[528,128]{1,0:T(8,128)(2,1)S(1)}, bf16[528,128]{1,0:T(8,128)(2,1)S(1)}, u32[]{:S(2)}, u32[]{:S(2)}) collective-permute-start(bf16[528,128]{1,0:T(8,128)(2,1)S(1)} %returns.1), channel_id=1, source_target_pairs={{0,2},{2,0},{1,3},{3,1},{4,6},{6,4},{5,7},{7,5},{8,10},{10,8},{9,1... | collective-permute-start | bytes 405512 | tf_op jit(solution)/shard_map/ppermute | solution.py:549
  14.0 0.0 collective-permute-start.6
  14.0 0.3 %ready.1 = (bf16[1,256,256]{2,1,0:T(8,128)(2,1)S(1)}, f32[2,256,128]{2,1,0:T(8,128)S(1)}) custom-call(f32[1,8,128]{2,1,0:T(8,128)S(1)} %get-tuple-element.38.gates_ref, f32[1,256,128]{2,1,0:T(8,128)S(1)} %get-tuple-element.40.keep_ref, bf16[2,256,128]{2,1,0:T(8,128)(2,1)S(1)} %get-tuple-element.41.x_ref, ...), custom_call_target="tpu_custom_call" | custom-call | tf_op jit(solution)/shard_map/ready/pallas_call | solution.py:357
  14.3 0.8 %collective-permute-done.4.refs_0_ = bf16[2,256,128]{2,1,0:T(8,128)(2,1)S(1)} collective-permute-done((bf16[2,256,128]{2,1,0:T(8,128)(2,1)S(1)}, bf16[2,256,128]{2,1,0:T(8,128)(2,1)S(1)}, u32[]{:S(2)}, u32[]{:S(2)}) %collective-permute-start.4) | collective-permute-done | bytes 131104 | tf_op jit(solution)/shard_map/ppermute | solution.py:531
  15.1 0.0 collective-permute-start.7
  15.1 0.0 collective-permute-done.5.refs_1_
  15.1 0.5 %collective-permute-start.8 = (bf16[2,256,128]{2,1,0:T(8,128)(2,1)S(1)}, bf16[2,256,128]{2,1,0:T(8,128)(2,1)S(1)}, u32[]{:S(2)}, u32[]{:S(2)}) collective-permute-start(bf16[2,256,128]{2,1,0:T(8,128)(2,1)S(1)} %collective-permute-done.5.refs_1_), channel_id=1, source_target_pairs={{0,1},{1,0},{2,3},{3,2},{4,5},{5,4},{6,7},{7,6},{8,9},{9,8},{10,11... | collective-permute-start | bytes 393224 | tf_op jit(solution)/shard_map/ppermute | solution.py:537
  15.6 0.5 %sides.1.part_ref = f32[2,256,128]{2,1,0:T(8,128)S(1)} custom-call(f32[1,8,128]{2,1,0:T(8,128)S(1)} %get-tuple-element.38.gates_ref, bf16[2816,128]{1,0:T(8,128)(2,1)S(1)} %get-tuple-element.39.mine_ref.folded_ref, bf16[2816,128]{1,0:T(8,128)(2,1)S(1)} %collective-permute-done.other_ref, f32[2,256,128]{2,1,0:T(8,128)S(1)} %get-tuple-element.48.part_ref, ...), custom_call_target="tpu_custom_call" | custom-call | tf_op jit(solution)/shard_map/sides/pallas_call | solution.py:386
  16.1 0.0 collective-permute-done.6.refs_1_
  16.1 0.5 %near.1 = (f32[2,256,256]{2,1,0:T(8,128)S(1)}, f32[2,128,256]{2,1,0:T(8,128)S(1)}) custom-call(bf16[1,256,256]{2,1,0:T(8,128)(2,1)S(1)} %get-tuple-element.51.queries_ref, bf16[128,256]{1,0:T(8,128)(2,1)S(1)} %get-tuple-element.52.pool_ref, bf16[2,256,128]{2,1,0:T(8,128)(2,1)S(1)} %collective-permute-done.1.refs_0_, ...), custom_call_target="tpu_custom_call" | custom-call | tf_op jit(solution)/shard_map/near/pallas_call | solution.py:415
  16.6 0.0 collective-permute-done.7.refs_2_
  16.6 0.1 collective-permute-done.8.refs_3_
  16.7 0.5 %tables.1 = (f32[6,256,256]{2,1,0:T(8,128)S(1)}, f32[6,128,256]{2,1,0:T(8,128)S(1)}) custom-call(bf16[1,256,256]{2,1,0:T(8,128)(2,1)S(1)} %get-tuple-element.51.queries_ref, bf16[128,256]{1,0:T(8,128)(2,1)S(1)} %get-tuple-element.52.pool_ref, f32[2,256,256]{2,1,0:T(8,128)S(1)} %get-tuple-element.57.near_fine, ...), custom_call_target="tpu_custom_call" | custom-call | tf_op jit(solution)/shard_map/tables/pallas_call | solution.py:454
  17.1 0.7 %collective-permute-done.9.refs_0_ = bf16[528,128]{1,0:T(8,128)(2,1)S(1)} collective-permute-done((bf16[528,128]{1,0:T(8,128)(2,1)S(1)}, bf16[528,128]{1,0:T(8,128)(2,1)S(1)}, u32[]{:S(2)}, u32[]{:S(2)}) %collective-permute-start.9) | collective-permute-done | bytes 135200 | tf_op jit(solution)/shard_map/ppermute | solution.py:549
  17.9 1.5 %volume.1 = (bf16[6120,128]{1,0:T(8,128)(2,1)}, f32[1,2,256,128]{3,2,1,0:T(8,128)}) custom-call(s32[2,9]{1,0:T(2,128)S(1)} %get-tuple-element.37.list_ref, f32[2,256,128]{2,1,0:T(8,128)S(1)} %sides.1.part_ref, f32[6,256,256]{2,1,0:T(8,128)S(1)} %get-tuple-element.67.fine_table, f32[6,128,256]{2,1,0:T(8,128)S(1)} %get-tuple-element.68.coarse_table, ...), custom_call_target="tpu_custom_call" | custom-call | tf_op jit(solution)/shard_map/volume/pallas_call | solution.py:501
Async XLA Ops:
  2.7 3.4 %collective-permute-start = (bf16[2816,128]{1,0:T(8,128)(2,1)S(1)}, bf16[2816,128]{1,0:T(8,128)(2,1)S(1)}, u32[]{:S(2)}, u32[]{:S(2)}) collective-permute-start(bf16[2816,128]{1,0:T(8,128)(2,1)S(1)} %get-tuple-element.39.mine_ref.folded_ref), channel_id=1, source_target_pairs={{0,1},{1,0},{2,3},{3,2},{4,5},{5,4},{6,7},{7,6},{8,9},{9,8},{10,11... | collective-permute-start | bytes 2162696 | tf_op jit(solution)/shard_map/ppermute | solution.py:537
  3.2 6.7 %collective-permute-start.1 = (bf16[2,256,128]{2,1,0:T(8,128)(2,1)S(1)}, bf16[2,256,128]{2,1,0:T(8,128)(2,1)S(1)}, u32[]{:S(2)}, u32[]{:S(2)}) collective-permute-start(bf16[2,256,128]{2,1,0:T(8,128)(2,1)S(1)} %get-tuple-element.41.x_ref), channel_id=1, source_target_pairs={{0,2},{2,0},{1,3},{3,1},{4,6},{6,4},{5,7},{7,5},{8,10},{10,8},{9,1... | collective-permute-start | bytes 393224 | tf_op jit(solution)/shard_map/ppermute | solution.py:542
  6.5 5.7 %collective-permute-start.2 = (bf16[2,256,128]{2,1,0:T(8,128)(2,1)S(1)}, bf16[2,256,128]{2,1,0:T(8,128)(2,1)S(1)}, u32[]{:S(2)}, u32[]{:S(2)}) collective-permute-start(bf16[2,256,128]{2,1,0:T(8,128)(2,1)S(1)} %get-tuple-element.44), channel_id=1, source_target_pairs={{0,4},{4,0},{8,12},{12,8},{1,5},{5,1},{9,13},{13,9},{2,6},{6,2},{1... | collective-permute-start | bytes 393224 | tf_op jit(solution)/shard_map/ppermute | solution.py:531
  8.4 3.8 %collective-permute-start.3 = (bf16[2,256,128]{2,1,0:T(8,128)(2,1)S(1)}, bf16[2,256,128]{2,1,0:T(8,128)(2,1)S(1)}, u32[]{:S(2)}, u32[]{:S(2)}) collective-permute-start(bf16[2,256,128]{2,1,0:T(8,128)(2,1)S(1)} %get-tuple-element.45), channel_id=1, source_target_pairs={{4,8},{8,4},{5,9},{9,5},{0,1},{1,0},{12,13},{13,12},{6,10},{10,6},... | collective-permute-start | bytes 393224 | tf_op jit(solution)/shard_map/ppermute | solution.py:534
  9.9 5.3 %collective-permute-start.4 = (bf16[2,256,128]{2,1,0:T(8,128)(2,1)S(1)}, bf16[2,256,128]{2,1,0:T(8,128)(2,1)S(1)}, u32[]{:S(2)}, u32[]{:S(2)}) collective-permute-start(bf16[2,256,128]{2,1,0:T(8,128)(2,1)S(1)} %collective-permute-done.1.refs_0_), channel_id=1, source_target_pairs={{0,4},{4,0},{8,12},{12,8},{1,5},{5,1},{9,13},{13,9},{2,6},{6,2},{1... | collective-permute-start | bytes 393224 | tf_op jit(solution)/shard_map/ppermute | solution.py:531
  11.7 3.4 %collective-permute-start.5 = (bf16[2,256,128]{2,1,0:T(8,128)(2,1)S(1)}, bf16[2,256,128]{2,1,0:T(8,128)(2,1)S(1)}, u32[]{:S(2)}, u32[]{:S(2)}) collective-permute-start(bf16[2,256,128]{2,1,0:T(8,128)(2,1)S(1)} %collective-permute-done.1.refs_0_), channel_id=1, source_target_pairs={{4,8},{8,4},{5,9},{9,5},{0,1},{1,0},{12,13},{13,12},{6,10},{10,6},... | collective-permute-start | bytes 393224 | tf_op jit(solution)/shard_map/ppermute | solution.py:534
  12.3 5.6 %collective-permute-start.9 = (bf16[528,128]{1,0:T(8,128)(2,1)S(1)}, bf16[528,128]{1,0:T(8,128)(2,1)S(1)}, u32[]{:S(2)}, u32[]{:S(2)}) collective-permute-start(bf16[528,128]{1,0:T(8,128)(2,1)S(1)} %returns.1), channel_id=1, source_target_pairs={{0,2},{2,0},{1,3},{3,1},{4,6},{6,4},{5,7},{7,5},{8,10},{10,8},{9,1... | collective-permute-start | bytes 405512 | tf_op jit(solution)/shard_map/ppermute | solution.py:549
  14.0 2.1 %collective-permute-start.6 = (bf16[2,256,128]{2,1,0:T(8,128)(2,1)S(1)}, bf16[2,256,128]{2,1,0:T(8,128)(2,1)S(1)}, u32[]{:S(2)}, u32[]{:S(2)}) collective-permute-start(bf16[2,256,128]{2,1,0:T(8,128)(2,1)S(1)} %collective-permute-done.1.refs_0_), channel_id=1, source_target_pairs={{0,1},{1,0},{2,3},{3,2},{4,5},{5,4},{6,7},{7,6},{8,9},{9,8},{10,11... | collective-permute-start | bytes 393224 | tf_op jit(solution)/shard_map/ppermute | solution.py:537
  15.1 1.5 %collective-permute-start.7 = (bf16[2,256,128]{2,1,0:T(8,128)(2,1)S(1)}, bf16[2,256,128]{2,1,0:T(8,128)(2,1)S(1)}, u32[]{:S(2)}, u32[]{:S(2)}) collective-permute-start(bf16[2,256,128]{2,1,0:T(8,128)(2,1)S(1)} %collective-permute-done.4.refs_0_), channel_id=1, source_target_pairs={{0,1},{1,0},{2,3},{3,2},{4,5},{5,4},{6,7},{7,6},{8,9},{9,8},{10,11... | collective-permute-start | bytes 393224 | tf_op jit(solution)/shard_map/ppermute | solution.py:537
  15.1 1.5 %collective-permute-start.8 = (bf16[2,256,128]{2,1,0:T(8,128)(2,1)S(1)}, bf16[2,256,128]{2,1,0:T(8,128)(2,1)S(1)}, u32[]{:S(2)}, u32[]{:S(2)}) collective-permute-start(bf16[2,256,128]{2,1,0:T(8,128)(2,1)S(1)} %collective-permute-done.5.refs_1_), channel_id=1, source_target_pairs={{0,1},{1,0},{2,3},{3,2},{4,5},{5,4},{6,7},{7,6},{8,9},{9,8},{10,11... | collective-permute-start | bytes 393224 | tf_op jit(solution)/shard_map/ppermute | solution.py:537

commit v7 on v6

--- a/solution.py
+++ b/solution.py
@@ -134,10 +134,12 @@
     neighbours_ref, valid_ref, pairing_ref, cot_ref, stage, sems, *totals = refs[6:]
     core = lax.axis_index("chan")
     first = lax.axis_index("tile") * tiles
-    small, (features_copy, list_copy, *waits) = split(
+    small, (*waits, features_copy, list_copy) = split(
         copies(
-            [neighbours_hbm, valid_hbm, pairing_hbm, features_hbm.at[0], neighbours_hbm] + [cot_hbm.at[k] for k in range(NEIGHBOURS)],
-            [neighbours_ref, valid_ref, pairing_ref, x_ref, list_ref] + [cot_ref.at[k] for k in range(NEIGHBOURS)],
+            [neighbours_hbm, valid_hbm, pairing_hbm]
+            + [cot_hbm.at[k] for k in range(NEIGHBOURS)]
+            + [features_hbm.at[0], neighbours_hbm],
+            [neighbours_ref, valid_ref, pairing_ref] + [cot_ref.at[k] for k in range(NEIGHBOURS)] + [x_ref, list_ref],
             sems,
         ),
         3,
@@ -168,9 +170,6 @@
             folded_ref[fold_rows(a, w)] = ((totals[a][w, :PIXELS] + spread) * keep[a]).astype(jnp.bfloat16)
     features_copy.wait()
     list_copy.wait()
-    _, there = halves(core, half)
-    for a in range(tiles):
-        folded_ref[query_rows(tiles, half, a)] = x_ref[a, there, :]
 
 
 def split(items, count):
@@ -182,11 +181,6 @@
     return slice(start, start + PIXELS)
 
 
-def query_rows(tiles, half, a):
-    start = tiles * SPAN * PIXELS + a * half
-    return slice(start, start + half)
-
-
 def fold(partners, neighbours, valid, pairing, cotangent, features):
     half = cotangent.shape[-1]
     _, tiles, pixels, channels = features.shape
@@ -194,7 +188,7 @@
         functools.partial(fold_kernel, tiles, half, partners),
         "fold",
         (
-            shape_of((tiles * SPAN * PIXELS + tiles * half, half)),
+            shape_of((tiles * SPAN * PIXELS, half)),
             shape_of((tiles, pixels, channels)),
             shape_of((partners, 8, channels), jnp.float32),
             shape_of((partners, tiles * half, channels), jnp.float32),
@@ -337,11 +331,11 @@
     return grads
 
 
-def ready_kernel(tiles, half, partners, gates_ref, keep_ref, x_ref, folded_ref, other_ref, *refs):
+def ready_kernel(tiles, half, partners, gates_ref, keep_ref, x_ref, xo_ref, folded_ref, other_ref, *refs):
     same, (queries_ref, grad_ref) = refs[:partners], refs[partners:]
     here, _ = halves(lax.axis_index("chan"), half)
     mine = jnp.concatenate([x_ref[a, here, :] for a in range(tiles)], axis=0).astype(jnp.float32)
-    other = jnp.concatenate([other_ref[query_rows(tiles, half, a)] for a in range(tiles)], axis=0).astype(jnp.float32)
+    other = jnp.concatenate([xo_ref[a, here, :] for a in range(tiles)], axis=0).astype(jnp.float32)
     for j in range(partners):
         queries_ref[j] = join(mine * keep_ref[j], other * keep_ref[j]).T.astype(jnp.bfloat16)
     slots = range(tiles, 2 * tiles)
@@ -352,17 +346,17 @@
         grad_ref[a] = grads[a]
 
 
-def ready(partners, gates, keep, x, folded, other, same):
+def ready(partners, gates, keep, x, xo, folded, other, same):
     tiles, pixels, channels = x.shape
     return call(
         functools.partial(ready_kernel, tiles, pixels // 2, partners),
         "ready",
         (shape_of((partners, 2 * channels, tiles * pixels // 2)), shape_of(x.shape, jnp.float32)),
-        [VMEM] * (5 + len(same)),
+        [VMEM] * (6 + len(same)),
         (VMEM,) * 2,
         [],
         6,
-    )(gates, keep, x, folded, other, *same)
+    )(gates, keep, x, xo, folded, other, *same)
 
 
 def sides_kernel(tiles, half, partners, gates_ref, folded_ref, other_ref, part_ref, *refs):
@@ -541,13 +535,14 @@
     other = over_cores(folded)
     arrived = [lax.ppermute(x, "frame", ahead) for ahead, _ in links]
     own, to_even, to_odd = keys(x, early(x, folded), other)
+    xo = over_cores(x)
     arrived = [after(y, own) for y in arrived]
     beside = [(over_even(y), over_odd(y)) for y in arrived]
     from_odd = over_odd(to_odd)
     from_even = after(over_even(to_even), from_odd)
     sent = returns(partners, gates, own, from_even, from_odd)
     returned = [lax.ppermute(z, "frame", back) for z, (_, back) in zip(sent, links, strict=True)]
-    queries, part = ready(partners, gates, keep, x, folded, other, [after(y, sent[0]) for y in arrived])
+    queries, part = ready(partners, gates, keep, x, xo, folded, other, [after(y, sent[0]) for y in arrived])
     same, mine, exchanged = [], [], []
     for y, (even, odd) in zip(arrived, beside, strict=True):
         even, odd = after(even, part), after(odd, part)

time: 19.6 us -> 19.5 us (level)
  starting transfers between devices: 9.08 us -> 9.49 us
  waiting for transfers between devices: 3.51 us -> 3.11 us
    ppermute x4 -> x5, starting transfers between devices: 1.03 us -> 1.54 us  [over_cores(): return lax.ppermute(z, 'chan', swap)]
    ppermute x2, waiting for transfers between devices: 1.24 us -> 1.73 us  [over_even(): return lax.ppermute(z, 'tile', evens)]
    ppermute x1, waiting for transfers between devices: 0.73 us -> 0.24 us  [local(): lax.ppermute(z, 'frame', back)]
    ppermute x1, waiting for transfers between devices: 1.49 us -> 1.07 us  [local(): arrived = [lax.ppermute(x, 'frame', ahead) for ahead, _ in links]]
  transfers between devices with their start and end apart: 10 -> 11, of which waited for: 5 -> 5; matrix products, arithmetic and copies ran while one was open for 0% -> 0% of each run, Pallas kernels for 13% -> 13%
where the time goes in v7:
time: 19.5 us; the launch traced here: 19.3 us
  starting transfers between devices  9.49 us (49%)
  Pallas kernels  6.02 us (31%)
  waiting for transfers between devices  3.11 us (16%)
  between operations  0.71 us (4%)
    ppermute x2, starting transfers between devices, over_even(): return lax.ppermute(z, 'tile', evens)  3.67 us
    ppermute x1, starting transfers between devices, local(): arrived = [lax.ppermute(x, 'frame', ahead) for ahead, _ in links]  2.56 us
    pallas_call x1, Pallas kernels, fold(): call(functools.partial(fold_kernel, tiles, half, partners), 'fold', (shap...  1.97 us
    ppermute x2, waiting for transfers between devices, over_even(): return lax.ppermute(z, 'tile', evens)  1.73 us
    ppermute x1, starting transfers between devices, local(): lax.ppermute(z, 'frame', back)  1.71 us
    ppermute x5, starting transfers between devices, over_cores(): return lax.ppermute(z, 'chan', swap)  1.54 us
    pallas_call x1, Pallas kernels, volumes(): call(functools.partial(volume_kernel, tiles, half, partners), 'volume', (...  1.54 us
    ppermute x1, waiting for transfers between devices, local(): arrived = [lax.ppermute(x, 'frame', ahead) for ahead, _ in links]  1.07 us
  transfers between devices with their start and end apart: 11, of which 5 were waited for; matrix products, arithmetic and copies ran while one was open for 0% of the time, Pallas kernels for 13%

profile of v7, /device:TPU:0, one launch (start us, length us, event | category | flops | bytes accessed | tf_op | source)
XLA Modules:
  0.0 19.3 jit_solution(8174999617204479008)
XLA Ops:
  0.6 2.0 %fold.1 = (bf16[2560,128]{1,0:T(8,128)(2,1)S(1)}, bf16[2,256,128]{2,1,0:T(8,128)(2,1)S(1)}, f32[1,8,128]{2,1,0:T(8,128)S(1)}, f32[1,256,128]{2,1,0:T(8,128)S(1)}...) custom-call(s32[2,9]{1,0:T(2,128)} %neighbours_hbm.1, s32[2,256]{1,0:T(2,128)} %valid_hbm.1, s32[1,2]{1,0:T(1,128)} %pairing_hbm.1, ...), custom_call_target="tpu_custom_call" | custom-call | tf_op jit(solution)/shard_map/fold/pallas_call | solution.py:187
  2.6 0.5 %collective-permute-start = (bf16[2560,128]{1,0:T(8,128)(2,1)S(1)}, bf16[2560,128]{1,0:T(8,128)(2,1)S(1)}, u32[]{:S(2)}, u32[]{:S(2)}) collective-permute-start(bf16[2560,128]{1,0:T(8,128)(2,1)S(1)} %get-tuple-element.39.mine_ref.folded_ref), channel_id=1, source_target_pairs={{0,1},{1,0},{2,3},{3,2},{4,5},{5,4},{6,7},{7,6},{8,9},{9,8},{10,11... | collective-permute-start | bytes 1966088 | tf_op jit(solution)/shard_map/ppermute | solution.py:531
  3.1 2.6 %collective-permute-start.2 = (bf16[2,256,128]{2,1,0:T(8,128)(2,1)S(1)}, bf16[2,256,128]{2,1,0:T(8,128)(2,1)S(1)}, u32[]{:S(2)}, u32[]{:S(2)}) collective-permute-start(bf16[2,256,128]{2,1,0:T(8,128)(2,1)S(1)} %get-tuple-element.41.x_ref), channel_id=1, source_target_pairs={{0,2},{2,0},{1,3},{3,1},{4,6},{6,4},{5,7},{7,5},{8,10},{10,8},{9,1... | collective-permute-start | bytes 393224 | tf_op jit(solution)/shard_map/ppermute | solution.py:536
  5.7 0.3 %early.1.part_ref = f32[6,256,128]{2,1,0:T(8,128)S(1)} custom-call(bf16[2,256,128]{2,1,0:T(8,128)(2,1)S(1)} %get-tuple-element.41.x_ref, bf16[2560,128]{1,0:T(8,128)(2,1)S(1)} %get-tuple-element.39.mine_ref.folded_ref), custom_call_target="tpu_custom_call" | custom-call | tf_op jit(solution)/shard_map/early/pallas_call | solution.py:238
  6.0 0.0 collective-permute-done.other_ref
  6.0 0.3 %keys.1 = (f32[2,256,128]{2,1,0:T(8,128)S(1)}, bf16[2,256,128]{2,1,0:T(8,128)(2,1)S(1)}, bf16[2,256,128]{2,1,0:T(8,128)(2,1)S(1)}) custom-call(bf16[2,256,128]{2,1,0:T(8,128)(2,1)S(1)} %get-tuple-element.41.x_ref, f32[6,256,128]{2,1,0:T(8,128)S(1)} %early.1.part_ref, bf16[2560,128]{1,0:T(8,128)(2,1)S(1)} %collective-permute-done.other_ref), custom_call_target="tpu_custom_call" | custom-call | tf_op jit(solution)/shard_map/keys/pallas_call | solution.py:267
  6.4 1.8 %collective-permute-start.3 = (bf16[2,256,128]{2,1,0:T(8,128)(2,1)S(1)}, bf16[2,256,128]{2,1,0:T(8,128)(2,1)S(1)}, u32[]{:S(2)}, u32[]{:S(2)}) collective-permute-start(bf16[2,256,128]{2,1,0:T(8,128)(2,1)S(1)} %get-tuple-element.44), channel_id=1, source_target_pairs={{0,4},{4,0},{8,12},{12,8},{1,5},{5,1},{9,13},{13,9},{2,6},{6,2},{1... | collective-permute-start | bytes 393224 | tf_op jit(solution)/shard_map/ppermute | solution.py:525
  8.2 0.0 collective-permute-start.4
  8.2 0.5 %collective-permute-start.1 = (bf16[2,256,128]{2,1,0:T(8,128)(2,1)S(1)}, bf16[2,256,128]{2,1,0:T(8,128)(2,1)S(1)}, u32[]{:S(2)}, u32[]{:S(2)}) collective-permute-start(bf16[2,256,128]{2,1,0:T(8,128)(2,1)S(1)} %get-tuple-element.41.x_ref), channel_id=1, source_target_pairs={{0,1},{1,0},{2,3},{3,2},{4,5},{5,4},{6,7},{7,6},{8,9},{9,8},{10,11... | collective-permute-start | bytes 393224 | tf_op jit(solution)/shard_map/ppermute | solution.py:531
  8.7 1.1 %collective-permute-done.2.refs_0_ = bf16[2,256,128]{2,1,0:T(8,128)(2,1)S(1)} collective-permute-done((bf16[2,256,128]{2,1,0:T(8,128)(2,1)S(1)}, bf16[2,256,128]{2,1,0:T(8,128)(2,1)S(1)}, u32[]{:S(2)}, u32[]{:S(2)}) %collective-permute-start.2) | collective-permute-done | bytes 131104 | tf_op jit(solution)/shard_map/ppermute | solution.py:536
  9.8 1.8 %collective-permute-start.5 = (bf16[2,256,128]{2,1,0:T(8,128)(2,1)S(1)}, bf16[2,256,128]{2,1,0:T(8,128)(2,1)S(1)}, u32[]{:S(2)}, u32[]{:S(2)}) collective-permute-start(bf16[2,256,128]{2,1,0:T(8,128)(2,1)S(1)} %collective-permute-done.2.refs_0_), channel_id=1, source_target_pairs={{0,4},{4,0},{8,12},{12,8},{1,5},{5,1},{9,13},{13,9},{2,6},{6,2},{1... | collective-permute-start | bytes 393224 | tf_op jit(solution)/shard_map/ppermute | solution.py:525
  11.6 0.0 collective-permute-start.6
  11.6 0.4 %collective-permute-done.3.even_ref = bf16[2,256,128]{2,1,0:T(8,128)(2,1)S(1)} collective-permute-done((bf16[2,256,128]{2,1,0:T(8,128)(2,1)S(1)}, bf16[2,256,128]{2,1,0:T(8,128)(2,1)S(1)}, u32[]{:S(2)}, u32[]{:S(2)}) %collective-permute-start.3) | collective-permute-done | bytes 131104 | tf_op jit(solution)/shard_map/ppermute | solution.py:525
  12.0 0.0 collective-permute-done.4.odd_ref
  12.0 0.1 returns.1
  12.1 1.7 %collective-permute-start.10 = (bf16[528,128]{1,0:T(8,128)(2,1)S(1)}, bf16[528,128]{1,0:T(8,128)(2,1)S(1)}, u32[]{:S(2)}, u32[]{:S(2)}) collective-permute-start(bf16[528,128]{1,0:T(8,128)(2,1)S(1)} %returns.1), channel_id=1, source_target_pairs={{0,2},{2,0},{1,3},{3,1},{4,6},{6,4},{5,7},{7,5},{8,10},{10,8},{9,1... | collective-permute-start | bytes 405512 | tf_op jit(solution)/shard_map/ppermute | solution.py:544
  13.8 0.0 collective-permute-start.7
  13.8 0.0 collective-permute-done.1.xo_ref
  13.8 0.3 %ready.1 = (bf16[1,256,256]{2,1,0:T(8,128)(2,1)S(1)}, f32[2,256,128]{2,1,0:T(8,128)S(1)}) custom-call(f32[1,8,128]{2,1,0:T(8,128)S(1)} %get-tuple-element.38.gates_ref, f32[1,256,128]{2,1,0:T(8,128)S(1)} %get-tuple-element.40.keep_ref, bf16[2,256,128]{2,1,0:T(8,128)(2,1)S(1)} %get-tuple-element.41.x_ref, ...), custom_call_target="tpu_custom_call" | custom-call | tf_op jit(solution)/shard_map/ready/pallas_call | solution.py:351
  14.2 1.4 %collective-permute-done.5.refs_0_ = bf16[2,256,128]{2,1,0:T(8,128)(2,1)S(1)} collective-permute-done((bf16[2,256,128]{2,1,0:T(8,128)(2,1)S(1)}, bf16[2,256,128]{2,1,0:T(8,128)(2,1)S(1)}, u32[]{:S(2)}, u32[]{:S(2)}) %collective-permute-start.5) | collective-permute-done | bytes 131104 | tf_op jit(solution)/shard_map/ppermute | solution.py:525
  15.5 0.0 collective-permute-start.8
  15.5 0.0 collective-permute-done.6.refs_1_
  15.5 0.5 %collective-permute-start.9 = (bf16[2,256,128]{2,1,0:T(8,128)(2,1)S(1)}, bf16[2,256,128]{2,1,0:T(8,128)(2,1)S(1)}, u32[]{:S(2)}, u32[]{:S(2)}) collective-permute-start(bf16[2,256,128]{2,1,0:T(8,128)(2,1)S(1)} %collective-permute-done.6.refs_1_), channel_id=1, source_target_pairs={{0,1},{1,0},{2,3},{3,2},{4,5},{5,4},{6,7},{7,6},{8,9},{9,8},{10,11... | collective-permute-start | bytes 393224 | tf_op jit(solution)/shard_map/ppermute | solution.py:531
  16.0 0.5 %sides.1.part_ref = f32[2,256,128]{2,1,0:T(8,128)S(1)} custom-call(f32[1,8,128]{2,1,0:T(8,128)S(1)} %get-tuple-element.38.gates_ref, bf16[2560,128]{1,0:T(8,128)(2,1)S(1)} %get-tuple-element.39.mine_ref.folded_ref, bf16[2560,128]{1,0:T(8,128)(2,1)S(1)} %collective-permute-done.other_ref, f32[2,256,128]{2,1,0:T(8,128)S(1)} %get-tuple-element.48.part_ref, ...), custom_call_target="tpu_custom_call" | custom-call | tf_op jit(solution)/shard_map/sides/pallas_call | solution.py:380
  16.5 0.0 collective-permute-done.7.refs_1_
  16.5 0.5 %near.1 = (f32[2,256,256]{2,1,0:T(8,128)S(1)}, f32[2,128,256]{2,1,0:T(8,128)S(1)}) custom-call(bf16[1,256,256]{2,1,0:T(8,128)(2,1)S(1)} %get-tuple-element.51.queries_ref, bf16[128,256]{1,0:T(8,128)(2,1)S(1)} %get-tuple-element.52.pool_ref, bf16[2,256,128]{2,1,0:T(8,128)(2,1)S(1)} %collective-permute-done.2.refs_0_, ...), custom_call_target="tpu_custom_call" | custom-call | tf_op jit(solution)/shard_map/near/pallas_call | solution.py:409
  17.0 0.0 collective-permute-done.8.refs_2_
  17.0 0.1 collective-permute-done.9.refs_3_
  17.1 0.5 %tables.1 = (f32[6,256,256]{2,1,0:T(8,128)S(1)}, f32[6,128,256]{2,1,0:T(8,128)S(1)}) custom-call(bf16[1,256,256]{2,1,0:T(8,128)(2,1)S(1)} %get-tuple-element.51.queries_ref, bf16[128,256]{1,0:T(8,128)(2,1)S(1)} %get-tuple-element.52.pool_ref, f32[2,256,256]{2,1,0:T(8,128)S(1)} %get-tuple-element.57.near_fine, ...), custom_call_target="tpu_custom_call" | custom-call | tf_op jit(solution)/shard_map/tables/pallas_call | solution.py:448
  17.6 0.2 %collective-permute-done.10.refs_0_ = bf16[528,128]{1,0:T(8,128)(2,1)S(1)} collective-permute-done((bf16[528,128]{1,0:T(8,128)(2,1)S(1)}, bf16[528,128]{1,0:T(8,128)(2,1)S(1)}, u32[]{:S(2)}, u32[]{:S(2)}) %collective-permute-start.10) | collective-permute-done | bytes 135200 | tf_op jit(solution)/shard_map/ppermute | solution.py:544
  17.8 1.5 %volume.1 = (bf16[6120,128]{1,0:T(8,128)(2,1)}, f32[1,2,256,128]{3,2,1,0:T(8,128)}) custom-call(s32[2,9]{1,0:T(2,128)S(1)} %get-tuple-element.37.list_ref, f32[2,256,128]{2,1,0:T(8,128)S(1)} %sides.1.part_ref, f32[6,256,256]{2,1,0:T(8,128)S(1)} %get-tuple-element.67.fine_table, f32[6,128,256]{2,1,0:T(8,128)S(1)} %get-tuple-element.68.coarse_table, ...), custom_call_target="tpu_custom_call" | custom-call | tf_op jit(solution)/shard_map/volume/pallas_call | solution.py:495
Async XLA Ops:
  2.6 3.4 %collective-permute-start = (bf16[2560,128]{1,0:T(8,128)(2,1)S(1)}, bf16[2560,128]{1,0:T(8,128)(2,1)S(1)}, u32[]{:S(2)}, u32[]{:S(2)}) collective-permute-start(bf16[2560,128]{1,0:T(8,128)(2,1)S(1)} %get-tuple-element.39.mine_ref.folded_ref), channel_id=1, source_target_pairs={{0,1},{1,0},{2,3},{3,2},{4,5},{5,4},{6,7},{7,6},{8,9},{9,8},{10,11... | collective-permute-start | bytes 1966088 | tf_op jit(solution)/shard_map/ppermute | solution.py:531
  3.1 6.7 %collective-permute-start.2 = (bf16[2,256,128]{2,1,0:T(8,128)(2,1)S(1)}, bf16[2,256,128]{2,1,0:T(8,128)(2,1)S(1)}, u32[]{:S(2)}, u32[]{:S(2)}) collective-permute-start(bf16[2,256,128]{2,1,0:T(8,128)(2,1)S(1)} %get-tuple-element.41.x_ref), channel_id=1, source_target_pairs={{0,2},{2,0},{1,3},{3,1},{4,6},{6,4},{5,7},{7,5},{8,10},{10,8},{9,1... | collective-permute-start | bytes 393224 | tf_op jit(solution)/shard_map/ppermute | solution.py:536
  6.4 5.6 %collective-permute-start.3 = (bf16[2,256,128]{2,1,0:T(8,128)(2,1)S(1)}, bf16[2,256,128]{2,1,0:T(8,128)(2,1)S(1)}, u32[]{:S(2)}, u32[]{:S(2)}) collective-permute-start(bf16[2,256,128]{2,1,0:T(8,128)(2,1)S(1)} %get-tuple-element.44), channel_id=1, source_target_pairs={{0,4},{4,0},{8,12},{12,8},{1,5},{5,1},{9,13},{13,9},{2,6},{6,2},{1... | collective-permute-start | bytes 393224 | tf_op jit(solution)/shard_map/ppermute | solution.py:525
  8.2 3.8 %collective-permute-start.4 = (bf16[2,256,128]{2,1,0:T(8,128)(2,1)S(1)}, bf16[2,256,128]{2,1,0:T(8,128)(2,1)S(1)}, u32[]{:S(2)}, u32[]{:S(2)}) collective-permute-start(bf16[2,256,128]{2,1,0:T(8,128)(2,1)S(1)} %get-tuple-element.45), channel_id=1, source_target_pairs={{4,8},{8,4},{5,9},{9,5},{0,1},{1,0},{12,13},{13,12},{6,10},{10,6},... | collective-permute-start | bytes 393224 | tf_op jit(solution)/shard_map/ppermute | solution.py:528
  8.2 5.6 %collective-permute-start.1 = (bf16[2,256,128]{2,1,0:T(8,128)(2,1)S(1)}, bf16[2,256,128]{2,1,0:T(8,128)(2,1)S(1)}, u32[]{:S(2)}, u32[]{:S(2)}) collective-permute-start(bf16[2,256,128]{2,1,0:T(8,128)(2,1)S(1)} %get-tuple-element.41.x_ref), channel_id=1, source_target_pairs={{0,1},{1,0},{2,3},{3,2},{4,5},{5,4},{6,7},{7,6},{8,9},{9,8},{10,11... | collective-permute-start | bytes 393224 | tf_op jit(solution)/shard_map/ppermute | solution.py:531
  9.8 5.7 %collective-permute-start.5 = (bf16[2,256,128]{2,1,0:T(8,128)(2,1)S(1)}, bf16[2,256,128]{2,1,0:T(8,128)(2,1)S(1)}, u32[]{:S(2)}, u32[]{:S(2)}) collective-permute-start(bf16[2,256,128]{2,1,0:T(8,128)(2,1)S(1)} %collective-permute-done.2.refs_0_), channel_id=1, source_target_pairs={{0,4},{4,0},{8,12},{12,8},{1,5},{5,1},{9,13},{13,9},{2,6},{6,2},{1... | collective-permute-start | bytes 393224 | tf_op jit(solution)/shard_map/ppermute | solution.py:525
  11.6 3.9 %collective-permute-start.6 = (bf16[2,256,128]{2,1,0:T(8,128)(2,1)S(1)}, bf16[2,256,128]{2,1,0:T(8,128)(2,1)S(1)}, u32[]{:S(2)}, u32[]{:S(2)}) collective-permute-start(bf16[2,256,128]{2,1,0:T(8,128)(2,1)S(1)} %collective-permute-done.2.refs_0_), channel_id=1, source_target_pairs={{4,8},{8,4},{5,9},{9,5},{0,1},{1,0},{12,13},{13,12},{6,10},{10,6},... | collective-permute-start | bytes 393224 | tf_op jit(solution)/shard_map/ppermute | solution.py:528
  12.1 5.7 %collective-permute-start.10 = (bf16[528,128]{1,0:T(8,128)(2,1)S(1)}, bf16[528,128]{1,0:T(8,128)(2,1)S(1)}, u32[]{:S(2)}, u32[]{:S(2)}) collective-permute-start(bf16[528,128]{1,0:T(8,128)(2,1)S(1)} %returns.1), channel_id=1, source_target_pairs={{0,2},{2,0},{1,3},{3,1},{4,6},{6,4},{5,7},{7,5},{8,10},{10,8},{9,1... | collective-permute-start | bytes 405512 | tf_op jit(solution)/shard_map/ppermute | solution.py:544
  13.8 2.7 %collective-permute-start.7 = (bf16[2,256,128]{2,1,0:T(8,128)(2,1)S(1)}, bf16[2,256,128]{2,1,0:T(8,128)(2,1)S(1)}, u32[]{:S(2)}, u32[]{:S(2)}) collective-permute-start(bf16[2,256,128]{2,1,0:T(8,128)(2,1)S(1)} %collective-permute-done.2.refs_0_), channel_id=1, source_target_pairs={{0,1},{1,0},{2,3},{3,2},{4,5},{5,4},{6,7},{7,6},{8,9},{9,8},{10,11... | collective-permute-start | bytes 393224 | tf_op jit(solution)/shard_map/ppermute | solution.py:531
  15.5 1.5 %collective-permute-start.8 = (bf16[2,256,128]{2,1,0:T(8,128)(2,1)S(1)}, bf16[2,256,128]{2,1,0:T(8,128)(2,1)S(1)}, u32[]{:S(2)}, u32[]{:S(2)}) collective-permute-start(bf16[2,256,128]{2,1,0:T(8,128)(2,1)S(1)} %collective-permute-done.5.refs_0_), channel_id=1, source_target_pairs={{0,1},{1,0},{2,3},{3,2},{4,5},{5,4},{6,7},{7,6},{8,9},{9,8},{10,11... | collective-permute-start | bytes 393224 | tf_op jit(solution)/shard_map/ppermute | solution.py:531
  15.5 1.5 %collective-permute-start.9 = (bf16[2,256,128]{2,1,0:T(8,128)(2,1)S(1)}, bf16[2,256,128]{2,1,0:T(8,128)(2,1)S(1)}, u32[]{:S(2)}, u32[]{:S(2)}) collective-permute-start(bf16[2,256,128]{2,1,0:T(8,128)(2,1)S(1)} %collective-permute-done.6.refs_1_), channel_id=1, source_target_pairs={{0,1},{1,0},{2,3},{3,2},{4,5},{5,4},{6,7},{7,6},{8,9},{9,8},{10,11... | collective-permute-start | bytes 393224 | tf_op jit(solution)/shard_map/ppermute | solution.py:531

commit v8 on v7

--- a/solution.py
+++ b/solution.py
@@ -464,13 +464,7 @@
     first = lax.axis_index("tile") * tiles
     listed = list_ref[...]
     pixels, channels = grad_ref.shape[1:]
-    for a in range(tiles):
-        summed = part_ref[a]
-        for j in range(partners):
-            summed = summed + returned[j][a * pixels : (a + 1) * pixels].astype(jnp.float32)
-        grad_ref[a] = summed
-    waits = [pltpu.make_async_copy(grad_ref, grad_hbm.at[0], sems.at[0])]
-    waits[0].start()
+    waits = []
     for i_part, (entries, start, size) in enumerate(entry_pairs(tiles)):
         for i, k in enumerate(entries):
             for a in range(tiles):
@@ -484,6 +478,15 @@
         copy = pltpu.make_async_copy(volume_ref.at[rows], volume_hbm.at[rows], sems.at[1 + i_part])
         copy.start()
         waits.append(copy)
+        if i_part == 1:
+            for a in range(tiles):
+                summed = part_ref[a]
+                for j in range(partners):
+                    summed = summed + returned[j][a * pixels : (a + 1) * pixels].astype(jnp.float32)
+                grad_ref[a] = summed
+            copy = pltpu.make_async_copy(grad_ref, grad_hbm.at[0], sems.at[0])
+            copy.start()
+            waits.append(copy)
     for copy in waits:
         copy.wait()
 

time: 19.5 us -> 19.5 us (level)
  no operation moved by 1% of the time
where the time goes in v8:
time: 19.5 us; the launch traced here: 19.3 us
  starting transfers between devices  9.49 us (49%)
  Pallas kernels  6.01 us (31%)
  waiting for transfers between devices  3.11 us (16%)
  between operations  0.71 us (4%)
    ppermute x2, starting transfers between devices, over_even(): return lax.ppermute(z, 'tile', evens)  3.67 us
    ppermute x1, starting transfers between devices, local(): arrived = [lax.ppermute(x, 'frame', ahead) for ahead, _ in links]  2.56 us
    pallas_call x1, Pallas kernels, fold(): call(functools.partial(fold_kernel, tiles, half, partners), 'fold', (shap...  1.97 us
    ppermute x2, waiting for transfers between devices, over_even(): return lax.ppermute(z, 'tile', evens)  1.73 us
    ppermute x1, starting transfers between devices, local(): lax.ppermute(z, 'frame', back)  1.71 us
    ppermute x5, starting transfers between devices, over_cores(): return lax.ppermute(z, 'chan', swap)  1.54 us
    pallas_call x1, Pallas kernels, volumes(): call(functools.partial(volume_kernel, tiles, half, partners), 'volume', (...  1.53 us
    ppermute x1, waiting for transfers between devices, local(): arrived = [lax.ppermute(x, 'frame', ahead) for ahead, _ in links]  1.07 us
  transfers between devices with their start and end apart: 11, of which 5 were waited for; matrix products, arithmetic and copies ran while one was open for 0% of the time, Pallas kernels for 13%

profile of v8, /device:TPU:0, one launch (start us, length us, event | category | flops | bytes accessed | tf_op | source)
XLA Modules:
  0.0 19.3 jit_solution(8816073466385605115)
XLA Ops:
  0.6 2.0 %fold.1 = (bf16[2560,128]{1,0:T(8,128)(2,1)S(1)}, bf16[2,256,128]{2,1,0:T(8,128)(2,1)S(1)}, f32[1,8,128]{2,1,0:T(8,128)S(1)}, f32[1,256,128]{2,1,0:T(8,128)S(1)}...) custom-call(s32[2,9]{1,0:T(2,128)} %neighbours_hbm.1, s32[2,256]{1,0:T(2,128)} %valid_hbm.1, s32[1,2]{1,0:T(1,128)} %pairing_hbm.1, ...), custom_call_target="tpu_custom_call" | custom-call | tf_op jit(solution)/shard_map/fold/pallas_call | solution.py:187
  2.6 0.5 %collective-permute-start = (bf16[2560,128]{1,0:T(8,128)(2,1)S(1)}, bf16[2560,128]{1,0:T(8,128)(2,1)S(1)}, u32[]{:S(2)}, u32[]{:S(2)}) collective-permute-start(bf16[2560,128]{1,0:T(8,128)(2,1)S(1)} %get-tuple-element.39.mine_ref.folded_ref), channel_id=1, source_target_pairs={{0,1},{1,0},{2,3},{3,2},{4,5},{5,4},{6,7},{7,6},{8,9},{9,8},{10,11... | collective-permute-start | bytes 1966088 | tf_op jit(solution)/shard_map/ppermute | solution.py:534
  3.1 2.6 %collective-permute-start.2 = (bf16[2,256,128]{2,1,0:T(8,128)(2,1)S(1)}, bf16[2,256,128]{2,1,0:T(8,128)(2,1)S(1)}, u32[]{:S(2)}, u32[]{:S(2)}) collective-permute-start(bf16[2,256,128]{2,1,0:T(8,128)(2,1)S(1)} %get-tuple-element.41.x_ref), channel_id=1, source_target_pairs={{0,2},{2,0},{1,3},{3,1},{4,6},{6,4},{5,7},{7,5},{8,10},{10,8},{9,1... | collective-permute-start | bytes 393224 | tf_op jit(solution)/shard_map/ppermute | solution.py:539
  5.7 0.3 %early.1.part_ref = f32[6,256,128]{2,1,0:T(8,128)S(1)} custom-call(bf16[2,256,128]{2,1,0:T(8,128)(2,1)S(1)} %get-tuple-element.41.x_ref, bf16[2560,128]{1,0:T(8,128)(2,1)S(1)} %get-tuple-element.39.mine_ref.folded_ref), custom_call_target="tpu_custom_call" | custom-call | tf_op jit(solution)/shard_map/early/pallas_call | solution.py:238
  6.0 0.0 collective-permute-done.other_ref
  6.0 0.3 %keys.1 = (f32[2,256,128]{2,1,0:T(8,128)S(1)}, bf16[2,256,128]{2,1,0:T(8,128)(2,1)S(1)}, bf16[2,256,128]{2,1,0:T(8,128)(2,1)S(1)}) custom-call(bf16[2,256,128]{2,1,0:T(8,128)(2,1)S(1)} %get-tuple-element.41.x_ref, f32[6,256,128]{2,1,0:T(8,128)S(1)} %early.1.part_ref, bf16[2560,128]{1,0:T(8,128)(2,1)S(1)} %collective-permute-done.other_ref), custom_call_target="tpu_custom_call" | custom-call | tf_op jit(solution)/shard_map/keys/pallas_call | solution.py:267
  6.4 1.8 %collective-permute-start.3 = (bf16[2,256,128]{2,1,0:T(8,128)(2,1)S(1)}, bf16[2,256,128]{2,1,0:T(8,128)(2,1)S(1)}, u32[]{:S(2)}, u32[]{:S(2)}) collective-permute-start(bf16[2,256,128]{2,1,0:T(8,128)(2,1)S(1)} %get-tuple-element.44), channel_id=1, source_target_pairs={{0,4},{4,0},{8,12},{12,8},{1,5},{5,1},{9,13},{13,9},{2,6},{6,2},{1... | collective-permute-start | bytes 393224 | tf_op jit(solution)/shard_map/ppermute | solution.py:528
  8.2 0.0 collective-permute-start.4
  8.2 0.5 %collective-permute-start.1 = (bf16[2,256,128]{2,1,0:T(8,128)(2,1)S(1)}, bf16[2,256,128]{2,1,0:T(8,128)(2,1)S(1)}, u32[]{:S(2)}, u32[]{:S(2)}) collective-permute-start(bf16[2,256,128]{2,1,0:T(8,128)(2,1)S(1)} %get-tuple-element.41.x_ref), channel_id=1, source_target_pairs={{0,1},{1,0},{2,3},{3,2},{4,5},{5,4},{6,7},{7,6},{8,9},{9,8},{10,11... | collective-permute-start | bytes 393224 | tf_op jit(solution)/shard_map/ppermute | solution.py:534
  8.7 1.1 %collective-permute-done.2.refs_0_ = bf16[2,256,128]{2,1,0:T(8,128)(2,1)S(1)} collective-permute-done((bf16[2,256,128]{2,1,0:T(8,128)(2,1)S(1)}, bf16[2,256,128]{2,1,0:T(8,128)(2,1)S(1)}, u32[]{:S(2)}, u32[]{:S(2)}) %collective-permute-start.2) | collective-permute-done | bytes 131104 | tf_op jit(solution)/shard_map/ppermute | solution.py:539
  9.8 1.8 %collective-permute-start.5 = (bf16[2,256,128]{2,1,0:T(8,128)(2,1)S(1)}, bf16[2,256,128]{2,1,0:T(8,128)(2,1)S(1)}, u32[]{:S(2)}, u32[]{:S(2)}) collective-permute-start(bf16[2,256,128]{2,1,0:T(8,128)(2,1)S(1)} %collective-permute-done.2.refs_0_), channel_id=1, source_target_pairs={{0,4},{4,0},{8,12},{12,8},{1,5},{5,1},{9,13},{13,9},{2,6},{6,2},{1... | collective-permute-start | bytes 393224 | tf_op jit(solution)/shard_map/ppermute | solution.py:528
  11.6 0.0 collective-permute-start.6
  11.6 0.4 %collective-permute-done.3.even_ref = bf16[2,256,128]{2,1,0:T(8,128)(2,1)S(1)} collective-permute-done((bf16[2,256,128]{2,1,0:T(8,128)(2,1)S(1)}, bf16[2,256,128]{2,1,0:T(8,128)(2,1)S(1)}, u32[]{:S(2)}, u32[]{:S(2)}) %collective-permute-start.3) | collective-permute-done | bytes 131104 | tf_op jit(solution)/shard_map/ppermute | solution.py:528
  12.0 0.0 collective-permute-done.4.odd_ref
  12.0 0.1 returns.1
  12.1 1.7 %collective-permute-start.10 = (bf16[528,128]{1,0:T(8,128)(2,1)S(1)}, bf16[528,128]{1,0:T(8,128)(2,1)S(1)}, u32[]{:S(2)}, u32[]{:S(2)}) collective-permute-start(bf16[528,128]{1,0:T(8,128)(2,1)S(1)} %returns.1), channel_id=1, source_target_pairs={{0,2},{2,0},{1,3},{3,1},{4,6},{6,4},{5,7},{7,5},{8,10},{10,8},{9,1... | collective-permute-start | bytes 405512 | tf_op jit(solution)/shard_map/ppermute | solution.py:547
  13.8 0.0 collective-permute-start.7
  13.8 0.0 collective-permute-done.1.xo_ref
  13.8 0.3 %ready.1 = (bf16[1,256,256]{2,1,0:T(8,128)(2,1)S(1)}, f32[2,256,128]{2,1,0:T(8,128)S(1)}) custom-call(f32[1,8,128]{2,1,0:T(8,128)S(1)} %get-tuple-element.38.gates_ref, f32[1,256,128]{2,1,0:T(8,128)S(1)} %get-tuple-element.40.keep_ref, bf16[2,256,128]{2,1,0:T(8,128)(2,1)S(1)} %get-tuple-element.41.x_ref, ...), custom_call_target="tpu_custom_call" | custom-call | tf_op jit(solution)/shard_map/ready/pallas_call | solution.py:351
  14.2 1.4 %collective-permute-done.5.refs_0_ = bf16[2,256,128]{2,1,0:T(8,128)(2,1)S(1)} collective-permute-done((bf16[2,256,128]{2,1,0:T(8,128)(2,1)S(1)}, bf16[2,256,128]{2,1,0:T(8,128)(2,1)S(1)}, u32[]{:S(2)}, u32[]{:S(2)}) %collective-permute-start.5) | collective-permute-done | bytes 131104 | tf_op jit(solution)/shard_map/ppermute | solution.py:528
  15.5 0.0 collective-permute-start.8
  15.5 0.0 collective-permute-done.6.refs_1_
  15.5 0.5 %collective-permute-start.9 = (bf16[2,256,128]{2,1,0:T(8,128)(2,1)S(1)}, bf16[2,256,128]{2,1,0:T(8,128)(2,1)S(1)}, u32[]{:S(2)}, u32[]{:S(2)}) collective-permute-start(bf16[2,256,128]{2,1,0:T(8,128)(2,1)S(1)} %collective-permute-done.6.refs_1_), channel_id=1, source_target_pairs={{0,1},{1,0},{2,3},{3,2},{4,5},{5,4},{6,7},{7,6},{8,9},{9,8},{10,11... | collective-permute-start | bytes 393224 | tf_op jit(solution)/shard_map/ppermute | solution.py:534
  16.0 0.5 %sides.1.part_ref = f32[2,256,128]{2,1,0:T(8,128)S(1)} custom-call(f32[1,8,128]{2,1,0:T(8,128)S(1)} %get-tuple-element.38.gates_ref, bf16[2560,128]{1,0:T(8,128)(2,1)S(1)} %get-tuple-element.39.mine_ref.folded_ref, bf16[2560,128]{1,0:T(8,128)(2,1)S(1)} %collective-permute-done.other_ref, f32[2,256,128]{2,1,0:T(8,128)S(1)} %get-tuple-element.48.part_ref, ...), custom_call_target="tpu_custom_call" | custom-call | tf_op jit(solution)/shard_map/sides/pallas_call | solution.py:380
  16.5 0.0 collective-permute-done.7.refs_1_
  16.5 0.5 %near.1 = (f32[2,256,256]{2,1,0:T(8,128)S(1)}, f32[2,128,256]{2,1,0:T(8,128)S(1)}) custom-call(bf16[1,256,256]{2,1,0:T(8,128)(2,1)S(1)} %get-tuple-element.51.queries_ref, bf16[128,256]{1,0:T(8,128)(2,1)S(1)} %get-tuple-element.52.pool_ref, bf16[2,256,128]{2,1,0:T(8,128)(2,1)S(1)} %collective-permute-done.2.refs_0_, ...), custom_call_target="tpu_custom_call" | custom-call | tf_op jit(solution)/shard_map/near/pallas_call | solution.py:409
  17.0 0.0 collective-permute-done.8.refs_2_
  17.0 0.1 collective-permute-done.9.refs_3_
  17.1 0.5 %tables.1 = (f32[6,256,256]{2,1,0:T(8,128)S(1)}, f32[6,128,256]{2,1,0:T(8,128)S(1)}) custom-call(bf16[1,256,256]{2,1,0:T(8,128)(2,1)S(1)} %get-tuple-element.51.queries_ref, bf16[128,256]{1,0:T(8,128)(2,1)S(1)} %get-tuple-element.52.pool_ref, f32[2,256,256]{2,1,0:T(8,128)S(1)} %get-tuple-element.57.near_fine, ...), custom_call_target="tpu_custom_call" | custom-call | tf_op jit(solution)/shard_map/tables/pallas_call | solution.py:448
  17.6 0.2 %collective-permute-done.10.refs_0_ = bf16[528,128]{1,0:T(8,128)(2,1)S(1)} collective-permute-done((bf16[528,128]{1,0:T(8,128)(2,1)S(1)}, bf16[528,128]{1,0:T(8,128)(2,1)S(1)}, u32[]{:S(2)}, u32[]{:S(2)}) %collective-permute-start.10) | collective-permute-done | bytes 135200 | tf_op jit(solution)/shard_map/ppermute | solution.py:547
  17.8 1.5 %volume.1 = (bf16[6120,128]{1,0:T(8,128)(2,1)}, f32[1,2,256,128]{3,2,1,0:T(8,128)}) custom-call(s32[2,9]{1,0:T(2,128)S(1)} %get-tuple-element.37.list_ref, f32[2,256,128]{2,1,0:T(8,128)S(1)} %sides.1.part_ref, f32[6,256,256]{2,1,0:T(8,128)S(1)} %get-tuple-element.67.fine_table, f32[6,128,256]{2,1,0:T(8,128)S(1)} %get-tuple-element.68.coarse_table, ...), custom_call_target="tpu_custom_call" | custom-call | tf_op jit(solution)/shard_map/volume/pallas_call | solution.py:498
Async XLA Ops:
  2.6 3.4 %collective-permute-start = (bf16[2560,128]{1,0:T(8,128)(2,1)S(1)}, bf16[2560,128]{1,0:T(8,128)(2,1)S(1)}, u32[]{:S(2)}, u32[]{:S(2)}) collective-permute-start(bf16[2560,128]{1,0:T(8,128)(2,1)S(1)} %get-tuple-element.39.mine_ref.folded_ref), channel_id=1, source_target_pairs={{0,1},{1,0},{2,3},{3,2},{4,5},{5,4},{6,7},{7,6},{8,9},{9,8},{10,11... | collective-permute-start | bytes 1966088 | tf_op jit(solution)/shard_map/ppermute | solution.py:534
  3.1 6.7 %collective-permute-start.2 = (bf16[2,256,128]{2,1,0:T(8,128)(2,1)S(1)}, bf16[2,256,128]{2,1,0:T(8,128)(2,1)S(1)}, u32[]{:S(2)}, u32[]{:S(2)}) collective-permute-start(bf16[2,256,128]{2,1,0:T(8,128)(2,1)S(1)} %get-tuple-element.41.x_ref), channel_id=1, source_target_pairs={{0,2},{2,0},{1,3},{3,1},{4,6},{6,4},{5,7},{7,5},{8,10},{10,8},{9,1... | collective-permute-start | bytes 393224 | tf_op jit(solution)/shard_map/ppermute | solution.py:539
  6.4 5.6 %collective-permute-start.3 = (bf16[2,256,128]{2,1,0:T(8,128)(2,1)S(1)}, bf16[2,256,128]{2,1,0:T(8,128)(2,1)S(1)}, u32[]{:S(2)}, u32[]{:S(2)}) collective-permute-start(bf16[2,256,128]{2,1,0:T(8,128)(2,1)S(1)} %get-tuple-element.44), channel_id=1, source_target_pairs={{0,4},{4,0},{8,12},{12,8},{1,5},{5,1},{9,13},{13,9},{2,6},{6,2},{1... | collective-permute-start | bytes 393224 | tf_op jit(solution)/shard_map/ppermute | solution.py:528
  8.2 3.8 %collective-permute-start.4 = (bf16[2,256,128]{2,1,0:T(8,128)(2,1)S(1)}, bf16[2,256,128]{2,1,0:T(8,128)(2,1)S(1)}, u32[]{:S(2)}, u32[]{:S(2)}) collective-permute-start(bf16[2,256,128]{2,1,0:T(8,128)(2,1)S(1)} %get-tuple-element.45), channel_id=1, source_target_pairs={{4,8},{8,4},{5,9},{9,5},{0,1},{1,0},{12,13},{13,12},{6,10},{10,6},... | collective-permute-start | bytes 393224 | tf_op jit(solution)/shard_map/ppermute | solution.py:531
  8.2 5.6 %collective-permute-start.1 = (bf16[2,256,128]{2,1,0:T(8,128)(2,1)S(1)}, bf16[2,256,128]{2,1,0:T(8,128)(2,1)S(1)}, u32[]{:S(2)}, u32[]{:S(2)}) collective-permute-start(bf16[2,256,128]{2,1,0:T(8,128)(2,1)S(1)} %get-tuple-element.41.x_ref), channel_id=1, source_target_pairs={{0,1},{1,0},{2,3},{3,2},{4,5},{5,4},{6,7},{7,6},{8,9},{9,8},{10,11... | collective-permute-start | bytes 393224 | tf_op jit(solution)/shard_map/ppermute | solution.py:534
  9.8 5.7 %collective-permute-start.5 = (bf16[2,256,128]{2,1,0:T(8,128)(2,1)S(1)}, bf16[2,256,128]{2,1,0:T(8,128)(2,1)S(1)}, u32[]{:S(2)}, u32[]{:S(2)}) collective-permute-start(bf16[2,256,128]{2,1,0:T(8,128)(2,1)S(1)} %collective-permute-done.2.refs_0_), channel_id=1, source_target_pairs={{0,4},{4,0},{8,12},{12,8},{1,5},{5,1},{9,13},{13,9},{2,6},{6,2},{1... | collective-permute-start | bytes 393224 | tf_op jit(solution)/shard_map/ppermute | solution.py:528
  11.6 3.9 %collective-permute-start.6 = (bf16[2,256,128]{2,1,0:T(8,128)(2,1)S(1)}, bf16[2,256,128]{2,1,0:T(8,128)(2,1)S(1)}, u32[]{:S(2)}, u32[]{:S(2)}) collective-permute-start(bf16[2,256,128]{2,1,0:T(8,128)(2,1)S(1)} %collective-permute-done.2.refs_0_), channel_id=1, source_target_pairs={{4,8},{8,4},{5,9},{9,5},{0,1},{1,0},{12,13},{13,12},{6,10},{10,6},... | collective-permute-start | bytes 393224 | tf_op jit(solution)/shard_map/ppermute | solution.py:531
  12.1 5.7 %collective-permute-start.10 = (bf16[528,128]{1,0:T(8,128)(2,1)S(1)}, bf16[528,128]{1,0:T(8,128)(2,1)S(1)}, u32[]{:S(2)}, u32[]{:S(2)}) collective-permute-start(bf16[528,128]{1,0:T(8,128)(2,1)S(1)} %returns.1), channel_id=1, source_target_pairs={{0,2},{2,0},{1,3},{3,1},{4,6},{6,4},{5,7},{7,5},{8,10},{10,8},{9,1... | collective-permute-start | bytes 405512 | tf_op jit(solution)/shard_map/ppermute | solution.py:547
  13.8 2.7 %collective-permute-start.7 = (bf16[2,256,128]{2,1,0:T(8,128)(2,1)S(1)}, bf16[2,256,128]{2,1,0:T(8,128)(2,1)S(1)}, u32[]{:S(2)}, u32[]{:S(2)}) collective-permute-start(bf16[2,256,128]{2,1,0:T(8,128)(2,1)S(1)} %collective-permute-done.2.refs_0_), channel_id=1, source_target_pairs={{0,1},{1,0},{2,3},{3,2},{4,5},{5,4},{6,7},{7,6},{8,9},{9,8},{10,11... | collective-permute-start | bytes 393224 | tf_op jit(solution)/shard_map/ppermute | solution.py:534
  15.5 1.5 %collective-permute-start.8 = (bf16[2,256,128]{2,1,0:T(8,128)(2,1)S(1)}, bf16[2,256,128]{2,1,0:T(8,128)(2,1)S(1)}, u32[]{:S(2)}, u32[]{:S(2)}) collective-permute-start(bf16[2,256,128]{2,1,0:T(8,128)(2,1)S(1)} %collective-permute-done.5.refs_0_), channel_id=1, source_target_pairs={{0,1},{1,0},{2,3},{3,2},{4,5},{5,4},{6,7},{7,6},{8,9},{9,8},{10,11... | collective-permute-start | bytes 393224 | tf_op jit(solution)/shard_map/ppermute | solution.py:534
  15.5 1.5 %collective-permute-start.9 = (bf16[2,256,128]{2,1,0:T(8,128)(2,1)S(1)}, bf16[2,256,128]{2,1,0:T(8,128)(2,1)S(1)}, u32[]{:S(2)}, u32[]{:S(2)}) collective-permute-start(bf16[2,256,128]{2,1,0:T(8,128)(2,1)S(1)} %collective-permute-done.6.refs_1_), channel_id=1, source_target_pairs={{0,1},{1,0},{2,3},{3,2},{4,5},{5,4},{6,7},{7,6},{8,9},{9,8},{10,11... | collective-permute-start | bytes 393224 | tf_op jit(solution)/shard_map/ppermute | solution.py:534
